TPU v7x, 512 devices: a whole 4x8x8 slice. The times are simulated.
512 devices in a mesh: op: 16 (over x, z_lo, core), sec: 32 (over y, z_hi).
Axes of the slice: x: 4, y: 8, z: 8 (z_hi: 4, z_lo: 2; z = z_hi * 2 + z_lo), core: 2. Of those that a mesh axis runs over, the one named last changes fastest.
Arguments:
- psi: float32 [64, 128, 128], P('sec', 'op'), may hold values from -6 to 6
- left_env: float32 [256, 64, 128, 128], P('op', 'sec'), may hold values from -0.078125 to 0.078125
- right_env: float32 [256, 64, 128, 128], P('op', 'sec'), may hold values from -0.5 to 0.5
- coupling: int32 [64, 256], P('sec', 'op'), may hold values from 0 to 63
- assign: int32 [64], replicated, may hold values from 0 to 63, each once
- sizes: int32 [64], replicated, may hold values from 1 to 128, 6144 in all
Outputs:
- sigma_first: float32 [64, 128, 128], P('sec', 'op')
- next_vector: float32 [64, 128, 128], P('sec', 'op')
- sigma_next: float32 [64, 128, 128], P('sec', 'op')
Inputs may be any that keep to these rules, and one draw needn't show every extreme that they name: `assign`: each slot holds a different sector. `sizes`: sector dimensions sum to 64 * 128 * 3 // 4, the largest is exactly 128.
All inputs are finite; a program needn't handle non-finite values.
Results may differ from a plain program's by a relative error of at most 0.00011.
Values sent between devices are 32-bit elements; how exact they have to be, the bound alone decides.
No kernel may reach another device: no remote copies, remote signals or barrier semaphores. Data moves between devices by JAX's collectives and lax.ppermute only.
A program may use at most 64 MiB of HBM per device.

v0:
```python
import jax
import jax.numpy as jnp
from jax import lax
from jax.sharding import PartitionSpec as P


def on_device(psi, left_env, right_env, coupling, assign, sizes):
    slots, rows, width = psi.shape
    sectors = assign.shape[0]
    labels = jnp.arange(sectors, dtype=jnp.int32)
    match = (assign[:, None] == labels[None, :]).astype(jnp.int32)
    slot_of = jnp.sum(match * labels[:, None], axis=0)
    size_of = jnp.sum(match * sizes[None, :], axis=1)
    local_size = lax.dynamic_slice_in_dim(size_of, lax.axis_index("sec") * slots, slots)
    row_ids = lax.axis_index("op") * rows + jnp.arange(rows, dtype=jnp.int32)
    col_ids = jnp.arange(width, dtype=jnp.int32)
    row_in = (row_ids[None, :] < local_size[:, None]).astype(jnp.float32)
    col_in = (col_ids[None, :] < local_size[:, None]).astype(jnp.float32)
    mask = row_in[:, :, None] * col_in[:, None, :]
    source = slot_of[coupling]

    def apply(field):
        tall = lax.all_gather(field, "op", axis=1, tiled=True)
        whole = lax.all_gather(tall, "sec", axis=0, tiled=True)
        picked = whole[source]
        inner = jnp.einsum("tpij,ptjl->ptil", left_env, picked, precision=lax.Precision.HIGHEST)
        partial_sigma = jnp.einsum(
            "ptil,tpml->pim", inner, right_env, precision=lax.Precision.HIGHEST
        )
        summed = lax.psum(partial_sigma, "op")
        share = lax.dynamic_slice_in_dim(summed, lax.axis_index("op") * rows, rows, 1)
        return share * mask

    start = psi * mask
    sigma_first = apply(start)
    cross, square = lax.psum((jnp.sum(start * sigma_first), jnp.sum(start * start)), ("op", "sec"))
    theta = cross / square
    resid = sigma_first - theta * start
    total = lax.psum(jnp.sum(resid * resid), ("op", "sec"))
    next_vector = resid / jnp.sqrt(total + 1e-06)
    sigma_next = apply(next_vector)
    return (sigma_first, next_vector, sigma_next)


def solution(mesh):
    placed = (
        P("sec", "op", None),
        P("op", "sec", None, None),
        P("op", "sec", None, None),
        P("sec", "op"),
        P(),
        P(),
    )
    return jax.shard_map(
        on_device,
        mesh=mesh,
        in_specs=placed,
        out_specs=(P("sec", "op", None), P("sec", "op", None), P("sec", "op", None)),
        check_vma=False,
    )
```

profile of v0, /device:TPU:1, one launch (start us, length us, event | category | flops | bytes accessed | tf_op | source)
XLA Modules:
  0.0 732.9 jit_solution(14942883362059447354)
XLA Ops:
  7.2 0.0 all-gather.3.cloned.1.call-start
  7.2 1.0 select_reduce_fusion
  8.2 0.1 dynamic_slice.9
  8.3 0.1 compare_convert_fusion
  8.4 0.1 compare_convert_fusion.1
  8.5 0.8 multiply_multiply_fusion.2
  9.2 24.6 %all_gather.12 = f32[2,128,128]{2,1,0:T(8,128)} all-gather(f32[2,8,128]{2,1,0:T(8,128)S(1)} %multiply_multiply_fusion.2), channel_id=1, replica_groups=mesh['op'=16,'sec'=32] {'op'}, dimensions={1}, use_global_device_ids=true | all-gather | bytes 139264 | tf_op jit(solution)/shard_map/all_gather | solution.py:23
  33.8 0.0 all-reduce.4.cloned.1.call-start
  33.9 0.7 compare_select_fusion.1
  34.6 0.1 reshape.72
  34.7 0.7 gather_fusion
  35.4 0.1 gather.12
  35.4 0.1 reshape.80
  35.5 100.6 %all-gather.3.cloned.1.call-done = f32[64,128,128]{2,1,0:T(8,128)} async-done(((f32[2,128,128]{2,1,0:T(8,128)}), f32[64,128,128]{2,1,0:T(8,128)}) %all-gather.3.cloned.1.call-update) | async-done | bytes 4194320 | tf_op jit(solution)/shard_map/all_gather | solution.py:24
  136.1 4.2 gather_fusion.1
  140.3 5.2 fusion.8
  145.5 4.3 fusion.10
  149.9 0.0 all-gather.5.cloned.1.call-start
  149.9 122.3 %all-reduce.4.cloned.1.call-done = f32[2,128,128]{2,1,0:T(8,128)} async-done(((f32[2,128,128]{2,1,0:T(8,128)}), f32[2,128,128]{2,1,0:T(8,128)}) %all-reduce.4.cloned.1.call-update) | async-done | bytes 131088 | tf_op jit(solution)/shard_map/psum | solution.py:30
  272.2 1.4 multiply_reduce_fusion.1
  273.6 100.0 %all-reduce = (f32[]{:T(128)}, f32[]{:T(128)}) all-reduce(f32[]{:T(128)} %get-tuple-element.4, f32[]{:T(128)} %get-tuple-element.3), channel_id=1, replica_groups=mesh['op'=16,'sec'=32] {'op','sec'}, use_global_device_ids=true, to_apply=%region_4.0 | all-reduce | flops 2 | bytes 16 | tf_op jit(solution)/shard_map/psum | solution.py:36
  374.9 0.7 multiply_reduce_fusion
  375.6 94.1 %psum.38 = f32[]{:T(128)} all-reduce(f32[]{:T(128)} %multiply_reduce_fusion), channel_id=1, replica_groups=mesh['op'=16,'sec'=32] {'op','sec'}, use_global_device_ids=true, to_apply=%region_8.0 | all-reduce | flops 1 | bytes 8 | tf_op jit(solution)/shard_map/psum | solution.py:39
  470.4 0.1 broadcast_divide_fusion
  470.5 21.6 %all_gather.14 = f32[2,128,128]{2,1,0:T(8,128)} all-gather(f32[2,8,128]{2,1,0:T(8,128)S(1)} %broadcast_divide_fusion), channel_id=1, replica_groups=mesh['op'=16,'sec'=32] {'op'}, dimensions={1}, use_global_device_ids=true | all-gather | bytes 139264 | tf_op jit(solution)/shard_map/all_gather | solution.py:23
  492.1 0.2 all-reduce.6.cloned.1.call-start
  492.4 96.6 %all-gather.5.cloned.1.call-done = f32[64,128,128]{2,1,0:T(8,128)} async-done(((f32[2,128,128]{2,1,0:T(8,128)}), f32[64,128,128]{2,1,0:T(8,128)}) %all-gather.5.cloned.1.call-update) | async-done | bytes 4194320 | tf_op jit(solution)/shard_map/all_gather | solution.py:24
  588.9 4.2 gather_fusion.2
  593.1 5.2 fusion.6
  598.4 4.3 fusion.15
  602.7 122.4 %all-reduce.6.cloned.1.call-done = f32[2,128,128]{2,1,0:T(8,128)} async-done(((f32[2,128,128]{2,1,0:T(8,128)}), f32[2,128,128]{2,1,0:T(8,128)}) %all-reduce.6.cloned.1.call-update) | async-done | bytes 131088 | tf_op jit(solution)/shard_map/psum | solution.py:30
  725.0 1.4 multiply_multiply_fusion
  (20 shorter events, 0.1 us)
Async XLA Ops:
  7.2 133.1 %copy-start = (f32[16,2,128,128]{3,2,1,0:T(8,128)S(1)}, f32[16,2,128,128]{3,2,1,0:T(8,128)}, u32[]{:S(2)}) copy-start(f32[16,2,128,128]{3,2,1,0:T(8,128)} %param.7) | copy-start | bytes 6291460
  7.2 128.9 %all-gather.3.cloned.1.call-start = ((), (), s32[]{:S(2)}) async-start(), calls=%async_computation | async-start | bytes 4325376 | tf_op jit(solution)/shard_map/all_gather | solution.py:24
  33.8 238.4 %all-reduce.4.cloned.1.call-start = ((), (), s32[]{:S(2)}) async-start(), calls=%async_computation.1 | async-start | bytes 262144 | tf_op jit(solution)/shard_map/psum | solution.py:30
  140.3 5.2 copy-start.1
  145.5 126.7 %copy-start.3 = (f32[2,8,128]{2,1,0:T(8,128)S(1)}, f32[2,8,128]{2,1,0:T(8,128)}, u32[]{:S(2)}) copy-start(f32[2,8,128]{2,1,0:T(8,128)} %param.6) | copy-start | bytes 24580
  149.9 439.1 %all-gather.5.cloned.1.call-start = ((), (), s32[]{:S(2)}) async-start(), calls=%async_computation.2 | async-start | bytes 4325376 | tf_op jit(solution)/shard_map/all_gather | solution.py:24
  273.6 319.5 %copy-start.4 = (f32[2,8,128]{2,1,0:T(8,128)}, f32[2,8,128]{2,1,0:T(8,128)S(1)}, u32[]{:S(2)}) copy-start(f32[2,8,128]{2,1,0:T(8,128)S(1)} %get-tuple-element.9) | copy-start | bytes 24580
  470.5 122.6 %copy-start.5 = (f32[2,8,128]{2,1,0:T(8,128)}, f32[2,8,128]{2,1,0:T(8,128)S(1)}, u32[]{:S(2)}) copy-start(f32[2,8,128]{2,1,0:T(8,128)S(1)} %broadcast_divide_fusion) | copy-start | bytes 24580
  492.1 232.9 %all-reduce.6.cloned.1.call-start = ((), (), s32[]{:S(2)}) async-start(), calls=%async_computation.3 | async-start | bytes 262144 | tf_op jit(solution)/shard_map/psum | solution.py:30
  593.1 5.2 copy-start.2
Sparse Core Ops, SparseCore 0:
  34.0 102.0 all-gather.2
  150.0 122.2 all-reduce.3
  492.2 96.6 all-gather.4
  602.8 122.1 all-reduce.5
where the time goes:
time: 733 us
  waiting for transfers between devices  442 us (60%)
  blocking collectives  240 us (33%)
  matrix products  19 us (3%)
  between operations  15.9 us (2%)
  local copies, waits for them, and re-layouts  9.45 us (1%)
    psum x2, waiting for transfers between devices, apply(): summed = lax.psum(partial_sigma, 'op')  245 us
    all_gather x2, waiting for transfers between devices, apply(): whole = lax.all_gather(tall, 'sec', axis=0, tiled=True)  197 us
    psum x1, blocking collectives, on_device(): lax.psum((jnp.sum(start * sigma_first), jnp.sum(start * start)), ('op', '...  100 us
    psum x1, blocking collectives, on_device(): total = lax.psum(jnp.sum(resid * resid), ('op', 'sec'))  94.1 us
    all_gather x2, blocking collectives, apply(): tall = lax.all_gather(field, 'op', axis=1, tiled=True)  46.1 us
  transfers between devices with their start and end apart: 4, of which 4 were waited for; matrix products, arithmetic and copies ran while one was open for 0% of the time, Pallas kernels for 0%

commit v1 on v0

v1 whole, which is shorter than its diff:
```python
import itertools

import jax
import jax.numpy as jnp
from jax import lax
from jax.experimental import pallas as pl
from jax.experimental.pallas import tpu as pltpu
from jax.sharding import PartitionSpec as P

AXES = ("op", "sec")
F32 = jnp.float32
BF16 = jnp.bfloat16
SLOTS, ROWS, WIDTH, LOCAL_TERMS = 2, 8, 128, 16
SECTORS = 64
OPS, SECS = 16, 32
CHUNKS = 512


PLACES = list(itertools.product(range(4), range(2), range(2), range(8), range(4)))


def number(x, zl, core, y, zh):
    return ((((x * 2 + zl) * 2 + core) * 8) + y) * 4 + zh


def groups(key, order):
    found = {}
    for place in PLACES:
        found.setdefault(key(*place), []).append((order(*place), number(*place)))
    return [[device for _, device in sorted(members)] for members in found.values()]


def cube(x, zl, core, y, zh):
    z = 2 * zh + zl
    return (x - core) % 4 // 2, (y - core) % 8 // 2, (z - core) % 8 // 2, core


SAME_SEC = groups(lambda x, zl, core, y, zh: (y, zh), lambda x, zl, core, y, zh: (x, zl, core))
FAR = groups(lambda x, zl, core, y, zh: (x % 2, y % 2, zl, core), lambda x, zl, core, y, zh: (x // 2, y // 2, zh))
NEAR = groups(cube, lambda x, zl, core, y, zh: (x % 2, y % 2, zl))
OTHER_CORE = [
    (number(x, zl, core, y, zh), number(x, zl, 1 - core, y, zh)) for x, zl, core, y, zh in PLACES
]
ROW_STEPS = [(x % 2) * 256 + zl * 64 + (x // 2) * 32 for x in range(4) for zl in range(2)]


def exchange(parts, members):
    return lax.all_to_all(parts, AXES, 0, 0, axis_index_groups=members)


VMEM = pl.BlockSpec(memory_space=pltpu.VMEM)
SMEM = pl.BlockSpec(memory_space=pltpu.SMEM)


def call(body, outs, out_specs, in_specs, scratch=(), flops=0, moved=1 << 20):
    return pl.pallas_call(
        body,
        out_shape=outs,
        in_specs=in_specs,
        out_specs=out_specs,
        scratch_shapes=list(scratch),
        compiler_params=pltpu.CompilerParams(vmem_limit_bytes=40 << 20),
        cost_estimate=pl.CostEstimate(flops=flops, bytes_accessed=moved, transcendentals=0),
    )


def shape(*dims, dtype=F32):
    return jax.ShapeDtypeStruct(dims, dtype)


def row_mask(size, first_row):
    rows = first_row + lax.broadcasted_iota(jnp.int32, (ROWS, WIDTH), 0)
    cols = lax.broadcasted_iota(jnp.int32, (ROWS, WIDTH), 1)
    return (rows < size) & (cols < size)


def begin(place, psi, coupling, assign, sizes, start, copies, base, local_size, slot_of):
    for p in range(SECTORS):
        slot_of[assign[p]] = p
    for t in range(SLOTS):
        for k in range(LOCAL_TERMS):
            p = slot_of[coupling[t, k]]
            y = p // 8
            base[t, k] = (y % 2) * 128 + (y // 2) * 8 + p % 8
        size = sizes[assign[place[1] * SLOTS + t]]
        local_size[t] = size
        block = jnp.where(row_mask(size, place[0] * ROWS), psi[t], 0.0)
        start[t] = block
        for i in range(SECS):
            copies[i, t] = block


def halves(values):
    high = values.astype(BF16)
    return high, (values - high.astype(F32)).astype(BF16)


def split_envs(place, left, right, lefts, rights):
    core = place[0] % 2
    row = lax.broadcasted_iota(jnp.int32, (WIDTH, WIDTH), 0)
    col = lax.broadcasted_iota(jnp.int32, (WIDTH, WIDTH), 1)
    other = (row // 8 % 2 != core).astype(jnp.int32)
    order = (col == other * 64 + row // 16 * 8 + row % 8).astype(F32).astype(BF16)
    for k in range(LOCAL_TERMS):
        for t in range(SLOTS):
            high, low = halves(left[k, t])
            both = jnp.concatenate([high, low], axis=0)
            moved = lax.dot_general(both, order, (((1,), (0,)), ((), ())), preferred_element_type=F32).astype(BF16)
            lefts[k, t, :, :WIDTH] = moved[:WIDTH]
            lefts[k, t, :, WIDTH:] = moved[WIDTH:]
            high, low = halves(right[k, t].T)
            rights[k, t, :, :WIDTH] = high
            rights[k, t, :, WIDTH:] = low


def matmul(a, b):
    return lax.dot_general(a, b, (((1,), (0,)), ((), ())), preferred_element_type=F32)


def products(block_of, base, lefts, rights, store):
    for t in range(SLOTS):
        total = jnp.zeros((WIDTH, 2 * WIDTH), F32)
        for k in range(LOCAL_TERMS):
            high, low = halves(block_of(base[t, k]))
            pair = jnp.concatenate([high, low], axis=1)
            inner = matmul(lefts[k, t], jnp.concatenate([pair, pair], axis=0))
            high, low = halves(inner[:, :WIDTH] + inner[:, WIDTH:])
            rows = rights[k, t]
            total = total + matmul(
                jnp.concatenate([high, low], axis=1), jnp.concatenate([rows, rows], axis=0)
            )
        result = total[:, :WIDTH] + total[:, WIDTH:]
        for i in range(OPS):
            store(i, t, result[i * ROWS : (i + 1) * ROWS])


def gathered_block(mine, other, first):
    return jnp.concatenate(
        [mine[first + step] for step in ROW_STEPS] + [other[first + step] for step in ROW_STEPS], axis=0
    )


def apply_first(base, mine, other, lefts, rights, out):
    def store(i, t, rows):
        out[i, t] = rows

    products(lambda first: gathered_block(mine, other, first), base, lefts, rights, store)


def finish_first(place, local_size, parts, sigma, copies):
    for t in range(SLOTS):
        total = parts[0, t]
        for i in range(1, OPS):
            total = total + parts[i, t]
        total = jnp.where(row_mask(local_size[t], place[0] * ROWS), total, 0.0)
        sigma[t] = total
        for i in range(SECS):
            copies[i, t] = total


def scan(arrays, step, parts):
    lanes = 4

    def body(i, sums):
        sums = list(sums)
        for u in range(8):
            terms = step(*[a[i * 8 + u] for a in arrays])
            for n in range(parts):
                sums[n * lanes + u % lanes] = sums[n * lanes + u % lanes] + terms[n]
        return tuple(sums)

    zero = jnp.zeros((ROWS, WIDTH), F32)
    sums = lax.fori_loop(0, CHUNKS // 8, body, (zero,) * (parts * lanes))
    return [sum(sums[n * lanes : (n + 1) * lanes]) for n in range(parts)]


def whole_sum(values):
    return jnp.sum(jnp.sum(values, axis=1, keepdims=True), axis=0, keepdims=True)


def apply_next(
    base, start_mine, start_other, mine, other, lefts, rights, start, sigma, out, next_vector
):
    def moments(s, g):
        return s * g, s * s

    cross_a, square_a = scan((start_mine, mine), moments, 2)
    cross_b, square_b = scan((start_other, other), moments, 2)
    theta = whole_sum(cross_a + cross_b) / whole_sum(square_a + square_b)

    def residual(s, g):
        r = g - theta * s
        return (r * r,)

    (norm_a,) = scan((start_mine, mine), residual, 1)
    (norm_b,) = scan((start_other, other), residual, 1)
    scale = 1.0 / jnp.sqrt(whole_sum(norm_a + norm_b) + 1e-06)
    for t in range(SLOTS):
        next_vector[t] = (sigma[t] - theta * start[t]) * scale

    def block(first):
        return gathered_block(mine, other, first) - theta * gathered_block(start_mine, start_other, first)

    def store(i, t, rows):
        out[i, t] = rows * scale

    products(block, base, lefts, rights, store)


def finish_next(place, local_size, parts, sigma):
    for t in range(SLOTS):
        total = parts[0, t]
        for i in range(1, OPS):
            total = total + parts[i, t]
        sigma[t] = jnp.where(row_mask(local_size[t], place[0] * ROWS), total, 0.0)


def gather(copies):
    part = exchange(copies, FAR).reshape(1, CHUNKS // 8, ROWS, WIDTH)
    part = jnp.broadcast_to(part, (8, CHUNKS // 8, ROWS, WIDTH))
    mine = exchange(part, NEAR).reshape(CHUNKS, ROWS, WIDTH)
    return mine, lax.ppermute(mine, AXES, OTHER_CORE)


def on_device(psi, left_env, right_env, coupling, assign, sizes):
    place = jnp.stack([lax.axis_index("op"), lax.axis_index("sec")]).astype(jnp.int32)
    vec = shape(SLOTS, ROWS, WIDTH)
    copies_shape = shape(SECS, SLOTS, ROWS, WIDTH)
    parts_shape = shape(OPS, SLOTS, ROWS, WIDTH)
    env_shape = shape(LOCAL_TERMS, SLOTS, WIDTH, 2 * WIDTH, dtype=BF16)
    flops = 2 * 2 * 32 * 128 * 256 * 256

    start, copies, base, local_size = call(
        begin,
        (vec, copies_shape, shape(SLOTS, LOCAL_TERMS, dtype=jnp.int32), shape(SLOTS, dtype=jnp.int32)),
        (VMEM, VMEM, SMEM, SMEM),
        (SMEM, VMEM, SMEM, SMEM, SMEM),
        scratch=(pltpu.SMEM((SECTORS,), jnp.int32),),
    )(place, psi, coupling, assign, sizes)
    start_mine, start_other = gather(copies)
    lefts, rights = call(
        split_envs, (env_shape, env_shape), (VMEM, VMEM), (SMEM, VMEM, VMEM), flops=flops, moved=8 << 20
    )(place, left_env, right_env)
    parts = call(apply_first, parts_shape, VMEM, (SMEM,) + (VMEM,) * 4, flops=flops)(
        base, start_mine, start_other, lefts, rights
    )
    parts = exchange(parts, SAME_SEC)
    sigma_first, copies = call(finish_first, (vec, copies_shape), (VMEM, VMEM), (SMEM, SMEM, VMEM))(
        place, local_size, parts
    )
    mine, other = gather(copies)
    parts, next_vector = call(apply_next, (parts_shape, vec), (VMEM, VMEM), (SMEM,) + (VMEM,) * 8, flops=flops)(
        base, start_mine, start_other, mine, other, lefts, rights, start, sigma_first
    )
    parts = exchange(parts, SAME_SEC)
    sigma_next = call(finish_next, vec, VMEM, (SMEM, SMEM, VMEM))(place, local_size, parts)
    return sigma_first, next_vector, sigma_next


def solution(mesh):
    placed = (
        P("sec", "op", None),
        P("op", "sec", None, None),
        P("op", "sec", None, None),
        P("sec", "op"),
        P(),
        P(),
    )
    return jax.shard_map(
        on_device,
        mesh=mesh,
        in_specs=placed,
        out_specs=(P("sec", "op", None),) * 3,
        check_vma=False,
    )
```

time: 733 us -> 145 us (0.20)
  waiting for transfers between devices: 442 us -> 6.65 us
  blocking collectives: 240 us -> 118 us
  matrix products: 19 us -> 0 us
  between operations: 15.9 us -> 0.73 us
  Pallas kernels: 0 us -> 12.4 us
    psum x2 -> x0, waiting for transfers between devices: 245 us -> none  [apply(): summed = lax.psum(partial_sigma, 'op')]
    all_gather x2 -> x0, waiting for transfers between devices: 197 us -> none  [apply(): whole = lax.all_gather(tall, 'sec', axis=0, tiled=True)]
    psum x2 -> x0, blocking collectives: 194 us -> none  [the longest x1 100 us: on_device(): lax.psum((jnp.sum(start * sigma_first), jnp.sum(start * start)), ('op', '...]
    all_to_all x0 -> x6, blocking collectives: none -> 118 us  [exchange(): return lax.all_to_all(parts, AXES, 0, 0, axis_index_groups=members)]
    all_gather x2 -> x0, blocking collectives: 46.1 us -> none  [apply(): tall = lax.all_gather(field, 'op', axis=1, tiled=True)]
    dot_general x4 -> x0, matrix products: 19 us -> none  [the longest x2 10.5 us: apply(): jnp.einsum('tpij,ptjl->ptil', left_env, picked, precision=lax.Precision.H...]
    pallas_call x0 -> x6, Pallas kernels: none -> 12.4 us  [the longest x1 4.92 us: on_device(): call(apply_next, (parts_shape, vec), (VMEM, VMEM), (SMEM,) + (VMEM,) * 8,...]
    gather x4 -> x0, local copies, waits for them, and re-layouts: 9.17 us -> none  [the longest x2 8.39 us: apply(): picked = whole[source]]
  transfers between devices with their start and end apart: 4 -> 2, of which waited for: 4 -> 2; matrix products, arithmetic and copies ran while one was open for 0% -> 0% of each run, Pallas kernels for 0% -> 1%
where the time goes in v1:
time: 145 us; the launch traced here: 144 us
  blocking collectives  118 us (81%)
  Pallas kernels  12.4 us (9%)
  waiting for transfers between devices  6.65 us (5%)
  starting transfers between devices  3.9 us (3%)
  local copies, waits for them, and re-layouts  2.98 us (2%)
    all_to_all x6, blocking collectives, exchange(): return lax.all_to_all(parts, AXES, 0, 0, axis_index_groups=members)  118 us
    ppermute x2, waiting for transfers between devices, gather(): return (mine, lax.ppermute(mine, AXES, OTHER_CORE))  6.65 us
    pallas_call x1, Pallas kernels, on_device(): call(apply_next, (parts_shape, vec), (VMEM, VMEM), (SMEM,) + (VMEM,) * 8,...  4.92 us
    ppermute x2, starting transfers between devices, gather(): return (mine, lax.ppermute(mine, AXES, OTHER_CORE))  3.9 us
  transfers between devices with their start and end apart: 2, of which 2 were waited for; matrix products, arithmetic and copies ran while one was open for 0% of the time, Pallas kernels for 1%

profile of v1, /device:TPU:1, one launch (start us, length us, event | category | flops | bytes accessed | tf_op | source)
XLA Modules:
  0.0 144.4 jit_solution(14588158379832685537)
XLA Ops:
  0.6 0.1 pad_add_fusion.place
  0.7 0.0 copy-start.3
  0.7 0.7 copy-done.3
  1.4 0.0 copy-start.4
  1.4 0.7 copy-done.4
  2.1 0.0 copy-start.5
  2.1 0.7 copy-done.5
  2.7 0.7 copy-done.6
  3.4 1.6 %shard_map.85 = (f32[2,8,128]{2,1,0:T(8,128)S(1)}, f32[32,2,8,128]{3,2,1,0:T(8,128)S(1)}, s32[2,16]{1,0:T(2,128)S(1)}, s32[2]{0:T(128)S(1)}) custom-call(s32[2]{0:T(128)S(1)} %pad_add_fusion.place, f32[2,8,128]{2,1,0:T(8,128)S(1)} %copy-done.3, s32[2,16]{1,0:T(2,128)S(1)} %copy-done.4, s32[64]{0:T(128)S(1)} %copy-done.5, s32[64]{0:T(128)S(1)} %copy-done.6), custom_call_target="tpu_custom_call" | custom-call | bytes 1048576 | tf_op jit(solution)/shard_map/pallas_call | solution.py:233
  5.0 33.1 %all_to_all.30 = f32[32,2,8,128]{3,2,1,0:T(8,128)S(1)} all-to-all(f32[32,2,8,128]{3,2,1,0:T(8,128)S(1)} %get-tuple-element.15), channel_id=1, replica_groups={{0,1,2,3,8,9,10,11,16,17,18,19,24,25,26,27,256,257,258,259,264,265,266,..., dimensions={0} | all-to-all | bytes 524288 | tf_op jit(solution)/shard_map/all_to_all | solution.py:48
  38.2 0.1 broadcast_in_dim.15
  38.3 0.0 copy-start
  38.3 0.0 copy-start.1
  38.4 22.0 %all_to_all.31 = f32[8,64,8,128]{3,2,1,0:T(8,128)S(1)} all-to-all(f32[8,64,8,128]{3,2,1,0:T(8,128)S(1)} %broadcast_in_dim.15), channel_id=1, replica_groups={{0,64,4,68,128,192,132,196},{1,65,5,69,129,193,133,197},{2,66,6,70,130,..., dimensions={0} | all-to-all | bytes 4194304 | tf_op jit(solution)/shard_map/all_to_all | solution.py:48
  60.4 2.0 %collective-permute-start = (f32[512,8,128]{2,1,0:T(8,128)S(1)}, f32[512,8,128]{2,1,0:T(8,128)S(1)}, u32[]{:S(2)}, u32[]{:S(2)}) collective-permute-start(f32[512,8,128]{2,1,0:T(8,128)S(1)} %bitcast.6), channel_id=1, source_target_pairs={{0,32},{1,33},{2,34},{3,35},{4,36},{5,37},{6,38},{7,39},{8,40},{9,... | collective-permute-start | bytes 6291464 | tf_op jit(solution)/shard_map/ppermute | solution.py:222
  62.4 0.0 copy-done
  62.4 0.0 copy-done.1
  62.4 1.5 %shard_map.86 = (bf16[16,2,128,256]{3,2,1,0:T(8,128)(2,1)S(1)}, bf16[16,2,128,256]{3,2,1,0:T(8,128)(2,1)S(1)}) custom-call(s32[2]{0:T(128)S(1)} %pad_add_fusion.place, f32[16,2,128,128]{3,2,1,0:T(8,128)S(1)} %copy-done, f32[16,2,128,128]{3,2,1,0:T(8,128)S(1)} %copy-done.1), custom_call_target="tpu_custom_call" | custom-call | flops 1073741824 | bytes 8388608 | tf_op jit(solution)/shard_map/pallas_call | solution.py:241
  63.9 2.5 %collective-permute-done.other.start_other = f32[512,8,128]{2,1,0:T(8,128)S(1)} collective-permute-done((f32[512,8,128]{2,1,0:T(8,128)S(1)}, f32[512,8,128]{2,1,0:T(8,128)S(1)}, u32[]{:S(2)}, u32[]{:S(2)}) %collective-permute-start) | collective-permute-done | bytes 2097184 | tf_op jit(solution)/shard_map/ppermute | solution.py:222
  66.4 2.0 %shard_map.87 = f32[16,2,8,128]{3,2,1,0:T(8,128)S(1)} custom-call(s32[2,16]{1,0:T(2,128)S(1)} %get-tuple-element.14.base, f32[512,8,128]{2,1,0:T(8,128)S(1)} %bitcast.7, f32[512,8,128]{2,1,0:T(8,128)S(1)} %collective-permute-done.other.start_other, bf16[16,2,128,256]{3,2,1,0:T(8,128)(2,1)S(1)} %get-tuple-element.16.lefts, ...), custom_call_target="tpu_custom_call" | custom-call | flops 1073741824 | bytes 1048576 | tf_op jit(solution)/shard_map/pallas_call | solution.py:244
  68.4 9.2 %all_to_all.32.parts = f32[16,2,8,128]{3,2,1,0:T(8,128)S(1)} all-to-all(f32[16,2,8,128]{3,2,1,0:T(8,128)S(1)} %shard_map.87), channel_id=1, replica_groups={{0,32,64,96,128,160,192,224,256,288,320,352,384,416,448,480},{1,33,65,9..., dimensions={0} | all-to-all | bytes 262144 | tf_op jit(solution)/shard_map/all_to_all | solution.py:48
  77.6 1.2 shard_map.88
  78.8 22.4 %all_to_all.33 = f32[32,2,8,128]{3,2,1,0:T(8,128)S(1)} all-to-all(f32[32,2,8,128]{3,2,1,0:T(8,128)S(1)} %get-tuple-element.19), channel_id=1, replica_groups={{0,1,2,3,8,9,10,11,16,17,18,19,24,25,26,27,256,257,258,259,264,265,266,..., dimensions={0} | all-to-all | bytes 524288 | tf_op jit(solution)/shard_map/all_to_all | solution.py:48
  101.2 0.1 broadcast_in_dim.17
  101.4 0.0 copy-start.2
  101.4 22.1 %all_to_all.34 = f32[8,64,8,128]{3,2,1,0:T(8,128)S(1)} all-to-all(f32[8,64,8,128]{3,2,1,0:T(8,128)S(1)} %broadcast_in_dim.17), channel_id=1, replica_groups={{0,64,4,68,128,192,132,196},{1,65,5,69,129,193,133,197},{2,66,6,70,130,..., dimensions={0} | all-to-all | bytes 4194304 | tf_op jit(solution)/shard_map/all_to_all | solution.py:48
  123.5 1.9 %collective-permute-start.1 = (f32[512,8,128]{2,1,0:T(8,128)S(1)}, f32[512,8,128]{2,1,0:T(8,128)S(1)}, u32[]{:S(2)}, u32[]{:S(2)}) collective-permute-start(f32[512,8,128]{2,1,0:T(8,128)S(1)} %bitcast.9), channel_id=1, source_target_pairs={{0,32},{1,33},{2,34},{3,35},{4,36},{5,37},{6,38},{7,39},{8,40},{9,... | collective-permute-start | bytes 6291464 | tf_op jit(solution)/shard_map/ppermute | solution.py:222
  125.5 4.1 %collective-permute-done.1.other = f32[512,8,128]{2,1,0:T(8,128)S(1)} collective-permute-done((f32[512,8,128]{2,1,0:T(8,128)S(1)}, f32[512,8,128]{2,1,0:T(8,128)S(1)}, u32[]{:S(2)}, u32[]{:S(2)}) %collective-permute-start.1) | collective-permute-done | bytes 2097184 | tf_op jit(solution)/shard_map/ppermute | solution.py:222
  129.6 0.0 copy-done.2
  129.6 4.9 %shard_map.89 = (f32[16,2,8,128]{3,2,1,0:T(8,128)S(1)}, f32[2,8,128]{2,1,0:T(8,128)}) custom-call(s32[2,16]{1,0:T(2,128)S(1)} %get-tuple-element.14.base, f32[512,8,128]{2,1,0:T(8,128)S(1)} %bitcast.8, f32[512,8,128]{2,1,0:T(8,128)S(1)} %collective-permute-done.other.start_other, f32[512,8,128]{2,1,0:T(8,128)S(1)} %bitcast.10, ...), custom_call_target="tpu_custom_call" | custom-call | flops 1073741824 | bytes 1048576 | tf_op jit(solution)/shard_map/pallas_call | solution.py:252
  134.5 8.7 %all_to_all.35.parts = f32[16,2,8,128]{3,2,1,0:T(8,128)S(1)} all-to-all(f32[16,2,8,128]{3,2,1,0:T(8,128)S(1)} %get-tuple-element.22), channel_id=1, replica_groups={{0,32,64,96,128,160,192,224,256,288,320,352,384,416,448,480},{1,33,65,9..., dimensions={0} | all-to-all | bytes 262144 | tf_op jit(solution)/shard_map/all_to_all | solution.py:48
  143.3 1.2 shard_map.90
  (1 shorter events, 0.0 us)
Async XLA Ops:
  0.7 0.7 copy-start.3
  1.4 0.7 copy-start.4
  2.1 0.7 copy-start.5
  2.7 0.7 copy-start.6
  38.3 24.0 %copy-start = (f32[16,2,128,128]{3,2,1,0:T(8,128)S(1)}, f32[16,2,128,128]{3,2,1,0:T(8,128)}, u32[]{:S(2)}) copy-start(f32[16,2,128,128]{3,2,1,0:T(8,128)} %left.1) | copy-start | bytes 6291460
  38.3 24.0 %copy-start.1 = (f32[16,2,128,128]{3,2,1,0:T(8,128)S(1)}, f32[16,2,128,128]{3,2,1,0:T(8,128)}, u32[]{:S(2)}) copy-start(f32[16,2,128,128]{3,2,1,0:T(8,128)} %right.1) | copy-start | bytes 6291460
  60.4 6.0 %collective-permute-start = (f32[512,8,128]{2,1,0:T(8,128)S(1)}, f32[512,8,128]{2,1,0:T(8,128)S(1)}, u32[]{:S(2)}, u32[]{:S(2)}) collective-permute-start(f32[512,8,128]{2,1,0:T(8,128)S(1)} %bitcast.6), channel_id=1, source_target_pairs={{0,32},{1,33},{2,34},{3,35},{4,36},{5,37},{6,38},{7,39},{8,40},{9,... | collective-permute-start | bytes 6291464 | tf_op jit(solution)/shard_map/ppermute | solution.py:222
  101.4 28.2 %copy-start.2 = (f32[2,8,128]{2,1,0:T(8,128)S(1)}, f32[2,8,128]{2,1,0:T(8,128)}, u32[]{:S(2)}) copy-start(f32[2,8,128]{2,1,0:T(8,128)} %get-tuple-element.10.sigma) | copy-start | bytes 24580
  123.5 6.0 %collective-permute-start.1 = (f32[512,8,128]{2,1,0:T(8,128)S(1)}, f32[512,8,128]{2,1,0:T(8,128)S(1)}, u32[]{:S(2)}, u32[]{:S(2)}) collective-permute-start(f32[512,8,128]{2,1,0:T(8,128)S(1)} %bitcast.9), channel_id=1, source_target_pairs={{0,32},{1,33},{2,34},{3,35},{4,36},{5,37},{6,38},{7,39},{8,40},{9,... | collective-permute-start | bytes 6291464 | tf_op jit(solution)/shard_map/ppermute | solution.py:222

commit v2 on v1

v2 whole, which is shorter than its diff:
```python
import itertools

import jax
import jax.numpy as jnp
from jax import lax
from jax.experimental import pallas as pl
from jax.experimental.pallas import tpu as pltpu
from jax.sharding import PartitionSpec as P

AXES = ("op", "sec")
F32 = jnp.float32
BF16 = jnp.bfloat16
SLOTS, ROWS, WIDTH, LOCAL_TERMS = 2, 8, 128, 16
SECTORS = 64
OPS, SECS = 16, 32
CHUNKS = 512


PLACES = list(itertools.product(range(4), range(2), range(2), range(8), range(4)))


def number(x, zl, core, y, zh):
    return ((((x * 2 + zl) * 2 + core) * 8) + y) * 4 + zh


def groups(key, order):
    found = {}
    for place in PLACES:
        found.setdefault(key(*place), []).append((order(*place), number(*place)))
    return [[device for _, device in sorted(members)] for members in found.values()]


def cube(x, zl, core, y, zh):
    z = 2 * zh + zl
    return (x - core) % 4 // 2, (y - core) % 8 // 2, (z - core) % 8 // 2, core


SAME_SEC = groups(lambda x, zl, core, y, zh: (y, zh), lambda x, zl, core, y, zh: (x, zl, core))
FAR = groups(lambda x, zl, core, y, zh: (x % 2, y % 2, zl, core), lambda x, zl, core, y, zh: (y // 2, zh, x // 2))
FAR_YZ = groups(lambda x, zl, core, y, zh: (x, y % 2, zl, core), lambda x, zl, core, y, zh: (y // 2, zh))
NEAR = groups(cube, lambda x, zl, core, y, zh: (x % 2, y % 2, zl))
OTHER_CORE = [
    (number(x, zl, core, y, zh), number(x, zl, 1 - core, y, zh)) for x, zl, core, y, zh in PLACES
]
ROW_STEPS = [(x % 2) * 256 + zl * 64 + (x // 2) * 2 for x in range(4) for zl in range(2)]


def exchange(parts, members):
    return lax.all_to_all(parts, AXES, 0, 0, axis_index_groups=members)


VMEM = pl.BlockSpec(memory_space=pltpu.VMEM)
SMEM = pl.BlockSpec(memory_space=pltpu.SMEM)
HBM = pl.BlockSpec(memory_space=pltpu.HBM)


def call(body, outs, out_specs, in_specs, scratch=(), flops=0, moved=1 << 20, aliases=None):
    return pl.pallas_call(
        body,
        out_shape=outs,
        in_specs=in_specs,
        out_specs=out_specs,
        scratch_shapes=list(scratch),
        input_output_aliases=aliases or {},
        compiler_params=pltpu.CompilerParams(vmem_limit_bytes=40 << 20),
        cost_estimate=pl.CostEstimate(flops=flops, bytes_accessed=moved, transcendentals=0),
    )


def shape(*dims, dtype=F32):
    return jax.ShapeDtypeStruct(dims, dtype)


def inside(size, first_row):
    rows = first_row + lax.broadcasted_iota(jnp.int32, (ROWS, WIDTH), 0)
    cols = lax.broadcasted_iota(jnp.int32, (ROWS, WIDTH), 1)
    return (rows < size) & (cols < size)


def fetch(pairs, done):
    copies = [pltpu.make_async_copy(source, target, done.at[i]) for i, (source, target) in enumerate(pairs)]
    for copy in copies:
        copy.start()
    for copy in copies:
        copy.wait()


def halves(values):
    high = values.astype(BF16)
    return high, (values - high.astype(F32)).astype(BF16)


def prepare(
    coupling_hbm, assign_hbm, sizes_hbm, left, right, base, size_of, masks, lefts, rights, coupling, assign, sizes, slot_of, done
):
    fetch([(coupling_hbm, coupling), (assign_hbm, assign), (sizes_hbm, sizes)], done)
    op = lax.axis_index("op")
    for p in range(SECTORS):
        sector = assign[p]
        slot_of[sector] = p
        size_of[p] = sizes[sector]
    for t in range(SLOTS):
        for k in range(LOCAL_TERMS):
            p = slot_of[coupling[t, k]]
            y = p // 8
            base[t, k] = (y % 2) * 128 + (y // 2) * 16 + p % 8 // 2 * 4 + p % 2
        size = size_of[lax.axis_index("sec") * SLOTS + t]
        for xh in range(2):
            masks[xh, t] = inside(size, (xh * 8 + op % 8) * ROWS).astype(F32)
    row = lax.broadcasted_iota(jnp.int32, (WIDTH, WIDTH), 0)
    col = lax.broadcasted_iota(jnp.int32, (WIDTH, WIDTH), 1)
    other = (row // 8 % 2 != op % 2).astype(jnp.int32)
    order = (col == other * 64 + row // 16 * 8 + row % 8).astype(F32).astype(BF16)
    for k in range(LOCAL_TERMS):
        for t in range(SLOTS):
            size = sizes[coupling[t, k]]
            high, low = halves(jnp.where(col < size, left[k, t], 0.0))
            moved = matmul(jnp.concatenate([high, low], axis=0), order).astype(BF16)
            lefts[k, t, :, :WIDTH] = moved[:WIDTH]
            lefts[k, t, :, WIDTH:] = moved[WIDTH:]
            high, low = halves(jnp.where(col < size, right[k, t], 0.0).T)
            rights[k, t, :, :WIDTH] = high
            rights[k, t, :, WIDTH:] = low


def matmul(a, b):
    return lax.dot_general(a, b, (((1,), (0,)), ((), ())), preferred_element_type=F32)


def products(block_of, base, lefts, rights, store, beside=None):
    results = []
    for t in range(SLOTS):
        total = jnp.zeros((WIDTH, 2 * WIDTH), F32)
        for k in range(LOCAL_TERMS):
            if beside is not None:
                beside(t * LOCAL_TERMS + k)
            high, low = halves(block_of(base[t, k]))
            pair = jnp.concatenate([high, low], axis=1)
            inner = matmul(lefts[k, t], jnp.concatenate([pair, pair], axis=0))
            high, low = halves(inner[:, :WIDTH] + inner[:, WIDTH:])
            rows = rights[k, t]
            total = total + matmul(
                jnp.concatenate([high, low], axis=1), jnp.concatenate([rows, rows], axis=0)
            )
        results.append(total[:, :WIDTH] + total[:, WIDTH:])
    for t in range(SLOTS):
        for i in range(OPS):
            store(i, t, results[t][i * ROWS : (i + 1) * ROWS])


def gathered_block(mine, other, first):
    return jnp.concatenate(
        [mine[first + step] for step in ROW_STEPS] + [other[first + step] for step in ROW_STEPS], axis=0
    )


def apply_first(base, mine, other, lefts, rights, out):
    def store(i, t, rows):
        for x in range(2):
            out[x * 8 + i % 8, i // 8, t] = rows

    products(lambda first: gathered_block(mine, other, first), base, lefts, rights, store)


def finish_first(masks, parts, sigma, copies):
    mine = lax.axis_index("op") // 8
    for xh in range(2):
        for t in range(SLOTS):
            total = parts[0, xh, t]
            for i in range(1, OPS):
                total = total + parts[i, xh, t]
            total = total * masks[xh, t]
            for i in range(OPS):
                copies[i, xh, t] = total
    for t in range(SLOTS):
        sigma[t] = copies[0, mine, t]


LANES = 4


def scan(step, sums):
    def body(i, sums):
        sums = list(sums)
        for u in range(16):
            for n, term in enumerate(step(i * 16 + u)):
                sums[n * LANES + u % LANES] = sums[n * LANES + u % LANES] + term
        return tuple(sums)

    zero = jnp.zeros((ROWS, WIDTH), F32)
    sums = lax.fori_loop(0, CHUNKS // 16, body, (zero,) * (sums * LANES))
    return [sum(sums[n : n + LANES]) for n in range(0, len(sums), LANES)]


def moments(size_of, start_mine, start_other, mine, masked_mine, masked_other, sums):
    core = lax.axis_index("op") % 2
    rows = lax.broadcasted_iota(jnp.int32, (ROWS, WIDTH), 0)
    cols = lax.broadcasted_iota(jnp.int32, (ROWS, WIDTH), 1)

    def body(i, sums):
        sums = list(sums)
        xl, yl, zl, yh = i // 16, i // 8 % 2, i // 4 % 2, i % 4
        for u in range(16):
            zh, xh, t = u // 4, u // 2 % 2, u % 2
            size = size_of[(yh * 2 + yl) * 8 + zh * 2 + t]
            pair = (xh * 4 + xl * 2 + zl) * 2
            here = i * 16 + u
            wide = cols < size
            m = jnp.where(wide & (rows < size - (pair + core) * ROWS), start_mine[here], 0.0)
            o = jnp.where(wide & (rows < size - (pair + 1 - core) * ROWS), start_other[here], 0.0)
            masked_mine[here] = m
            masked_other[here] = o
            lane = u % LANES
            sums[lane] = sums[lane] + m * mine[here]
            sums[LANES + lane] = sums[LANES + lane] + (m * m + o * o)
        return tuple(sums)

    totals = lax.fori_loop(0, CHUNKS // 16, body, (jnp.zeros((ROWS, WIDTH), F32),) * (2 * LANES))
    sums[0] = sum(totals[:LANES])
    sums[1] = sum(totals[LANES:])


def whole_sum(values):
    return jnp.sum(jnp.sum(values, axis=1, keepdims=True), axis=0, keepdims=True)


def apply_next(
    base, start_mine, start_other, mine, other, lefts, rights, psi, masks, sigma, sums, out, next_vector
):
    (cross,) = scan(lambda i: (start_other[i] * other[i],), 1)
    theta = whole_sum(cross + sums[0]) / whole_sum(sums[1])
    norms = [jnp.zeros((ROWS, WIDTH), F32)] * LANES

    def beside(n):
        each = CHUNKS // (SLOTS * LOCAL_TERMS)
        for i in range(n * each, (n + 1) * each):
            for s, g in ((start_mine, mine), (start_other, other)):
                r = g[i] - theta * s[i]
                norms[i % LANES] = norms[i % LANES] + r * r

    def block(first):
        return gathered_block(mine, other, first) - theta * gathered_block(start_mine, start_other, first)

    scale = []

    def store(i, t, rows):
        if not scale:
            scale.append(1.0 / jnp.sqrt(whole_sum(sum(norms)) + 1e-06))
        out[i, t] = rows * scale[0]

    products(block, base, lefts, rights, store, beside)
    xh = lax.axis_index("op") // 8
    for t in range(SLOTS):
        next_vector[t] = (sigma[t] - theta * (psi[t] * masks[xh, t])) * scale[0]


def finish_next(masks, parts, sigma):
    mine = lax.axis_index("op") // 8
    for t in range(SLOTS):
        total = parts[0, t]
        for i in range(1, OPS):
            total = total + parts[i, t]
        sigma[t] = total * masks[mine, t]


def gather(copies, far):
    part = exchange(copies, far).reshape(1, CHUNKS // 8, ROWS, WIDTH)
    part = jnp.broadcast_to(part, (8, CHUNKS // 8, ROWS, WIDTH))
    mine = exchange(part, NEAR).reshape(CHUNKS, ROWS, WIDTH)
    return mine, lax.ppermute(mine, AXES, OTHER_CORE)


def on_device(psi, left_env, right_env, coupling, assign, sizes):
    ints = jnp.int32
    vec = shape(SLOTS, ROWS, WIDTH)
    env_shape = shape(LOCAL_TERMS, SLOTS, WIDTH, 2 * WIDTH, dtype=BF16)
    flops = 2 * 2 * 32 * 128 * 256 * 256

    start_mine, start_other = gather(jnp.broadcast_to(psi[None], (SECS,) + psi.shape), FAR)
    base, size_of, masks, lefts, rights = call(
        prepare,
        (
            shape(SLOTS, LOCAL_TERMS, dtype=ints),
            shape(SECTORS, dtype=ints),
            shape(2, SLOTS, ROWS, WIDTH),
            env_shape,
            env_shape,
        ),
        (SMEM, SMEM, VMEM, VMEM, VMEM),
        (HBM,) * 3 + (VMEM,) * 2,
        scratch=(
            pltpu.SMEM((SLOTS, LOCAL_TERMS), ints),
            pltpu.SMEM((SECTORS,), ints),
            pltpu.SMEM((SECTORS,), ints),
            pltpu.SMEM((SECTORS,), ints),
            pltpu.SemaphoreType.DMA((3,)),
        ),
        flops=flops,
        moved=8 << 20,
    )(coupling, assign, sizes, left_env, right_env)
    parts = call(apply_first, shape(OPS, 2, SLOTS, ROWS, WIDTH), VMEM, (SMEM,) + (VMEM,) * 4, flops=flops)(
        base, start_mine, start_other, lefts, rights
    )
    parts = exchange(parts, SAME_SEC)
    sigma_first, copies = call(
        finish_first, (vec, shape(OPS, 2, SLOTS, ROWS, WIDTH)), (VMEM, VMEM), (VMEM, VMEM)
    )(masks, parts)
    mine, other = gather(copies, FAR_YZ)
    whole = shape(CHUNKS, ROWS, WIDTH)
    start_mine, start_other, sums = call(
        moments,
        (whole, whole, shape(2, ROWS, WIDTH)),
        (VMEM,) * 3,
        (SMEM,) + (VMEM,) * 3,
        flops=flops,
        aliases={1: 0, 2: 1},
    )(size_of, start_mine, start_other, mine)
    parts, next_vector = call(
        apply_next, (shape(OPS, SLOTS, ROWS, WIDTH), vec), (VMEM, VMEM), (SMEM,) + (VMEM,) * 10, flops=flops
    )(base, start_mine, start_other, mine, other, lefts, rights, psi, masks, sigma_first, sums)
    parts = exchange(parts, SAME_SEC)
    sigma_next = call(finish_next, vec, VMEM, (VMEM, VMEM))(masks, parts)
    return sigma_first, next_vector, sigma_next


def solution(mesh):
    placed = (
        P("sec", "op", None),
        P("op", "sec", None, None),
        P("op", "sec", None, None),
        P("sec", "op"),
        P(),
        P(),
    )
    return jax.shard_map(
        on_device,
        mesh=mesh,
        in_specs=placed,
        out_specs=(P("sec", "op", None),) * 3,
        check_vma=False,
    )
```

time: 145 us -> 138 us (0.952)
  waiting for transfers between devices: 6.65 us -> 1.35 us
  local copies, waits for them, and re-layouts: 2.98 us -> 1.03 us
    ppermute x2, waiting for transfers between devices: 6.65 us -> 1.35 us  [gather(): return (mine, lax.ppermute(mine, AXES, OTHER_CORE))]
    unnamed x14, local copies, waits for them, and re-layouts: 2.7 us -> 0.04 us
  transfers between devices with their start and end apart: 2 -> 2, of which waited for: 2 -> 2; matrix products, arithmetic and copies ran while one was open for 0% -> 0% of each run, Pallas kernels for 1% -> 5%
where the time goes in v2:
time: 138 us; the launch traced here: 137 us
  blocking collectives  117 us (85%)
  Pallas kernels  13.1 us (9%)
  starting transfers between devices  4.02 us (3%)
    all_to_all x6, blocking collectives, exchange(): return lax.all_to_all(parts, AXES, 0, 0, axis_index_groups=members)  117 us
    ppermute x2, starting transfers between devices, gather(): return (mine, lax.ppermute(mine, AXES, OTHER_CORE))  4.02 us
    pallas_call x1, Pallas kernels, on_device(): call(moments, (whole, whole, shape(2, ROWS, WIDTH)), (VMEM,) * 3, (SMEM,)...  3.66 us
    pallas_call x1, Pallas kernels, on_device(): call(apply_next, (shape(OPS, SLOTS, ROWS, WIDTH), vec), (VMEM, VMEM), (SM...  3.27 us
    pallas_call x1, Pallas kernels, on_device(): call(prepare, (shape(SLOTS, LOCAL_TERMS, dtype=ints), shape(SECTORS, dtyp...  2.95 us
  transfers between devices with their start and end apart: 2, of which 2 were waited for; matrix products, arithmetic and copies ran while one was open for 0% of the time, Pallas kernels for 5%

profile of v2, /device:TPU:1, one launch (start us, length us, event | category | flops | bytes accessed | tf_op | source)
XLA Modules:
  0.0 137.3 jit_solution(15016028044641690645)
XLA Ops:
  0.6 0.7 broadcast_in_dim.20
  1.3 33.6 %all_to_all.30 = f32[32,2,8,128]{3,2,1,0:T(8,128)S(1)} all-to-all(f32[32,2,8,128]{3,2,1,0:T(8,128)S(1)} %broadcast_in_dim.20), channel_id=1, replica_groups={{0,256,1,257,2,258,3,259,8,264,9,265,10,266,11,267,16,272,17,273,18,274..., dimensions={0} | all-to-all | bytes 524288 | tf_op jit(solution)/shard_map/all_to_all | solution.py:49
  34.9 0.1 broadcast_in_dim.22
  35.1 0.0 copy-start
  35.1 0.0 copy-start.1
  35.1 0.0 copy-start.4
  35.1 0.0 copy-start.5
  35.1 22.0 %all_to_all.31 = f32[8,64,8,128]{3,2,1,0:T(8,128)S(1)} all-to-all(f32[8,64,8,128]{3,2,1,0:T(8,128)S(1)} %broadcast_in_dim.22), channel_id=1, replica_groups={{0,64,4,68,128,192,132,196},{1,65,5,69,129,193,133,197},{2,66,6,70,130,..., dimensions={0} | all-to-all | bytes 4194304 | tf_op jit(solution)/shard_map/all_to_all | solution.py:49
  57.1 2.1 %collective-permute-start = (f32[512,8,128]{2,1,0:T(8,128)S(1)}, f32[512,8,128]{2,1,0:T(8,128)S(1)}, u32[]{:S(2)}, u32[]{:S(2)}) collective-permute-start(f32[512,8,128]{2,1,0:T(8,128)S(1)} %bitcast.4), channel_id=1, source_target_pairs={{0,32},{1,33},{2,34},{3,35},{4,36},{5,37},{6,38},{7,39},{8,40},{9,... | collective-permute-start | bytes 6291464 | tf_op jit(solution)/shard_map/ppermute | solution.py:270
  59.2 0.0 copy-done.6
  59.3 0.0 copy-done
  59.3 0.0 copy-done.1
  59.3 0.0 copy-done.4
  59.3 0.0 copy-done.5
  59.3 3.0 %shard_map.85 = (s32[2,16]{1,0:T(2,128)S(1)}, s32[64]{0:T(128)S(1)}, f32[2,2,8,128]{3,2,1,0:T(8,128)S(1)}, bf16[16,2,128,256]{3,2,1,0:T(8,128)(2,1)S(1)}, bf16[16,2,128,256]{3,2,1,0:T(8,128)(2,1)S(1)}) custom-call(s32[2,16]{1,0:T(2,128)S(1)} %copy-done.4, s32[64]{0:T(128)S(1)} %copy-done.5, s32[64]{0:T(128)S(1)} %copy-done.6, ...), custom_call_target="tpu_custom_call" | custom-call | flops 1073741824 | bytes 8388608 | tf_op jit(solution)/shard_map/pallas_call | solution.py:280
  62.3 0.9 collective-permute-done.other.start_other
  63.2 2.0 %shard_map.86 = f32[16,2,2,8,128]{4,3,2,1,0:T(8,128)S(1)} custom-call(s32[2,16]{1,0:T(2,128)S(1)} %get-tuple-element.16.base, f32[512,8,128]{2,1,0:T(8,128)S(1)} %bitcast.5, f32[512,8,128]{2,1,0:T(8,128)S(1)} %collective-permute-done.other.start_other, bf16[16,2,128,256]{3,2,1,0:T(8,128)(2,1)S(1)} %get-tuple-element.17.lefts, ...), custom_call_target="tpu_custom_call" | custom-call | flops 1073741824 | bytes 1048576 | tf_op jit(solution)/shard_map/pallas_call | solution.py:301
  65.2 10.8 %all_to_all.32.parts = f32[16,2,2,8,128]{4,3,2,1,0:T(8,128)S(1)} all-to-all(f32[16,2,2,8,128]{4,3,2,1,0:T(8,128)S(1)} %shard_map.86), channel_id=1, replica_groups={{0,32,64,96,128,160,192,224,256,288,320,352,384,416,448,480},{1,33,65,9..., dimensions={0} | all-to-all | bytes 524288 | tf_op jit(solution)/shard_map/all_to_all | solution.py:49
  76.0 0.6 shard_map.87
  76.6 18.9 %all_to_all.33 = f32[16,2,2,8,128]{4,3,2,1,0:T(8,128)S(1)} all-to-all(f32[16,2,2,8,128]{4,3,2,1,0:T(8,128)S(1)} %get-tuple-element.21), channel_id=1, replica_groups={{0,1,2,3,8,9,10,11,16,17,18,19,24,25,26,27},{4,5,6,7,12,13,14,15,20,21,..., dimensions={0} | all-to-all | bytes 524288 | tf_op jit(solution)/shard_map/all_to_all | solution.py:49
  95.5 0.1 broadcast_in_dim.24
  95.7 22.9 %all_to_all.34 = f32[8,64,8,128]{3,2,1,0:T(8,128)S(1)} all-to-all(f32[8,64,8,128]{3,2,1,0:T(8,128)S(1)} %broadcast_in_dim.24), channel_id=1, replica_groups={{0,64,4,68,128,192,132,196},{1,65,5,69,129,193,133,197},{2,66,6,70,130,..., dimensions={0} | all-to-all | bytes 4194304 | tf_op jit(solution)/shard_map/all_to_all | solution.py:49
  118.6 1.9 %collective-permute-start.1 = (f32[512,8,128]{2,1,0:T(8,128)S(1)}, f32[512,8,128]{2,1,0:T(8,128)S(1)}, u32[]{:S(2)}, u32[]{:S(2)}) collective-permute-start(f32[512,8,128]{2,1,0:T(8,128)S(1)} %bitcast.7), channel_id=1, source_target_pairs={{0,32},{1,33},{2,34},{3,35},{4,36},{5,37},{6,38},{7,39},{8,40},{9,... | collective-permute-start | bytes 6291464 | tf_op jit(solution)/shard_map/ppermute | solution.py:270
  120.5 0.0 copy-start.2
  120.5 0.0 copy-start.3
  120.5 3.7 %shard_map.88 = (f32[512,8,128]{2,1,0:T(8,128)S(1)}, f32[512,8,128]{2,1,0:T(8,128)S(1)}, f32[2,8,128]{2,1,0:T(8,128)S(1)}) custom-call(s32[64]{0:T(128)S(1)} %get-tuple-element.20.size_of, f32[512,8,128]{2,1,0:T(8,128)S(1)} %bitcast.6, f32[512,8,128]{2,1,0:T(8,128)S(1)} %collective-permute-done.other.start_other, ...), custom_call_target="tpu_custom_call", output_to_operand_aliasing={{0}: (1, {}), {1}: (2, {})} | custom-call | flops 1073741824 | bytes 1048576 | tf_op jit(solution)/shard_map/pallas_call | solution.py:310
  124.2 0.4 collective-permute-done.1.other
  124.6 0.0 copy-done.2
  124.6 0.0 copy-done.3
  124.6 3.3 %shard_map.89 = (f32[16,2,8,128]{3,2,1,0:T(8,128)S(1)}, f32[2,8,128]{2,1,0:T(8,128)}) custom-call(s32[2,16]{1,0:T(2,128)S(1)} %get-tuple-element.16.base, f32[512,8,128]{2,1,0:T(8,128)S(1)} %get-tuple-element.22.start_mine, f32[512,8,128]{2,1,0:T(8,128)S(1)} %get-tuple-element.23.start_other, f32[512,8,128]{2,1,0:T(8,128)S(1)} %bitcast.9, ...), custom_call_target="tpu_custom_call" | custom-call | flops 1073741824 | bytes 1048576 | tf_op jit(solution)/shard_map/pallas_call | solution.py:318
  127.9 8.8 %all_to_all.35.parts = f32[16,2,8,128]{3,2,1,0:T(8,128)S(1)} all-to-all(f32[16,2,8,128]{3,2,1,0:T(8,128)S(1)} %get-tuple-element.26), channel_id=1, replica_groups={{0,32,64,96,128,160,192,224,256,288,320,352,384,416,448,480},{1,33,65,9..., dimensions={0} | all-to-all | bytes 262144 | tf_op jit(solution)/shard_map/all_to_all | solution.py:49
  136.7 0.6 shard_map.90
  (1 shorter events, 0.0 us)
Async XLA Ops:
  34.9 24.3 %copy-start.6 = (s32[64]{0:T(128)S(1)}, s32[64]{0:T(128)}, u32[]{:S(2)}) copy-start(s32[64]{0:T(128)} %sizes_hbm.1) | copy-start | bytes 772
  35.1 24.2 %copy-start = (f32[16,2,128,128]{3,2,1,0:T(8,128)S(1)}, f32[16,2,128,128]{3,2,1,0:T(8,128)}, u32[]{:S(2)}) copy-start(f32[16,2,128,128]{3,2,1,0:T(8,128)} %left.1) | copy-start | bytes 6291460
  35.1 24.2 %copy-start.1 = (f32[16,2,128,128]{3,2,1,0:T(8,128)S(1)}, f32[16,2,128,128]{3,2,1,0:T(8,128)}, u32[]{:S(2)}) copy-start(f32[16,2,128,128]{3,2,1,0:T(8,128)} %right.1) | copy-start | bytes 6291460
  35.1 24.2 %copy-start.4 = (s32[2,16]{1,0:T(2,128)S(1)}, s32[2,16]{1,0:T(2,128)}, u32[]{:S(2)}) copy-start(s32[2,16]{1,0:T(2,128)} %coupling_hbm.1) | copy-start | bytes 388
  35.1 24.2 %copy-start.5 = (s32[64]{0:T(128)S(1)}, s32[64]{0:T(128)}, u32[]{:S(2)}) copy-start(s32[64]{0:T(128)} %assign_hbm.1) | copy-start | bytes 772
  57.1 6.0 %collective-permute-start = (f32[512,8,128]{2,1,0:T(8,128)S(1)}, f32[512,8,128]{2,1,0:T(8,128)S(1)}, u32[]{:S(2)}, u32[]{:S(2)}) collective-permute-start(f32[512,8,128]{2,1,0:T(8,128)S(1)} %bitcast.4), channel_id=1, source_target_pairs={{0,32},{1,33},{2,34},{3,35},{4,36},{5,37},{6,38},{7,39},{8,40},{9,... | collective-permute-start | bytes 6291464 | tf_op jit(solution)/shard_map/ppermute | solution.py:270
  118.6 6.0 %collective-permute-start.1 = (f32[512,8,128]{2,1,0:T(8,128)S(1)}, f32[512,8,128]{2,1,0:T(8,128)S(1)}, u32[]{:S(2)}, u32[]{:S(2)}) collective-permute-start(f32[512,8,128]{2,1,0:T(8,128)S(1)} %bitcast.7), channel_id=1, source_target_pairs={{0,32},{1,33},{2,34},{3,35},{4,36},{5,37},{6,38},{7,39},{8,40},{9,... | collective-permute-start | bytes 6291464 | tf_op jit(solution)/shard_map/ppermute | solution.py:270
  120.5 4.1 %copy-start.2 = (f32[2,8,128]{2,1,0:T(8,128)S(1)}, f32[2,8,128]{2,1,0:T(8,128)}, u32[]{:S(2)}) copy-start(f32[2,8,128]{2,1,0:T(8,128)} %psi.1) | copy-start | bytes 24580
  120.5 4.1 %copy-start.3 = (f32[2,8,128]{2,1,0:T(8,128)S(1)}, f32[2,8,128]{2,1,0:T(8,128)}, u32[]{:S(2)}) copy-start(f32[2,8,128]{2,1,0:T(8,128)} %get-tuple-element.12.sigma) | copy-start | bytes 24580

commit v3 on v2

--- a/solution.py
+++ b/solution.py
@@ -54,14 +54,13 @@
 HBM = pl.BlockSpec(memory_space=pltpu.HBM)
 
 
-def call(body, outs, out_specs, in_specs, scratch=(), flops=0, moved=1 << 20, aliases=None):
+def call(body, outs, out_specs, in_specs, scratch=(), flops=0, moved=1 << 20):
     return pl.pallas_call(
         body,
         out_shape=outs,
         in_specs=in_specs,
         out_specs=out_specs,
         scratch_shapes=list(scratch),
-        input_output_aliases=aliases or {},
         compiler_params=pltpu.CompilerParams(vmem_limit_bytes=40 << 20),
         cost_estimate=pl.CostEstimate(flops=flops, bytes_accessed=moved, transcendentals=0),
     )
@@ -127,13 +126,11 @@
     return lax.dot_general(a, b, (((1,), (0,)), ((), ())), preferred_element_type=F32)
 
 
-def products(block_of, base, lefts, rights, store, beside=None):
+def products(block_of, base, lefts, rights, store):
     results = []
     for t in range(SLOTS):
         total = jnp.zeros((WIDTH, 2 * WIDTH), F32)
         for k in range(LOCAL_TERMS):
-            if beside is not None:
-                beside(t * LOCAL_TERMS + k)
             high, low = halves(block_of(base[t, k]))
             pair = jnp.concatenate([high, low], axis=1)
             inner = matmul(lefts[k, t], jnp.concatenate([pair, pair], axis=0))
@@ -179,88 +176,76 @@
 LANES = 4
 
 
-def scan(step, sums):
+def whole_sum(values):
+    return jnp.sum(jnp.sum(values, axis=1, keepdims=True), axis=0, keepdims=True)
+
+
+def scan(step, count):
     def body(i, sums):
         sums = list(sums)
         for u in range(16):
-            for n, term in enumerate(step(i * 16 + u)):
-                sums[n * LANES + u % LANES] = sums[n * LANES + u % LANES] + term
+            for n, term in enumerate(step(i, u)):
+                at = n * LANES + u % LANES
+                sums[at] = sums[at] + term
         return tuple(sums)
 
     zero = jnp.zeros((ROWS, WIDTH), F32)
-    sums = lax.fori_loop(0, CHUNKS // 16, body, (zero,) * (sums * LANES))
-    return [sum(sums[n : n + LANES]) for n in range(0, len(sums), LANES)]
-
-
-def moments(size_of, start_mine, start_other, mine, masked_mine, masked_other, sums):
+    sums = lax.fori_loop(0, CHUNKS // 16, body, (zero,) * (count * LANES))
+    return [whole_sum(sum(sums[n : n + LANES])) for n in range(0, len(sums), LANES)]
+
+
+def moments(size_of, start, field, sums, masked):
     core = lax.axis_index("op") % 2
     rows = lax.broadcasted_iota(jnp.int32, (ROWS, WIDTH), 0)
     cols = lax.broadcasted_iota(jnp.int32, (ROWS, WIDTH), 1)
 
-    def body(i, sums):
-        sums = list(sums)
+    def first(i, u):
         xl, yl, zl, yh = i // 16, i // 8 % 2, i // 4 % 2, i % 4
-        for u in range(16):
-            zh, xh, t = u // 4, u // 2 % 2, u % 2
-            size = size_of[(yh * 2 + yl) * 8 + zh * 2 + t]
-            pair = (xh * 4 + xl * 2 + zl) * 2
-            here = i * 16 + u
-            wide = cols < size
-            m = jnp.where(wide & (rows < size - (pair + core) * ROWS), start_mine[here], 0.0)
-            o = jnp.where(wide & (rows < size - (pair + 1 - core) * ROWS), start_other[here], 0.0)
-            masked_mine[here] = m
-            masked_other[here] = o
-            lane = u % LANES
-            sums[lane] = sums[lane] + m * mine[here]
-            sums[LANES + lane] = sums[LANES + lane] + (m * m + o * o)
-        return tuple(sums)
-
-    totals = lax.fori_loop(0, CHUNKS // 16, body, (jnp.zeros((ROWS, WIDTH), F32),) * (2 * LANES))
-    sums[0] = sum(totals[:LANES])
-    sums[1] = sum(totals[LANES:])
-
-
-def whole_sum(values):
-    return jnp.sum(jnp.sum(values, axis=1, keepdims=True), axis=0, keepdims=True)
-
-
-def apply_next(
-    base, start_mine, start_other, mine, other, lefts, rights, psi, masks, sigma, sums, out, next_vector
-):
-    (cross,) = scan(lambda i: (start_other[i] * other[i],), 1)
-    theta = whole_sum(cross + sums[0]) / whole_sum(sums[1])
-    norms = [jnp.zeros((ROWS, WIDTH), F32)] * LANES
-
-    def beside(n):
-        each = CHUNKS // (SLOTS * LOCAL_TERMS)
-        for i in range(n * each, (n + 1) * each):
-            for s, g in ((start_mine, mine), (start_other, other)):
-                r = g[i] - theta * s[i]
-                norms[i % LANES] = norms[i % LANES] + r * r
-
-    def block(first):
-        return gathered_block(mine, other, first) - theta * gathered_block(start_mine, start_other, first)
-
-    scale = []
-
+        zh, xh, t = u // 4, u // 2 % 2, u % 2
+        size = size_of[(yh * 2 + yl) * 8 + zh * 2 + t]
+        row_group = (xh * 4 + xl * 2 + zl) * 2 + core
+        here = i * 16 + u
+        s = jnp.where((cols < size) & (rows < size - row_group * ROWS), start[here], 0.0)
+        masked[here] = s
+        return s * field[here], s * s
+
+    cross, square = scan(first, 2)
+    theta = jnp.where(square > 0.0, cross / jnp.where(square > 0.0, square, 1.0), 0.0)
+
+    def second(i, u):
+        r = field[i * 16 + u] - theta * masked[i * 16 + u]
+        return (r * r,)
+
+    (left,) = scan(second, 1)
+    sums[...] = jnp.where(rows == 0, cross, jnp.where(rows == 1, square, left))
+
+
+def apply_next(base, mine, other, lefts, rights, sums, out):
     def store(i, t, rows):
-        if not scale:
-            scale.append(1.0 / jnp.sqrt(whole_sum(sum(norms)) + 1e-06))
-        out[i, t] = rows * scale[0]
-
-    products(block, base, lefts, rights, store, beside)
-    xh = lax.axis_index("op") // 8
-    for t in range(SLOTS):
-        next_vector[t] = (sigma[t] - theta * (psi[t] * masks[xh, t])) * scale[0]
-
-
-def finish_next(masks, parts, sigma):
-    mine = lax.axis_index("op") // 8
+        out[i, t] = rows
+
+    products(lambda first: gathered_block(mine, other, first), base, lefts, rights, store)
+    for i in range(OPS):
+        out[i, SLOTS] = sums[...]
+
+
+def finish_next(masks, parts, psi, sigma, next_vector, sigma_next):
+    op = lax.axis_index("op")
+    halves_sums = [parts[op - op % 2 + core, SLOTS] for core in range(2)]
+    cross, square, left = zip(*[(h[0:1, 0:1], h[1:2, 0:1], h[2:3, 0:1]) for h in halves_sums])
+    theta = (cross[0] + cross[1]) / (square[0] + square[1])
+    norm = left[0] + left[1]
+    for c, q in zip(cross, square):
+        shift = jnp.where(q > 0.0, c / jnp.where(q > 0.0, q, 1.0), 0.0) - theta
+        norm = norm + shift * q * shift
+    scale = 1.0 / jnp.sqrt(norm + 1e-06)
     for t in range(SLOTS):
         total = parts[0, t]
         for i in range(1, OPS):
             total = total + parts[i, t]
-        sigma[t] = total * masks[mine, t]
+        mask = masks[op // 8, t]
+        sigma_next[t] = (total * mask - theta * sigma[t]) * scale
+        next_vector[t] = (sigma[t] - theta * (psi[t] * mask)) * scale
 
 
 def gather(copies, far):
@@ -306,20 +291,21 @@
         finish_first, (vec, shape(OPS, 2, SLOTS, ROWS, WIDTH)), (VMEM, VMEM), (VMEM, VMEM)
     )(masks, parts)
     mine, other = gather(copies, FAR_YZ)
-    whole = shape(CHUNKS, ROWS, WIDTH)
-    start_mine, start_other, sums = call(
+    sums = call(
         moments,
-        (whole, whole, shape(2, ROWS, WIDTH)),
-        (VMEM,) * 3,
-        (SMEM,) + (VMEM,) * 3,
+        shape(ROWS, WIDTH),
+        VMEM,
+        (SMEM, VMEM, VMEM),
+        scratch=(pltpu.VMEM((CHUNKS, ROWS, WIDTH), F32),),
         flops=flops,
-        aliases={1: 0, 2: 1},
-    )(size_of, start_mine, start_other, mine)
-    parts, next_vector = call(
-        apply_next, (shape(OPS, SLOTS, ROWS, WIDTH), vec), (VMEM, VMEM), (SMEM,) + (VMEM,) * 10, flops=flops
-    )(base, start_mine, start_other, mine, other, lefts, rights, psi, masks, sigma_first, sums)
+    )(size_of, start_mine, mine)
+    parts = call(apply_next, shape(OPS, SLOTS + 1, ROWS, WIDTH), VMEM, (SMEM,) + (VMEM,) * 5, flops=flops)(
+        base, mine, other, lefts, rights, sums
+    )
     parts = exchange(parts, SAME_SEC)
-    sigma_next = call(finish_next, vec, VMEM, (VMEM, VMEM))(masks, parts)
+    next_vector, sigma_next = call(finish_next, (vec, vec), (VMEM, VMEM), (VMEM,) * 4)(
+        masks, parts, psi, sigma_first
+    )
     return sigma_first, next_vector, sigma_next
 
 

time: 138 us -> 137 us (level)
  Pallas kernels: 13.1 us -> 10.9 us
    pallas_call x3, Pallas kernels: 7.55 us -> 5.28 us  [the longest x1 2.61 us: on_device(): call(moments, shape(ROWS, WIDTH), VMEM, (SMEM, VMEM, VMEM), scratch=(pltp...]
  transfers between devices with their start and end apart: 2 -> 2, of which waited for: 2 -> 2; matrix products, arithmetic and copies ran while one was open for 0% -> 0% of each run, Pallas kernels for 5% -> 4%
where the time goes in v3:
time: 137 us
  blocking collectives  117 us (85%)
  Pallas kernels  10.9 us (8%)
  starting transfers between devices  4.02 us (3%)
  waiting for transfers between devices  2.42 us (2%)
    all_to_all x6, blocking collectives, exchange(): return lax.all_to_all(parts, AXES, 0, 0, axis_index_groups=members)  117 us
    ppermute x2, starting transfers between devices, gather(): return (mine, lax.ppermute(mine, AXES, OTHER_CORE))  4.02 us
    pallas_call x1, Pallas kernels, on_device(): call(prepare, (shape(SLOTS, LOCAL_TERMS, dtype=ints), shape(SECTORS, dtyp...  2.95 us
  transfers between devices with their start and end apart: 2, of which 2 were waited for; matrix products, arithmetic and copies ran while one was open for 0% of the time, Pallas kernels for 4%

profile of v3, /device:TPU:1, one launch (start us, length us, event | category | flops | bytes accessed | tf_op | source)
XLA Modules:
  0.0 136.6 jit_solution(191875459843012838)
XLA Ops:
  0.6 0.7 broadcast_in_dim.20
  1.3 33.6 %all_to_all.30 = f32[32,2,8,128]{3,2,1,0:T(8,128)S(1)} all-to-all(f32[32,2,8,128]{3,2,1,0:T(8,128)S(1)} %broadcast_in_dim.20), channel_id=1, replica_groups={{0,256,1,257,2,258,3,259,8,264,9,265,10,266,11,267,16,272,17,273,18,274..., dimensions={0} | all-to-all | bytes 524288 | tf_op jit(solution)/shard_map/all_to_all | solution.py:49
  34.9 0.0 copy-start.6
  34.9 0.1 broadcast_in_dim.22
  35.1 0.0 copy-start
  35.1 0.0 copy-start.1
  35.1 0.0 copy-start.4
  35.1 0.0 copy-start.5
  35.1 22.0 %all_to_all.31 = f32[8,64,8,128]{3,2,1,0:T(8,128)S(1)} all-to-all(f32[8,64,8,128]{3,2,1,0:T(8,128)S(1)} %broadcast_in_dim.22), channel_id=1, replica_groups={{0,64,4,68,128,192,132,196},{1,65,5,69,129,193,133,197},{2,66,6,70,130,..., dimensions={0} | all-to-all | bytes 4194304 | tf_op jit(solution)/shard_map/all_to_all | solution.py:49
  57.1 2.1 %collective-permute-start = (f32[512,8,128]{2,1,0:T(8,128)S(1)}, f32[512,8,128]{2,1,0:T(8,128)S(1)}, u32[]{:S(2)}, u32[]{:S(2)}) collective-permute-start(f32[512,8,128]{2,1,0:T(8,128)S(1)} %bitcast.4), channel_id=1, source_target_pairs={{0,32},{1,33},{2,34},{3,35},{4,36},{5,37},{6,38},{7,39},{8,40},{9,... | collective-permute-start | bytes 6291464 | tf_op jit(solution)/shard_map/ppermute | solution.py:255
  59.2 0.0 copy-done.6
  59.3 0.0 copy-done
  59.3 0.0 copy-done.1
  59.3 0.0 copy-done.4
  59.3 0.0 copy-done.5
  59.3 3.0 %shard_map.85 = (s32[2,16]{1,0:T(2,128)S(1)}, s32[64]{0:T(128)S(1)}, f32[2,2,8,128]{3,2,1,0:T(8,128)S(1)}, bf16[16,2,128,256]{3,2,1,0:T(8,128)(2,1)S(1)}, bf16[16,2,128,256]{3,2,1,0:T(8,128)(2,1)S(1)}) custom-call(s32[2,16]{1,0:T(2,128)S(1)} %copy-done.4, s32[64]{0:T(128)S(1)} %copy-done.5, s32[64]{0:T(128)S(1)} %copy-done.6, ...), custom_call_target="tpu_custom_call" | custom-call | flops 1073741824 | bytes 8388608 | tf_op jit(solution)/shard_map/pallas_call | solution.py:265
  62.3 0.9 collective-permute-done.other
  63.2 2.0 %shard_map.86 = f32[16,2,2,8,128]{4,3,2,1,0:T(8,128)S(1)} custom-call(s32[2,16]{1,0:T(2,128)S(1)} %get-tuple-element.13.base, f32[512,8,128]{2,1,0:T(8,128)S(1)} %bitcast.5, f32[512,8,128]{2,1,0:T(8,128)S(1)} %collective-permute-done.other, bf16[16,2,128,256]{3,2,1,0:T(8,128)(2,1)S(1)} %get-tuple-element.14.lefts, ...), custom_call_target="tpu_custom_call" | custom-call | flops 1073741824 | bytes 1048576 | tf_op jit(solution)/shard_map/pallas_call | solution.py:286
  65.2 10.8 %all_to_all.32.parts = f32[16,2,2,8,128]{4,3,2,1,0:T(8,128)S(1)} all-to-all(f32[16,2,2,8,128]{4,3,2,1,0:T(8,128)S(1)} %shard_map.86), channel_id=1, replica_groups={{0,32,64,96,128,160,192,224,256,288,320,352,384,416,448,480},{1,33,65,9..., dimensions={0} | all-to-all | bytes 524288 | tf_op jit(solution)/shard_map/all_to_all | solution.py:49
  76.0 0.6 shard_map.87
  76.6 18.9 %all_to_all.33 = f32[16,2,2,8,128]{4,3,2,1,0:T(8,128)S(1)} all-to-all(f32[16,2,2,8,128]{4,3,2,1,0:T(8,128)S(1)} %get-tuple-element.17), channel_id=1, replica_groups={{0,1,2,3,8,9,10,11,16,17,18,19,24,25,26,27},{4,5,6,7,12,13,14,15,20,21,..., dimensions={0} | all-to-all | bytes 524288 | tf_op jit(solution)/shard_map/all_to_all | solution.py:49
  95.5 0.1 broadcast_in_dim.24
  95.7 22.9 %all_to_all.34 = f32[8,64,8,128]{3,2,1,0:T(8,128)S(1)} all-to-all(f32[8,64,8,128]{3,2,1,0:T(8,128)S(1)} %broadcast_in_dim.24), channel_id=1, replica_groups={{0,64,4,68,128,192,132,196},{1,65,5,69,129,193,133,197},{2,66,6,70,130,..., dimensions={0} | all-to-all | bytes 4194304 | tf_op jit(solution)/shard_map/all_to_all | solution.py:49
  118.6 1.9 %collective-permute-start.1 = (f32[512,8,128]{2,1,0:T(8,128)S(1)}, f32[512,8,128]{2,1,0:T(8,128)S(1)}, u32[]{:S(2)}, u32[]{:S(2)}) collective-permute-start(f32[512,8,128]{2,1,0:T(8,128)S(1)} %bitcast.7), channel_id=1, source_target_pairs={{0,32},{1,33},{2,34},{3,35},{4,36},{5,37},{6,38},{7,39},{8,40},{9,... | collective-permute-start | bytes 6291464 | tf_op jit(solution)/shard_map/ppermute | solution.py:255
  120.5 2.6 %shard_map.88.sums = f32[8,128]{1,0:T(8,128)S(1)} custom-call(s32[64]{0:T(128)S(1)} %get-tuple-element.18.size_of, f32[512,8,128]{2,1,0:T(8,128)S(1)} %bitcast.6, f32[512,8,128]{2,1,0:T(8,128)S(1)} %bitcast.8), custom_call_target="tpu_custom_call" | custom-call | flops 1073741824 | bytes 1048576 | tf_op jit(solution)/shard_map/pallas_call | solution.py:294
  123.1 0.0 copy-start.2
  123.1 1.5 %collective-permute-done.1.other = f32[512,8,128]{2,1,0:T(8,128)S(1)} collective-permute-done((f32[512,8,128]{2,1,0:T(8,128)S(1)}, f32[512,8,128]{2,1,0:T(8,128)S(1)}, u32[]{:S(2)}, u32[]{:S(2)}) %collective-permute-start.1) | collective-permute-done | bytes 2097184 | tf_op jit(solution)/shard_map/ppermute | solution.py:255
  124.6 2.0 %shard_map.89 = f32[16,3,8,128]{3,2,1,0:T(8,128)S(1)} custom-call(s32[2,16]{1,0:T(2,128)S(1)} %get-tuple-element.13.base, f32[512,8,128]{2,1,0:T(8,128)S(1)} %bitcast.9, f32[512,8,128]{2,1,0:T(8,128)S(1)} %collective-permute-done.1.other, bf16[16,2,128,256]{3,2,1,0:T(8,128)(2,1)S(1)} %get-tuple-element.14.lefts, ...), custom_call_target="tpu_custom_call" | custom-call | flops 1073741824 | bytes 1048576 | tf_op jit(solution)/shard_map/pallas_call | solution.py:302
  126.6 9.3 %all_to_all.35.parts = f32[16,3,8,128]{3,2,1,0:T(8,128)S(1)} all-to-all(f32[16,3,8,128]{3,2,1,0:T(8,128)S(1)} %shard_map.89), channel_id=1, replica_groups={{0,32,64,96,128,160,192,224,256,288,320,352,384,416,448,480},{1,33,65,9..., dimensions={0} | all-to-all | bytes 393216 | tf_op jit(solution)/shard_map/all_to_all | solution.py:49
  135.9 0.0 copy-done.2
  135.9 0.0 copy-done.3
  135.9 0.7 shard_map.90
  (1 shorter events, 0.0 us)
Async XLA Ops:
  34.9 24.3 %copy-start.6 = (s32[64]{0:T(128)S(1)}, s32[64]{0:T(128)}, u32[]{:S(2)}) copy-start(s32[64]{0:T(128)} %sizes_hbm.1) | copy-start | bytes 772
  35.1 24.2 %copy-start = (f32[16,2,128,128]{3,2,1,0:T(8,128)S(1)}, f32[16,2,128,128]{3,2,1,0:T(8,128)}, u32[]{:S(2)}) copy-start(f32[16,2,128,128]{3,2,1,0:T(8,128)} %left.1) | copy-start | bytes 6291460
  35.1 24.2 %copy-start.1 = (f32[16,2,128,128]{3,2,1,0:T(8,128)S(1)}, f32[16,2,128,128]{3,2,1,0:T(8,128)}, u32[]{:S(2)}) copy-start(f32[16,2,128,128]{3,2,1,0:T(8,128)} %right.1) | copy-start | bytes 6291460
  35.1 24.2 %copy-start.4 = (s32[2,16]{1,0:T(2,128)S(1)}, s32[2,16]{1,0:T(2,128)}, u32[]{:S(2)}) copy-start(s32[2,16]{1,0:T(2,128)} %coupling_hbm.1) | copy-start | bytes 388
  35.1 24.2 %copy-start.5 = (s32[64]{0:T(128)S(1)}, s32[64]{0:T(128)}, u32[]{:S(2)}) copy-start(s32[64]{0:T(128)} %assign_hbm.1) | copy-start | bytes 772
  57.1 6.0 %collective-permute-start = (f32[512,8,128]{2,1,0:T(8,128)S(1)}, f32[512,8,128]{2,1,0:T(8,128)S(1)}, u32[]{:S(2)}, u32[]{:S(2)}) collective-permute-start(f32[512,8,128]{2,1,0:T(8,128)S(1)} %bitcast.4), channel_id=1, source_target_pairs={{0,32},{1,33},{2,34},{3,35},{4,36},{5,37},{6,38},{7,39},{8,40},{9,... | collective-permute-start | bytes 6291464 | tf_op jit(solution)/shard_map/ppermute | solution.py:255
  118.6 6.0 %collective-permute-start.1 = (f32[512,8,128]{2,1,0:T(8,128)S(1)}, f32[512,8,128]{2,1,0:T(8,128)S(1)}, u32[]{:S(2)}, u32[]{:S(2)}) collective-permute-start(f32[512,8,128]{2,1,0:T(8,128)S(1)} %bitcast.7), channel_id=1, source_target_pairs={{0,32},{1,33},{2,34},{3,35},{4,36},{5,37},{6,38},{7,39},{8,40},{9,... | collective-permute-start | bytes 6291464 | tf_op jit(solution)/shard_map/ppermute | solution.py:255
  123.1 12.8 %copy-start.2 = (f32[2,8,128]{2,1,0:T(8,128)S(1)}, f32[2,8,128]{2,1,0:T(8,128)}, u32[]{:S(2)}) copy-start(f32[2,8,128]{2,1,0:T(8,128)} %psi.1) | copy-start | bytes 24580
  123.1 12.8 %copy-start.3 = (f32[2,8,128]{2,1,0:T(8,128)S(1)}, f32[2,8,128]{2,1,0:T(8,128)}, u32[]{:S(2)}) copy-start(f32[2,8,128]{2,1,0:T(8,128)} %get-tuple-element.9.sigma) | copy-start | bytes 24580

commit v4 on v3

--- a/solution.py
+++ b/solution.py
@@ -90,10 +90,13 @@
 
 
 def prepare(
-    coupling_hbm, assign_hbm, sizes_hbm, left, right, base, size_of, masks, lefts, rights, coupling, assign, sizes, slot_of, done
+    coupling_hbm, assign_hbm, sizes_hbm, left, right, base, bases, size_of, masks, lefts, rights, coupling, assign, sizes, slot_of, done
 ):
     fetch([(coupling_hbm, coupling), (assign_hbm, assign), (sizes_hbm, sizes)], done)
     op = lax.axis_index("op")
+    sub = lax.broadcasted_iota(jnp.int32, (ROWS, WIDTH), 0)
+    lane = lax.broadcasted_iota(jnp.int32, (ROWS, WIDTH), 1)
+    table = jnp.zeros((ROWS, WIDTH), jnp.int32)
     for p in range(SECTORS):
         sector = assign[p]
         slot_of[sector] = p
@@ -102,10 +105,13 @@
         for k in range(LOCAL_TERMS):
             p = slot_of[coupling[t, k]]
             y = p // 8
-            base[t, k] = (y % 2) * 128 + (y // 2) * 16 + p % 8 // 2 * 4 + p % 2
+            first = (y % 2) * 128 + (y // 2) * 16 + p % 8 // 2 * 4 + p % 2
+            base[t, k] = first
+            table = jnp.where((sub == t) & (lane == k), first, table)
         size = size_of[lax.axis_index("sec") * SLOTS + t]
         for xh in range(2):
             masks[xh, t] = inside(size, (xh * 8 + op % 8) * ROWS).astype(F32)
+    bases[...] = table.astype(F32)
     row = lax.broadcasted_iota(jnp.int32, (WIDTH, WIDTH), 0)
     col = lax.broadcasted_iota(jnp.int32, (WIDTH, WIDTH), 1)
     other = (row // 8 % 2 != op % 2).astype(jnp.int32)
@@ -126,12 +132,12 @@
     return lax.dot_general(a, b, (((1,), (0,)), ((), ())), preferred_element_type=F32)
 
 
-def products(block_of, base, lefts, rights, store):
+def products(block_of, lefts, rights, store):
     results = []
     for t in range(SLOTS):
         total = jnp.zeros((WIDTH, 2 * WIDTH), F32)
         for k in range(LOCAL_TERMS):
-            high, low = halves(block_of(base[t, k]))
+            high, low = halves(block_of(t, k))
             pair = jnp.concatenate([high, low], axis=1)
             inner = matmul(lefts[k, t], jnp.concatenate([pair, pair], axis=0))
             high, low = halves(inner[:, :WIDTH] + inner[:, WIDTH:])
@@ -145,32 +151,45 @@
             store(i, t, results[t][i * ROWS : (i + 1) * ROWS])
 
 
+def own_rows(field, first):
+    return [field[first + step] for step in ROW_STEPS]
+
+
 def gathered_block(mine, other, first):
-    return jnp.concatenate(
-        [mine[first + step] for step in ROW_STEPS] + [other[first + step] for step in ROW_STEPS], axis=0
-    )
-
-
-def apply_first(base, mine, other, lefts, rights, out):
+    return jnp.concatenate(own_rows(mine, first) + own_rows(other, first), axis=0)
+
+
+def apply_first(base, bases, mine, other, lefts, rights, out):
     def store(i, t, rows):
         for x in range(2):
-            out[x * 8 + i % 8, i // 8, t] = rows
-
-    products(lambda first: gathered_block(mine, other, first), base, lefts, rights, store)
-
-
-def finish_first(masks, parts, sigma, copies):
-    mine = lax.axis_index("op") // 8
+            out[x * 8 + i % 8, i // 8 * SLOTS + t] = rows
+
+    products(lambda t, k: gathered_block(mine, other, base[t, k]), lefts, rights, store)
+    for i in range(OPS):
+        out[i, 2 * SLOTS] = bases[...]
+
+
+def finish_first(masks, parts, sigma, copies, other_base):
+    op = lax.axis_index("op")
     for xh in range(2):
         for t in range(SLOTS):
-            total = parts[0, xh, t]
+            total = parts[0, xh * SLOTS + t]
             for i in range(1, OPS):
-                total = total + parts[i, xh, t]
+                total = total + parts[i, xh * SLOTS + t]
             total = total * masks[xh, t]
             for i in range(OPS):
                 copies[i, xh, t] = total
     for t in range(SLOTS):
-        sigma[t] = copies[0, mine, t]
+        sigma[t] = copies[0, op // 8, t]
+    other_base[...] = parts[op + 1 - 2 * (op % 2), 2 * SLOTS].astype(jnp.int32)
+
+
+def pack(other_base, mine, packed):
+    for t in range(SLOTS):
+        for k in range(LOCAL_TERMS):
+            first = other_base[t, k]
+            for n, step in enumerate(ROW_STEPS):
+                packed[t, k, n] = mine[first + step]
 
 
 LANES = 4
@@ -181,69 +200,78 @@
 
 
 def scan(step, count):
+    op = lax.axis_index("op")
+    start = op // 4 % 2 * 256 + op // 2 % 2 * 64
+
     def body(i, sums):
         sums = list(sums)
-        for u in range(16):
-            for n, term in enumerate(step(i, u)):
-                at = n * LANES + u % LANES
-                sums[at] = sums[at] + term
+        for yl in range(2):
+            for u in range(16):
+                for n, term in enumerate(step(yl, i, u, start + yl * 128 + i * 16 + u)):
+                    at = n * LANES + u % LANES
+                    sums[at] = sums[at] + term
         return tuple(sums)
 
     zero = jnp.zeros((ROWS, WIDTH), F32)
-    sums = lax.fori_loop(0, CHUNKS // 16, body, (zero,) * (count * LANES))
+    sums = lax.fori_loop(0, 4, body, (zero,) * (count * LANES))
     return [whole_sum(sum(sums[n : n + LANES])) for n in range(0, len(sums), LANES)]
 
 
+def projection(cross, square):
+    some = square > 0.0
+    return jnp.where(some, cross / jnp.where(some, square, 1.0), 0.0)
+
+
 def moments(size_of, start, field, sums, masked):
-    core = lax.axis_index("op") % 2
+    op = lax.axis_index("op")
     rows = lax.broadcasted_iota(jnp.int32, (ROWS, WIDTH), 0)
     cols = lax.broadcasted_iota(jnp.int32, (ROWS, WIDTH), 1)
 
-    def first(i, u):
-        xl, yl, zl, yh = i // 16, i // 8 % 2, i // 4 % 2, i % 4
+    def first(yl, yh, u, here):
         zh, xh, t = u // 4, u // 2 % 2, u % 2
         size = size_of[(yh * 2 + yl) * 8 + zh * 2 + t]
-        row_group = (xh * 4 + xl * 2 + zl) * 2 + core
-        here = i * 16 + u
-        s = jnp.where((cols < size) & (rows < size - row_group * ROWS), start[here], 0.0)
-        masked[here] = s
+        s = jnp.where((cols < size) & (rows < size - (xh * 8 + op % 8) * ROWS), start[here], 0.0)
+        masked[yl * 64 + yh * 16 + u] = s
         return s * field[here], s * s
 
     cross, square = scan(first, 2)
-    theta = jnp.where(square > 0.0, cross / jnp.where(square > 0.0, square, 1.0), 0.0)
-
-    def second(i, u):
-        r = field[i * 16 + u] - theta * masked[i * 16 + u]
+    theta = projection(cross, square)
+
+    def second(yl, yh, u, here):
+        r = field[here] - theta * masked[yl * 64 + yh * 16 + u]
         return (r * r,)
 
     (left,) = scan(second, 1)
     sums[...] = jnp.where(rows == 0, cross, jnp.where(rows == 1, square, left))
 
 
-def apply_next(base, mine, other, lefts, rights, sums, out):
+def apply_next(base, mine, packed, lefts, rights, sums, out):
+    def block(t, k):
+        other = [packed[t, k, n] for n in range(len(ROW_STEPS))]
+        return jnp.concatenate(own_rows(mine, base[t, k]) + other, axis=0)
+
     def store(i, t, rows):
         out[i, t] = rows
 
-    products(lambda first: gathered_block(mine, other, first), base, lefts, rights, store)
+    products(block, lefts, rights, store)
     for i in range(OPS):
         out[i, SLOTS] = sums[...]
 
 
 def finish_next(masks, parts, psi, sigma, next_vector, sigma_next):
-    op = lax.axis_index("op")
-    halves_sums = [parts[op - op % 2 + core, SLOTS] for core in range(2)]
-    cross, square, left = zip(*[(h[0:1, 0:1], h[1:2, 0:1], h[2:3, 0:1]) for h in halves_sums])
-    theta = (cross[0] + cross[1]) / (square[0] + square[1])
-    norm = left[0] + left[1]
-    for c, q in zip(cross, square):
-        shift = jnp.where(q > 0.0, c / jnp.where(q > 0.0, q, 1.0), 0.0) - theta
-        norm = norm + shift * q * shift
+    xh = lax.axis_index("op") // 8
+    cross, square, left = [
+        jnp.concatenate([parts[xh * 8 + i, SLOTS, n : n + 1] for i in range(8)], axis=0) for n in range(3)
+    ]
+    theta = jnp.sum(cross, axis=0, keepdims=True) / jnp.sum(square, axis=0, keepdims=True)
+    shift = projection(cross, square) - theta
+    norm = jnp.sum(left + shift * square * shift, axis=0, keepdims=True)
     scale = 1.0 / jnp.sqrt(norm + 1e-06)
     for t in range(SLOTS):
         total = parts[0, t]
         for i in range(1, OPS):
             total = total + parts[i, t]
-        mask = masks[op // 8, t]
+        mask = masks[xh, t]
         sigma_next[t] = (total * mask - theta * sigma[t]) * scale
         next_vector[t] = (sigma[t] - theta * (psi[t] * mask)) * scale
 
@@ -251,27 +279,29 @@
 def gather(copies, far):
     part = exchange(copies, far).reshape(1, CHUNKS // 8, ROWS, WIDTH)
     part = jnp.broadcast_to(part, (8, CHUNKS // 8, ROWS, WIDTH))
-    mine = exchange(part, NEAR).reshape(CHUNKS, ROWS, WIDTH)
-    return mine, lax.ppermute(mine, AXES, OTHER_CORE)
+    return exchange(part, NEAR).reshape(CHUNKS, ROWS, WIDTH)
 
 
 def on_device(psi, left_env, right_env, coupling, assign, sizes):
     ints = jnp.int32
     vec = shape(SLOTS, ROWS, WIDTH)
+    chunk = shape(ROWS, WIDTH)
     env_shape = shape(LOCAL_TERMS, SLOTS, WIDTH, 2 * WIDTH, dtype=BF16)
     flops = 2 * 2 * 32 * 128 * 256 * 256
 
-    start_mine, start_other = gather(jnp.broadcast_to(psi[None], (SECS,) + psi.shape), FAR)
-    base, size_of, masks, lefts, rights = call(
+    start_mine = gather(jnp.broadcast_to(psi[None], (SECS,) + psi.shape), FAR)
+    start_other = lax.ppermute(start_mine, AXES, OTHER_CORE)
+    base, bases, size_of, masks, lefts, rights = call(
         prepare,
         (
             shape(SLOTS, LOCAL_TERMS, dtype=ints),
+            chunk,
             shape(SECTORS, dtype=ints),
             shape(2, SLOTS, ROWS, WIDTH),
             env_shape,
             env_shape,
         ),
-        (SMEM, SMEM, VMEM, VMEM, VMEM),
+        (SMEM, VMEM, SMEM, VMEM, VMEM, VMEM),
         (HBM,) * 3 + (VMEM,) * 2,
         scratch=(
             pltpu.SMEM((SLOTS, LOCAL_TERMS), ints),
@@ -283,20 +313,27 @@
         flops=flops,
         moved=8 << 20,
     )(coupling, assign, sizes, left_env, right_env)
-    parts = call(apply_first, shape(OPS, 2, SLOTS, ROWS, WIDTH), VMEM, (SMEM,) + (VMEM,) * 4, flops=flops)(
-        base, start_mine, start_other, lefts, rights
+    parts = call(apply_first, shape(OPS, 2 * SLOTS + 1, ROWS, WIDTH), VMEM, (SMEM,) + (VMEM,) * 5, flops=flops)(
+        base, bases, start_mine, start_other, lefts, rights
     )
     parts = exchange(parts, SAME_SEC)
-    sigma_first, copies = call(
-        finish_first, (vec, shape(OPS, 2, SLOTS, ROWS, WIDTH)), (VMEM, VMEM), (VMEM, VMEM)
+    sigma_first, copies, other_base = call(
+        finish_first,
+        (vec, shape(OPS, 2, SLOTS, ROWS, WIDTH), shape(ROWS, WIDTH, dtype=ints)),
+        (VMEM,) * 3,
+        (VMEM, VMEM),
     )(masks, parts)
-    mine, other = gather(copies, FAR_YZ)
+    mine = gather(copies, FAR_YZ)
+    packed = call(pack, shape(SLOTS, LOCAL_TERMS, len(ROW_STEPS), ROWS, WIDTH), VMEM, (SMEM, VMEM))(
+        other_base[:SLOTS, :LOCAL_TERMS], mine
+    )
+    other = lax.ppermute(packed, AXES, OTHER_CORE)
     sums = call(
         moments,
-        shape(ROWS, WIDTH),
+        chunk,
         VMEM,
         (SMEM, VMEM, VMEM),
-        scratch=(pltpu.VMEM((CHUNKS, ROWS, WIDTH), F32),),
+        scratch=(pltpu.VMEM((CHUNKS // 4, ROWS, WIDTH), F32),),
         flops=flops,
     )(size_of, start_mine, mine)
     parts = call(apply_next, shape(OPS, SLOTS + 1, ROWS, WIDTH), VMEM, (SMEM,) + (VMEM,) * 5, flops=flops)(

time: 137 us -> 141 us (1.029)
  blocking collectives: 117 us -> 95.2 us
  waiting for transfers between devices: 2.42 us -> 22.2 us
  starting transfers between devices: 4.02 us -> 9.71 us
    all_to_all x6 -> x5, blocking collectives: 117 us -> 95.2 us  [exchange(): return lax.all_to_all(parts, AXES, 0, 0, axis_index_groups=members)]
    all_to_all x0 -> x1, waiting for transfers between devices: none -> 20 us  [exchange(): return lax.all_to_all(parts, AXES, 0, 0, axis_index_groups=members)]
    all_to_all x0 -> x1, starting transfers between devices: none -> 4.05 us  [exchange(): return lax.all_to_all(parts, AXES, 0, 0, axis_index_groups=members)]
    ppermute x2, starting transfers between devices: 4.02 us -> 5.66 us  [the longest x1 3.55 us: on_device(): other = lax.ppermute(packed, AXES, OTHER_CORE)]
    pallas_call x4 -> x5, Pallas kernels: 8.19 us -> 7.18 us  [the longest x1 2.87 us: on_device(): call(prepare, (shape(SLOTS, LOCAL_TERMS, dtype=ints), chunk, shape(SECTOR...]
  transfers between devices with their start and end apart: 2 -> 3, of which waited for: 2 -> 3; matrix products, arithmetic and copies ran while one was open for 0% -> 0% of each run, Pallas kernels for 4% -> 3%
where the time goes in v4:
time: 141 us; the launch traced here: 140 us
  blocking collectives  95.2 us (68%)
  waiting for transfers between devices  22.2 us (16%)
  Pallas kernels  9.85 us (7%)
  starting transfers between devices  9.71 us (7%)
  local copies, waits for them, and re-layouts  2.41 us (2%)
    all_to_all x5, blocking collectives, exchange(): return lax.all_to_all(parts, AXES, 0, 0, axis_index_groups=members)  95.2 us
    all_to_all x1, waiting for transfers between devices, exchange(): return lax.all_to_all(parts, AXES, 0, 0, axis_index_groups=members)  20 us
    all_to_all x1, starting transfers between devices, exchange(): return lax.all_to_all(parts, AXES, 0, 0, axis_index_groups=members)  4.05 us
    ppermute x1, starting transfers between devices, on_device(): other = lax.ppermute(packed, AXES, OTHER_CORE)  3.55 us
    pallas_call x1, Pallas kernels, on_device(): call(prepare, (shape(SLOTS, LOCAL_TERMS, dtype=ints), chunk, shape(SECTOR...  2.87 us
  transfers between devices with their start and end apart: 3, of which 3 were waited for; matrix products, arithmetic and copies ran while one was open for 0% of the time, Pallas kernels for 3%

profile of v4, /device:TPU:1, one launch (start us, length us, event | category | flops | bytes accessed | tf_op | source)
XLA Modules:
  0.0 140.2 jit_solution(17345470226749668709)
XLA Ops:
  0.6 0.7 broadcast_in_dim.20
  1.3 33.6 %all_to_all.30 = f32[32,2,8,128]{3,2,1,0:T(8,128)S(1)} all-to-all(f32[32,2,8,128]{3,2,1,0:T(8,128)S(1)} %broadcast_in_dim.20), channel_id=1, replica_groups={{0,256,1,257,2,258,3,259,8,264,9,265,10,266,11,267,16,272,17,273,18,274..., dimensions={0} | all-to-all | bytes 524288 | tf_op jit(solution)/shard_map/all_to_all | solution.py:49
  34.9 0.1 broadcast_in_dim.22
  35.1 0.0 copy-start.6
  35.1 0.0 copy-start.7
  35.1 0.0 copy-start.10
  35.1 0.0 copy-start.11
  35.1 22.0 %all_to_all.31 = f32[8,64,8,128]{3,2,1,0:T(8,128)S(1)} all-to-all(f32[8,64,8,128]{3,2,1,0:T(8,128)S(1)} %broadcast_in_dim.22), channel_id=1, replica_groups={{0,64,4,68,128,192,132,196},{1,65,5,69,129,193,133,197},{2,66,6,70,130,..., dimensions={0} | all-to-all | bytes 4194304 | tf_op jit(solution)/shard_map/all_to_all | solution.py:49
  57.1 2.1 %collective-permute-start = (f32[512,8,128]{2,1,0:T(8,128)S(1)}, f32[512,8,128]{2,1,0:T(8,128)S(1)}, u32[]{:S(2)}, u32[]{:S(2)}) collective-permute-start(f32[512,8,128]{2,1,0:T(8,128)S(1)} %bitcast.7), channel_id=1, source_target_pairs={{0,32},{1,33},{2,34},{3,35},{4,36},{5,37},{6,38},{7,39},{8,40},{9,... | collective-permute-start | bytes 6291464 | tf_op jit(solution)/shard_map/ppermute | solution.py:293
  59.2 0.0 copy-done.12
  59.3 0.0 copy-done.6
  59.3 0.0 copy-done.7
  59.3 0.0 copy-done.10
  59.3 0.0 copy-done.11
  59.3 2.9 %shard_map.85 = (s32[2,16]{1,0:T(2,128)S(1)}, f32[8,128]{1,0:T(8,128)S(1)}, s32[64]{0:T(128)S(1)}, f32[2,2,8,128]{3,2,1,0:T(8,128)S(1)}, bf16[16,2,128,256]{3,2,...) custom-call(s32[2,16]{1,0:T(2,128)S(1)} %copy-done.10, s32[64]{0:T(128)S(1)} %copy-done.11, s32[64]{0:T(128)S(1)} %copy-done.12, ...), custom_call_target="tpu_custom_call" | custom-call | flops 1073741824 | bytes 8388608 | tf_op jit(solution)/shard_map/pallas_call | solution.py:294
  62.2 0.0 copy-start.2
  62.2 1.0 collective-permute-done.other
  63.2 2.0 %shard_map.86 = f32[16,5,8,128]{3,2,1,0:T(8,128)S(1)} custom-call(s32[2,16]{1,0:T(2,128)S(1)} %get-tuple-element.15.base, f32[8,128]{1,0:T(8,128)S(1)} %get-tuple-element.16.bases, f32[512,8,128]{2,1,0:T(8,128)S(1)} %bitcast.8, f32[512,8,128]{2,1,0:T(8,128)S(1)} %collective-permute-done.other, bf16[16,2,128,256]{3,2,1,0:T(8,128)(2,1)S(1)} %get-tuple-element.17.lefts, ...), custom_call_target="tpu_custom_call" | custom-call | flops 1073741824 | bytes 1048576 | tf_op jit(solution)/shard_map/pallas_call | solution.py:316
  65.2 11.3 %all_to_all.32.parts = f32[16,5,8,128]{3,2,1,0:T(8,128)S(1)} all-to-all(f32[16,5,8,128]{3,2,1,0:T(8,128)S(1)} %shard_map.86), channel_id=1, replica_groups={{0,32,64,96,128,160,192,224,256,288,320,352,384,416,448,480},{1,33,65,9..., dimensions={0} | all-to-all | bytes 655360 | tf_op jit(solution)/shard_map/all_to_all | solution.py:49
  76.5 0.6 shard_map.87
  77.2 18.8 %all_to_all.33 = f32[16,2,2,8,128]{4,3,2,1,0:T(8,128)S(1)} all-to-all(f32[16,2,2,8,128]{4,3,2,1,0:T(8,128)S(1)} %get-tuple-element.20), channel_id=1, replica_groups={{0,1,2,3,8,9,10,11,16,17,18,19,24,25,26,27},{4,5,6,7,12,13,14,15,20,21,..., dimensions={0} | all-to-all | bytes 524288 | tf_op jit(solution)/shard_map/all_to_all | solution.py:49
  96.0 1.5 %broadcast_in_dim.24 = f32[8,64,8,128]{3,2,1,0:T(8,128)} broadcast(f32[64,8,128]{2,1,0:T(8,128)S(1)} %bitcast.11), dimensions={1,2,3} | broadcast | bytes 2359296 | tf_op jit(solution)/shard_map/broadcast_in_dim | solution.py:281
  97.5 4.1 %all-to-all-start.4 = ((f32[8,64,8,128]{3,2,1,0:T(8,128)}), f32[8,64,8,128]{3,2,1,0:T(8,128)S(1)}, u32[]{:S(2)}, u32[]{:S(2)}) async-start(f32[8,64,8,128]{3,2,1,0:T(8,128)} %broadcast_in_dim.24), calls=%async_computation.4 | async-start | bytes 4194304 | tf_op jit(solution)/shard_map/all_to_all | solution.py:49
  101.5 20.0 %all-to-all-done.4 = f32[8,64,8,128]{3,2,1,0:T(8,128)S(1)} async-done(((f32[8,64,8,128]{3,2,1,0:T(8,128)}), f32[8,64,8,128]{3,2,1,0:T(8,128)S(1)}, u32[]{:S(2)}, u32[]{:S(2)}) %all-to-all-start.4) | async-done | bytes 2097184 | tf_op jit(solution)/shard_map/all_to_all | solution.py:49
  121.6 0.6 shard_map.88
  122.2 3.6 %collective-permute-start.1 = (f32[2,16,8,8,128]{4,3,2,1,0:T(8,128)S(1)}, f32[2,16,8,8,128]{4,3,2,1,0:T(8,128)S(1)}, u32[]{:S(2)}, u32[]{:S(2)}) collective-permute-start(f32[2,16,8,8,128]{4,3,2,1,0:T(8,128)S(1)} %shard_map.88), channel_id=1, source_target_pairs={{0,32},{1,33},{2,34},{3,35},{4,36},{5,37},{6,38},{7,39},{8,40},{9,... | collective-permute-start | bytes 3145736 | tf_op jit(solution)/shard_map/ppermute | solution.py:330
  125.8 1.0 shard_map.89.sums
  126.8 1.2 collective-permute-done.1.packed
  128.0 0.0 copy-done.3
  128.0 2.0 %shard_map.90 = f32[16,3,8,128]{3,2,1,0:T(8,128)S(1)} custom-call(s32[2,16]{1,0:T(2,128)S(1)} %get-tuple-element.15.base, f32[512,8,128]{2,1,0:T(8,128)S(1)} %bitcast.6, f32[2,16,8,8,128]{4,3,2,1,0:T(8,128)S(1)} %collective-permute-done.1.packed, bf16[16,2,128,256]{3,2,1,0:T(8,128)(2,1)S(1)} %copy-done.3, bf16[16,2,128,256]{3,2,1,0:T(8,128)(2,1)S(1)} %copy-done.5, ...), custom_call_target="tpu_custom_call" | custom-call | flops 1073741824 | bytes 1048576 | tf_op jit(solution)/shard_map/pallas_call | solution.py:339
  130.0 9.5 %all_to_all.34.parts = f32[16,3,8,128]{3,2,1,0:T(8,128)S(1)} all-to-all(f32[16,3,8,128]{3,2,1,0:T(8,128)S(1)} %shard_map.90), channel_id=1, replica_groups={{0,32,64,96,128,160,192,224,256,288,320,352,384,416,448,480},{1,33,65,9..., dimensions={0} | all-to-all | bytes 393216 | tf_op jit(solution)/shard_map/all_to_all | solution.py:49
  139.5 0.7 shard_map.91
  (16 shorter events, 0.0 us)
Async XLA Ops:
  34.9 24.3 %copy-start.12 = (s32[64]{0:T(128)S(1)}, s32[64]{0:T(128)}, u32[]{:S(2)}) copy-start(s32[64]{0:T(128)} %sizes_hbm.1) | copy-start | bytes 772
  35.1 24.2 %copy-start.6 = (f32[16,2,128,128]{3,2,1,0:T(8,128)S(1)}, f32[16,2,128,128]{3,2,1,0:T(8,128)}, u32[]{:S(2)}) copy-start(f32[16,2,128,128]{3,2,1,0:T(8,128)} %left.1) | copy-start | bytes 6291460
  35.1 24.2 %copy-start.7 = (f32[16,2,128,128]{3,2,1,0:T(8,128)S(1)}, f32[16,2,128,128]{3,2,1,0:T(8,128)}, u32[]{:S(2)}) copy-start(f32[16,2,128,128]{3,2,1,0:T(8,128)} %right.1) | copy-start | bytes 6291460
  35.1 24.2 %copy-start.10 = (s32[2,16]{1,0:T(2,128)S(1)}, s32[2,16]{1,0:T(2,128)}, u32[]{:S(2)}) copy-start(s32[2,16]{1,0:T(2,128)} %coupling_hbm.1) | copy-start | bytes 388
  35.1 24.2 %copy-start.11 = (s32[64]{0:T(128)S(1)}, s32[64]{0:T(128)}, u32[]{:S(2)}) copy-start(s32[64]{0:T(128)} %assign_hbm.1) | copy-start | bytes 772
  57.1 6.0 %copy-start = (f32[8,64,8,128]{3,2,1,0:T(8,128)}, f32[8,64,8,128]{3,2,1,0:T(8,128)S(1)}, u32[]{:S(2)}) copy-start(f32[8,64,8,128]{3,2,1,0:T(8,128)S(1)} %all_to_all.31) | copy-start | bytes 6291460
  57.1 6.0 %collective-permute-start = (f32[512,8,128]{2,1,0:T(8,128)S(1)}, f32[512,8,128]{2,1,0:T(8,128)S(1)}, u32[]{:S(2)}, u32[]{:S(2)}) collective-permute-start(f32[512,8,128]{2,1,0:T(8,128)S(1)} %bitcast.7), channel_id=1, source_target_pairs={{0,32},{1,33},{2,34},{3,35},{4,36},{5,37},{6,38},{7,39},{8,40},{9,... | collective-permute-start | bytes 6291464 | tf_op jit(solution)/shard_map/ppermute | solution.py:293
  62.2 3.0 %copy-start.2 = (bf16[16,2,128,256]{3,2,1,0:T(8,128)(2,1)}, bf16[16,2,128,256]{3,2,1,0:T(8,128)(2,1)S(1)}, u32[]{:S(2)}) copy-start(bf16[16,2,128,256]{3,2,1,0:T(8,128)(2,1)S(1)} %get-tuple-element.17.lefts) | copy-start | bytes 6291460
  62.2 3.0 %copy-start.4 = (bf16[16,2,128,256]{3,2,1,0:T(8,128)(2,1)}, bf16[16,2,128,256]{3,2,1,0:T(8,128)(2,1)S(1)}, u32[]{:S(2)}) copy-start(bf16[16,2,128,256]{3,2,1,0:T(8,128)(2,1)S(1)} %get-tuple-element.18.rights) | copy-start | bytes 6291460
  97.5 24.1 %all-to-all-start.4 = ((f32[8,64,8,128]{3,2,1,0:T(8,128)}), f32[8,64,8,128]{3,2,1,0:T(8,128)S(1)}, u32[]{:S(2)}, u32[]{:S(2)}) async-start(f32[8,64,8,128]{3,2,1,0:T(8,128)} %broadcast_in_dim.24), calls=%async_computation.4 | async-start | bytes 4194304 | tf_op jit(solution)/shard_map/all_to_all | solution.py:49
  121.6 4.2 %copy-start.1 = (f32[8,64,8,128]{3,2,1,0:T(8,128)S(1)}, f32[8,64,8,128]{3,2,1,0:T(8,128)}, u32[]{:S(2)}) copy-start(f32[8,64,8,128]{3,2,1,0:T(8,128)} %copy-done) | copy-start | bytes 6291460
  122.2 5.8 %collective-permute-start.1 = (f32[2,16,8,8,128]{4,3,2,1,0:T(8,128)S(1)}, f32[2,16,8,8,128]{4,3,2,1,0:T(8,128)S(1)}, u32[]{:S(2)}, u32[]{:S(2)}) collective-permute-start(f32[2,16,8,8,128]{4,3,2,1,0:T(8,128)S(1)} %shard_map.88), channel_id=1, source_target_pairs={{0,32},{1,33},{2,34},{3,35},{4,36},{5,37},{6,38},{7,39},{8,40},{9,... | collective-permute-start | bytes 3145736 | tf_op jit(solution)/shard_map/ppermute | solution.py:330
  125.8 2.3 %copy-start.3 = (bf16[16,2,128,256]{3,2,1,0:T(8,128)(2,1)S(1)}, bf16[16,2,128,256]{3,2,1,0:T(8,128)(2,1)}, u32[]{:S(2)}) copy-start(bf16[16,2,128,256]{3,2,1,0:T(8,128)(2,1)} %copy-done.2) | copy-start | bytes 6291460
  125.8 2.2 %copy-start.5 = (bf16[16,2,128,256]{3,2,1,0:T(8,128)(2,1)S(1)}, bf16[16,2,128,256]{3,2,1,0:T(8,128)(2,1)}, u32[]{:S(2)}) copy-start(bf16[16,2,128,256]{3,2,1,0:T(8,128)(2,1)} %copy-done.4) | copy-start | bytes 6291460
  126.8 12.7 %copy-start.8 = (f32[2,8,128]{2,1,0:T(8,128)S(1)}, f32[2,8,128]{2,1,0:T(8,128)}, u32[]{:S(2)}) copy-start(f32[2,8,128]{2,1,0:T(8,128)} %psi.1) | copy-start | bytes 24580
  126.8 12.7 %copy-start.9 = (f32[2,8,128]{2,1,0:T(8,128)S(1)}, f32[2,8,128]{2,1,0:T(8,128)}, u32[]{:S(2)}) copy-start(f32[2,8,128]{2,1,0:T(8,128)} %get-tuple-element.11.sigma) | copy-start | bytes 24580

commit v5 on v4

--- a/solution.py
+++ b/solution.py
@@ -325,7 +325,7 @@
     )(masks, parts)
     mine = gather(copies, FAR_YZ)
     packed = call(pack, shape(SLOTS, LOCAL_TERMS, len(ROW_STEPS), ROWS, WIDTH), VMEM, (SMEM, VMEM))(
-        other_base[:SLOTS, :LOCAL_TERMS], mine
+        other_base, mine
     )
     other = lax.ppermute(packed, AXES, OTHER_CORE)
     sums = call(

time: 141 us -> 137 us (0.972)
  blocking collectives: 95.2 us -> 118 us
  waiting for transfers between devices: 22.2 us -> 2.51 us
  starting transfers between devices: 9.71 us -> 4.03 us
    all_to_all x5 -> x6, blocking collectives: 95.2 us -> 118 us  [exchange(): return lax.all_to_all(parts, AXES, 0, 0, axis_index_groups=members)]
    all_to_all x1 -> x0, waiting for transfers between devices: 20 us -> none  [exchange(): return lax.all_to_all(parts, AXES, 0, 0, axis_index_groups=members)]
    all_to_all x1 -> x0, starting transfers between devices: 4.05 us -> none  [exchange(): return lax.all_to_all(parts, AXES, 0, 0, axis_index_groups=members)]
    ppermute x1, starting transfers between devices: 3.55 us -> 1.92 us  [on_device(): other = lax.ppermute(packed, AXES, OTHER_CORE)]
  transfers between devices with their start and end apart: 3 -> 2, of which waited for: 3 -> 2; matrix products, arithmetic and copies ran while one was open for 0% -> 0% of each run, Pallas kernels for 3% -> 3%
where the time goes in v5:
time: 137 us; the launch traced here: 136 us
  blocking collectives  118 us (86%)
  Pallas kernels  9.92 us (7%)
  starting transfers between devices  4.03 us (3%)
  waiting for transfers between devices  2.51 us (2%)
    all_to_all x6, blocking collectives, exchange(): return lax.all_to_all(parts, AXES, 0, 0, axis_index_groups=members)  118 us
    pallas_call x1, Pallas kernels, on_device(): call(prepare, (shape(SLOTS, LOCAL_TERMS, dtype=ints), chunk, shape(SECTOR...  2.92 us
  transfers between devices with their start and end apart: 2, of which 2 were waited for; matrix products, arithmetic and copies ran while one was open for 0% of the time, Pallas kernels for 3%

profile of v5, /device:TPU:1, one launch (start us, length us, event | category | flops | bytes accessed | tf_op | source)
XLA Modules:
  0.0 136.4 jit_solution(1856830131541907440)
XLA Ops:
  0.6 0.7 broadcast_in_dim.20
  1.3 33.6 %all_to_all.30 = f32[32,2,8,128]{3,2,1,0:T(8,128)S(1)} all-to-all(f32[32,2,8,128]{3,2,1,0:T(8,128)S(1)} %broadcast_in_dim.20), channel_id=1, replica_groups={{0,256,1,257,2,258,3,259,8,264,9,265,10,266,11,267,16,272,17,273,18,274..., dimensions={0} | all-to-all | bytes 524288 | tf_op jit(solution)/shard_map/all_to_all | solution.py:49
  34.9 0.0 copy-start.6
  34.9 0.1 broadcast_in_dim.22
  35.1 0.0 copy-start
  35.1 0.0 copy-start.1
  35.1 0.0 copy-start.4
  35.1 0.0 copy-start.5
  35.1 22.0 %all_to_all.31 = f32[8,64,8,128]{3,2,1,0:T(8,128)S(1)} all-to-all(f32[8,64,8,128]{3,2,1,0:T(8,128)S(1)} %broadcast_in_dim.22), channel_id=1, replica_groups={{0,64,4,68,128,192,132,196},{1,65,5,69,129,193,133,197},{2,66,6,70,130,..., dimensions={0} | all-to-all | bytes 4194304 | tf_op jit(solution)/shard_map/all_to_all | solution.py:49
  57.1 2.1 %collective-permute-start = (f32[512,8,128]{2,1,0:T(8,128)S(1)}, f32[512,8,128]{2,1,0:T(8,128)S(1)}, u32[]{:S(2)}, u32[]{:S(2)}) collective-permute-start(f32[512,8,128]{2,1,0:T(8,128)S(1)} %bitcast.7), channel_id=1, source_target_pairs={{0,32},{1,33},{2,34},{3,35},{4,36},{5,37},{6,38},{7,39},{8,40},{9,... | collective-permute-start | bytes 6291464 | tf_op jit(solution)/shard_map/ppermute | solution.py:293
  59.2 0.0 copy-done.6
  59.3 0.0 copy-done
  59.3 0.0 copy-done.1
  59.3 0.0 copy-done.4
  59.3 0.0 copy-done.5
  59.3 2.9 %shard_map.85 = (s32[2,16]{1,0:T(2,128)S(1)}, f32[8,128]{1,0:T(8,128)S(1)}, s32[64]{0:T(128)S(1)}, f32[2,2,8,128]{3,2,1,0:T(8,128)S(1)}, bf16[16,2,128,256]{3,2,...) custom-call(s32[2,16]{1,0:T(2,128)S(1)} %copy-done.4, s32[64]{0:T(128)S(1)} %copy-done.5, s32[64]{0:T(128)S(1)} %copy-done.6, ...), custom_call_target="tpu_custom_call" | custom-call | flops 1073741824 | bytes 8388608 | tf_op jit(solution)/shard_map/pallas_call | solution.py:294
  62.2 1.0 collective-permute-done.other
  63.2 2.0 %shard_map.86 = f32[16,5,8,128]{3,2,1,0:T(8,128)S(1)} custom-call(s32[2,16]{1,0:T(2,128)S(1)} %get-tuple-element.15.base, f32[8,128]{1,0:T(8,128)S(1)} %get-tuple-element.16.bases, f32[512,8,128]{2,1,0:T(8,128)S(1)} %bitcast.8, f32[512,8,128]{2,1,0:T(8,128)S(1)} %collective-permute-done.other, bf16[16,2,128,256]{3,2,1,0:T(8,128)(2,1)S(1)} %get-tuple-element.17.lefts, ...), custom_call_target="tpu_custom_call" | custom-call | flops 1073741824 | bytes 1048576 | tf_op jit(solution)/shard_map/pallas_call | solution.py:316
  65.2 11.3 %all_to_all.32.parts = f32[16,5,8,128]{3,2,1,0:T(8,128)S(1)} all-to-all(f32[16,5,8,128]{3,2,1,0:T(8,128)S(1)} %shard_map.86), channel_id=1, replica_groups={{0,32,64,96,128,160,192,224,256,288,320,352,384,416,448,480},{1,33,65,9..., dimensions={0} | all-to-all | bytes 655360 | tf_op jit(solution)/shard_map/all_to_all | solution.py:49
  76.5 0.6 shard_map.87
  77.2 18.8 %all_to_all.33 = f32[16,2,2,8,128]{4,3,2,1,0:T(8,128)S(1)} all-to-all(f32[16,2,2,8,128]{4,3,2,1,0:T(8,128)S(1)} %get-tuple-element.20), channel_id=1, replica_groups={{0,1,2,3,8,9,10,11,16,17,18,19,24,25,26,27},{4,5,6,7,12,13,14,15,20,21,..., dimensions={0} | all-to-all | bytes 524288 | tf_op jit(solution)/shard_map/all_to_all | solution.py:49
  95.9 0.1 broadcast_in_dim.24
  96.1 23.1 %all_to_all.34 = f32[8,64,8,128]{3,2,1,0:T(8,128)S(1)} all-to-all(f32[8,64,8,128]{3,2,1,0:T(8,128)S(1)} %broadcast_in_dim.24), channel_id=1, replica_groups={{0,64,4,68,128,192,132,196},{1,65,5,69,129,193,133,197},{2,66,6,70,130,..., dimensions={0} | all-to-all | bytes 4194304 | tf_op jit(solution)/shard_map/all_to_all | solution.py:49
  119.2 0.7 shard_map.88
  119.9 1.9 %collective-permute-start.1 = (f32[2,16,8,8,128]{4,3,2,1,0:T(8,128)S(1)}, f32[2,16,8,8,128]{4,3,2,1,0:T(8,128)S(1)}, u32[]{:S(2)}, u32[]{:S(2)}) collective-permute-start(f32[2,16,8,8,128]{4,3,2,1,0:T(8,128)S(1)} %shard_map.88), channel_id=1, source_target_pairs={{0,32},{1,33},{2,34},{3,35},{4,36},{5,37},{6,38},{7,39},{8,40},{9,... | collective-permute-start | bytes 3145736 | tf_op jit(solution)/shard_map/ppermute | solution.py:330
  121.8 1.1 shard_map.89.sums
  122.9 1.6 %collective-permute-done.1.packed = f32[2,16,8,8,128]{4,3,2,1,0:T(8,128)S(1)} collective-permute-done((f32[2,16,8,8,128]{4,3,2,1,0:T(8,128)S(1)}, f32[2,16,8,8,128]{4,3,2,1,0:T(8,128)S(1)}, u32[]{:S(2)}, u32[]{:S(2)}) %collective-permute-start.1) | collective-permute-done | bytes 1048608 | tf_op jit(solution)/shard_map/ppermute | solution.py:330
  124.4 2.0 %shard_map.90 = f32[16,3,8,128]{3,2,1,0:T(8,128)S(1)} custom-call(s32[2,16]{1,0:T(2,128)S(1)} %get-tuple-element.15.base, f32[512,8,128]{2,1,0:T(8,128)S(1)} %bitcast.6, f32[2,16,8,8,128]{4,3,2,1,0:T(8,128)S(1)} %collective-permute-done.1.packed, bf16[16,2,128,256]{3,2,1,0:T(8,128)(2,1)S(1)} %get-tuple-element.17.lefts, ...), custom_call_target="tpu_custom_call" | custom-call | flops 1073741824 | bytes 1048576 | tf_op jit(solution)/shard_map/pallas_call | solution.py:339
  126.4 9.3 %all_to_all.35.parts = f32[16,3,8,128]{3,2,1,0:T(8,128)S(1)} all-to-all(f32[16,3,8,128]{3,2,1,0:T(8,128)S(1)} %shard_map.90), channel_id=1, replica_groups={{0,32,64,96,128,160,192,224,256,288,320,352,384,416,448,480},{1,33,65,9..., dimensions={0} | all-to-all | bytes 393216 | tf_op jit(solution)/shard_map/all_to_all | solution.py:49
  135.7 0.0 copy-done.2
  135.7 0.0 copy-done.3
  135.7 0.7 shard_map.91
  (2 shorter events, 0.0 us)
Async XLA Ops:
  34.9 24.3 %copy-start.6 = (s32[64]{0:T(128)S(1)}, s32[64]{0:T(128)}, u32[]{:S(2)}) copy-start(s32[64]{0:T(128)} %sizes_hbm.1) | copy-start | bytes 772
  35.1 24.2 %copy-start = (f32[16,2,128,128]{3,2,1,0:T(8,128)S(1)}, f32[16,2,128,128]{3,2,1,0:T(8,128)}, u32[]{:S(2)}) copy-start(f32[16,2,128,128]{3,2,1,0:T(8,128)} %left.1) | copy-start | bytes 6291460
  35.1 24.2 %copy-start.1 = (f32[16,2,128,128]{3,2,1,0:T(8,128)S(1)}, f32[16,2,128,128]{3,2,1,0:T(8,128)}, u32[]{:S(2)}) copy-start(f32[16,2,128,128]{3,2,1,0:T(8,128)} %right.1) | copy-start | bytes 6291460
  35.1 24.2 %copy-start.4 = (s32[2,16]{1,0:T(2,128)S(1)}, s32[2,16]{1,0:T(2,128)}, u32[]{:S(2)}) copy-start(s32[2,16]{1,0:T(2,128)} %coupling_hbm.1) | copy-start | bytes 388
  35.1 24.2 %copy-start.5 = (s32[64]{0:T(128)S(1)}, s32[64]{0:T(128)}, u32[]{:S(2)}) copy-start(s32[64]{0:T(128)} %assign_hbm.1) | copy-start | bytes 772
  57.1 6.0 %collective-permute-start = (f32[512,8,128]{2,1,0:T(8,128)S(1)}, f32[512,8,128]{2,1,0:T(8,128)S(1)}, u32[]{:S(2)}, u32[]{:S(2)}) collective-permute-start(f32[512,8,128]{2,1,0:T(8,128)S(1)} %bitcast.7), channel_id=1, source_target_pairs={{0,32},{1,33},{2,34},{3,35},{4,36},{5,37},{6,38},{7,39},{8,40},{9,... | collective-permute-start | bytes 6291464 | tf_op jit(solution)/shard_map/ppermute | solution.py:293
  119.9 4.6 %collective-permute-start.1 = (f32[2,16,8,8,128]{4,3,2,1,0:T(8,128)S(1)}, f32[2,16,8,8,128]{4,3,2,1,0:T(8,128)S(1)}, u32[]{:S(2)}, u32[]{:S(2)}) collective-permute-start(f32[2,16,8,8,128]{4,3,2,1,0:T(8,128)S(1)} %shard_map.88), channel_id=1, source_target_pairs={{0,32},{1,33},{2,34},{3,35},{4,36},{5,37},{6,38},{7,39},{8,40},{9,... | collective-permute-start | bytes 3145736 | tf_op jit(solution)/shard_map/ppermute | solution.py:330
  122.9 12.8 %copy-start.2 = (f32[2,8,128]{2,1,0:T(8,128)S(1)}, f32[2,8,128]{2,1,0:T(8,128)}, u32[]{:S(2)}) copy-start(f32[2,8,128]{2,1,0:T(8,128)} %psi.1) | copy-start | bytes 24580
  122.9 12.8 %copy-start.3 = (f32[2,8,128]{2,1,0:T(8,128)S(1)}, f32[2,8,128]{2,1,0:T(8,128)}, u32[]{:S(2)}) copy-start(f32[2,8,128]{2,1,0:T(8,128)} %get-tuple-element.11.sigma) | copy-start | bytes 24580

commit v6 on v5

--- a/solution.py
+++ b/solution.py
@@ -35,14 +35,16 @@
     return (x - core) % 4 // 2, (y - core) % 8 // 2, (z - core) % 8 // 2, core
 
 
+def kind(x, zl, core, y, zh):
+    return (x + 2 * zl) % 4 * 2 + (y + zl) % 2
+
+
 SAME_SEC = groups(lambda x, zl, core, y, zh: (y, zh), lambda x, zl, core, y, zh: (x, zl, core))
-FAR = groups(lambda x, zl, core, y, zh: (x % 2, y % 2, zl, core), lambda x, zl, core, y, zh: (y // 2, zh, x // 2))
-FAR_YZ = groups(lambda x, zl, core, y, zh: (x, y % 2, zl, core), lambda x, zl, core, y, zh: (y // 2, zh))
-NEAR = groups(cube, lambda x, zl, core, y, zh: (x % 2, y % 2, zl))
+FAR = groups(lambda *place: (kind(*place), place[2]), lambda x, zl, core, y, zh: (zh, zl, y // 2))
+NEAR = groups(cube, kind)
 OTHER_CORE = [
     (number(x, zl, core, y, zh), number(x, zl, 1 - core, y, zh)) for x, zl, core, y, zh in PLACES
 ]
-ROW_STEPS = [(x % 2) * 256 + zl * 64 + (x // 2) * 2 for x in range(4) for zl in range(2)]
 
 
 def exchange(parts, members):
@@ -105,12 +107,10 @@
         for k in range(LOCAL_TERMS):
             p = slot_of[coupling[t, k]]
             y = p // 8
-            first = (y % 2) * 128 + (y // 2) * 16 + p % 8 // 2 * 4 + p % 2
+            first = y % 2 * 64 + p % 8 // 2 * 16 + y // 2 * 2 + p % 2
             base[t, k] = first
             table = jnp.where((sub == t) & (lane == k), first, table)
-        size = size_of[lax.axis_index("sec") * SLOTS + t]
-        for xh in range(2):
-            masks[xh, t] = inside(size, (xh * 8 + op % 8) * ROWS).astype(F32)
+        masks[t] = inside(size_of[lax.axis_index("sec") * SLOTS + t], op * ROWS).astype(F32)
     bases[...] = table.astype(F32)
     row = lax.broadcasted_iota(jnp.int32, (WIDTH, WIDTH), 0)
     col = lax.broadcasted_iota(jnp.int32, (WIDTH, WIDTH), 1)
@@ -152,44 +152,49 @@
 
 
 def own_rows(field, first):
-    return [field[first + step] for step in ROW_STEPS]
+    starts = (first, first ^ 64)
+    return [field[starts[zl] + ((x + 2 * zl) % 4 * 128 + zl * 8)] for x in range(4) for zl in range(2)]
 
 
 def gathered_block(mine, other, first):
     return jnp.concatenate(own_rows(mine, first) + own_rows(other, first), axis=0)
 
 
+def store_in(out):
+    def store(i, t, rows):
+        out[i, t] = rows
+
+    return store
+
+
 def apply_first(base, bases, mine, other, lefts, rights, out):
-    def store(i, t, rows):
-        for x in range(2):
-            out[x * 8 + i % 8, i // 8 * SLOTS + t] = rows
-
-    products(lambda t, k: gathered_block(mine, other, base[t, k]), lefts, rights, store)
+    products(lambda t, k: gathered_block(mine, other, base[t, k]), lefts, rights, store_in(out))
     for i in range(OPS):
-        out[i, 2 * SLOTS] = bases[...]
+        out[i, SLOTS] = bases[...]
+
+
+def reduced(parts, t):
+    total = parts[0, t]
+    for i in range(1, OPS):
+        total = total + parts[i, t]
+    return total
 
 
 def finish_first(masks, parts, sigma, copies, other_base):
     op = lax.axis_index("op")
-    for xh in range(2):
-        for t in range(SLOTS):
-            total = parts[0, xh * SLOTS + t]
-            for i in range(1, OPS):
-                total = total + parts[i, xh * SLOTS + t]
-            total = total * masks[xh, t]
-            for i in range(OPS):
-                copies[i, xh, t] = total
-    for t in range(SLOTS):
-        sigma[t] = copies[0, op // 8, t]
-    other_base[...] = parts[op + 1 - 2 * (op % 2), 2 * SLOTS].astype(jnp.int32)
+    for t in range(SLOTS):
+        total = reduced(parts, t) * masks[t]
+        sigma[t] = total
+        for i in range(SECS):
+            copies[i, t] = total
+    other_base[...] = parts[op + 1 - 2 * (op % 2), SLOTS].astype(jnp.int32)
 
 
 def pack(other_base, mine, packed):
     for t in range(SLOTS):
         for k in range(LOCAL_TERMS):
-            first = other_base[t, k]
-            for n, step in enumerate(ROW_STEPS):
-                packed[t, k, n] = mine[first + step]
+            for n, chunk in enumerate(own_rows(mine, other_base[t, k])):
+                packed[t, k, n] = chunk
 
 
 LANES = 4
@@ -200,20 +205,13 @@
 
 
 def scan(step, count):
-    op = lax.axis_index("op")
-    start = op // 4 % 2 * 256 + op // 2 % 2 * 64
-
-    def body(i, sums):
-        sums = list(sums)
-        for yl in range(2):
-            for u in range(16):
-                for n, term in enumerate(step(yl, i, u, start + yl * 128 + i * 16 + u)):
-                    at = n * LANES + u % LANES
-                    sums[at] = sums[at] + term
-        return tuple(sums)
-
-    zero = jnp.zeros((ROWS, WIDTH), F32)
-    sums = lax.fori_loop(0, 4, body, (zero,) * (count * LANES))
+    x, zl = lax.axis_index("op") // 4, lax.axis_index("op") // 2 % 2
+    start = (x + 2 * zl) % 4 * 128 + zl * 8
+    sums = [jnp.zeros((ROWS, WIDTH), F32)] * (count * LANES)
+    for u, (yl, zh, yh, t) in enumerate(itertools.product(range(2), range(4), range(4), range(2))):
+        for n, term in enumerate(step(u, (yl, zh, yh, t), start + (yl * 64 + zh * 16 + yh * 2 + t))):
+            at = n * LANES + u % LANES
+            sums[at] = sums[at] + term
     return [whole_sum(sum(sums[n : n + LANES])) for n in range(0, len(sums), LANES)]
 
 
@@ -227,18 +225,19 @@
     rows = lax.broadcasted_iota(jnp.int32, (ROWS, WIDTH), 0)
     cols = lax.broadcasted_iota(jnp.int32, (ROWS, WIDTH), 1)
 
-    def first(yl, yh, u, here):
-        zh, xh, t = u // 4, u // 2 % 2, u % 2
-        size = size_of[(yh * 2 + yl) * 8 + zh * 2 + t]
-        s = jnp.where((cols < size) & (rows < size - (xh * 8 + op % 8) * ROWS), start[here], 0.0)
-        masked[yl * 64 + yh * 16 + u] = s
+    def first(u, where, here):
+        yl, zh, yh, t = where
+        y = yh * 2 + (yl + op // 2) % 2
+        size = size_of[y * 8 + zh * 2 + t]
+        s = jnp.where((cols < size) & (rows < size - op * ROWS), start[here], 0.0)
+        masked[u] = s
         return s * field[here], s * s
 
     cross, square = scan(first, 2)
     theta = projection(cross, square)
 
-    def second(yl, yh, u, here):
-        r = field[here] - theta * masked[yl * 64 + yh * 16 + u]
+    def second(u, where, here):
+        r = field[here] - theta * masked[u]
         return (r * r,)
 
     (left,) = scan(second, 1)
@@ -247,37 +246,29 @@
 
 def apply_next(base, mine, packed, lefts, rights, sums, out):
     def block(t, k):
-        other = [packed[t, k, n] for n in range(len(ROW_STEPS))]
+        other = [packed[t, k, n] for n in range(OPS // 2)]
         return jnp.concatenate(own_rows(mine, base[t, k]) + other, axis=0)
 
-    def store(i, t, rows):
-        out[i, t] = rows
-
-    products(block, lefts, rights, store)
+    products(block, lefts, rights, store_in(out))
     for i in range(OPS):
         out[i, SLOTS] = sums[...]
 
 
 def finish_next(masks, parts, psi, sigma, next_vector, sigma_next):
-    xh = lax.axis_index("op") // 8
     cross, square, left = [
-        jnp.concatenate([parts[xh * 8 + i, SLOTS, n : n + 1] for i in range(8)], axis=0) for n in range(3)
+        jnp.concatenate([parts[i, SLOTS, n : n + 1] for i in range(OPS)], axis=0) for n in range(3)
     ]
     theta = jnp.sum(cross, axis=0, keepdims=True) / jnp.sum(square, axis=0, keepdims=True)
     shift = projection(cross, square) - theta
     norm = jnp.sum(left + shift * square * shift, axis=0, keepdims=True)
     scale = 1.0 / jnp.sqrt(norm + 1e-06)
     for t in range(SLOTS):
-        total = parts[0, t]
-        for i in range(1, OPS):
-            total = total + parts[i, t]
-        mask = masks[xh, t]
-        sigma_next[t] = (total * mask - theta * sigma[t]) * scale
-        next_vector[t] = (sigma[t] - theta * (psi[t] * mask)) * scale
-
-
-def gather(copies, far):
-    part = exchange(copies, far).reshape(1, CHUNKS // 8, ROWS, WIDTH)
+        sigma_next[t] = (reduced(parts, t) * masks[t] - theta * sigma[t]) * scale
+        next_vector[t] = (sigma[t] - theta * (psi[t] * masks[t])) * scale
+
+
+def gather(copies):
+    part = exchange(copies, FAR).reshape(1, CHUNKS // 8, ROWS, WIDTH)
     part = jnp.broadcast_to(part, (8, CHUNKS // 8, ROWS, WIDTH))
     return exchange(part, NEAR).reshape(CHUNKS, ROWS, WIDTH)
 
@@ -286,10 +277,11 @@
     ints = jnp.int32
     vec = shape(SLOTS, ROWS, WIDTH)
     chunk = shape(ROWS, WIDTH)
+    parts_shape = shape(OPS, SLOTS + 1, ROWS, WIDTH)
     env_shape = shape(LOCAL_TERMS, SLOTS, WIDTH, 2 * WIDTH, dtype=BF16)
     flops = 2 * 2 * 32 * 128 * 256 * 256
 
-    start_mine = gather(jnp.broadcast_to(psi[None], (SECS,) + psi.shape), FAR)
+    start_mine = gather(jnp.broadcast_to(psi[None], (SECS,) + psi.shape))
     start_other = lax.ppermute(start_mine, AXES, OTHER_CORE)
     base, bases, size_of, masks, lefts, rights = call(
         prepare,
@@ -297,7 +289,7 @@
             shape(SLOTS, LOCAL_TERMS, dtype=ints),
             chunk,
             shape(SECTORS, dtype=ints),
-            shape(2, SLOTS, ROWS, WIDTH),
+            vec,
             env_shape,
             env_shape,
         ),
@@ -313,18 +305,18 @@
         flops=flops,
         moved=8 << 20,
     )(coupling, assign, sizes, left_env, right_env)
-    parts = call(apply_first, shape(OPS, 2 * SLOTS + 1, ROWS, WIDTH), VMEM, (SMEM,) + (VMEM,) * 5, flops=flops)(
+    parts = call(apply_first, parts_shape, VMEM, (SMEM,) + (VMEM,) * 5, flops=flops)(
         base, bases, start_mine, start_other, lefts, rights
     )
     parts = exchange(parts, SAME_SEC)
     sigma_first, copies, other_base = call(
         finish_first,
-        (vec, shape(OPS, 2, SLOTS, ROWS, WIDTH), shape(ROWS, WIDTH, dtype=ints)),
+        (vec, shape(SECS, SLOTS, ROWS, WIDTH), shape(ROWS, WIDTH, dtype=ints)),
         (VMEM,) * 3,
         (VMEM, VMEM),
     )(masks, parts)
-    mine = gather(copies, FAR_YZ)
-    packed = call(pack, shape(SLOTS, LOCAL_TERMS, len(ROW_STEPS), ROWS, WIDTH), VMEM, (SMEM, VMEM))(
+    mine = gather(copies)
+    packed = call(pack, shape(SLOTS, LOCAL_TERMS, OPS // 2, ROWS, WIDTH), VMEM, (SMEM, VMEM))(
         other_base, mine
     )
     other = lax.ppermute(packed, AXES, OTHER_CORE)
@@ -333,10 +325,10 @@
         chunk,
         VMEM,
         (SMEM, VMEM, VMEM),
-        scratch=(pltpu.VMEM((CHUNKS // 4, ROWS, WIDTH), F32),),
+        scratch=(pltpu.VMEM((SECTORS, ROWS, WIDTH), F32),),
         flops=flops,
     )(size_of, start_mine, mine)
-    parts = call(apply_next, shape(OPS, SLOTS + 1, ROWS, WIDTH), VMEM, (SMEM,) + (VMEM,) * 5, flops=flops)(
+    parts = call(apply_next, parts_shape, VMEM, (SMEM,) + (VMEM,) * 5, flops=flops)(
         base, mine, other, lefts, rights, sums
     )
     parts = exchange(parts, SAME_SEC)

time: 137 us -> 136 us (level)
  no operation moved by 1% of the time
where the time goes in v6:
time: 136 us; the launch traced here: 135 us
  blocking collectives  117 us (86%)
  Pallas kernels  9.85 us (7%)
  starting transfers between devices  3.83 us (3%)
  waiting for transfers between devices  2.89 us (2%)
    all_to_all x6, blocking collectives, exchange(): return lax.all_to_all(parts, AXES, 0, 0, axis_index_groups=members)  117 us
    pallas_call x1, Pallas kernels, on_device(): call(prepare, (shape(SLOTS, LOCAL_TERMS, dtype=ints), chunk, shape(SECTOR...  2.93 us
  transfers between devices with their start and end apart: 2, of which 2 were waited for; matrix products, arithmetic and copies ran while one was open for 0% of the time, Pallas kernels for 3%

profile of v6, /device:TPU:1, one launch (start us, length us, event | category | flops | bytes accessed | tf_op | source)
XLA Modules:
  0.0 135.3 jit_solution(10325927841110870028)
XLA Ops:
  0.6 0.7 broadcast_in_dim.20
  1.3 30.8 %all_to_all.30 = f32[32,2,8,128]{3,2,1,0:T(8,128)S(1)} all-to-all(f32[32,2,8,128]{3,2,1,0:T(8,128)S(1)} %broadcast_in_dim.20), channel_id=1, replica_groups={{0,8,16,24,324,332,340,348,1,9,17,25,325,333,341,349,2,10,18,26,326,334..., dimensions={0} | all-to-all | bytes 524288 | tf_op jit(solution)/shard_map/all_to_all | solution.py:51
  32.2 0.0 copy-start.6
  32.2 0.1 broadcast_in_dim.22
  32.3 0.0 copy-start
  32.3 0.0 copy-start.1
  32.3 0.0 copy-start.4
  32.3 0.0 copy-start.5
  32.3 24.4 %all_to_all.31 = f32[8,64,8,128]{3,2,1,0:T(8,128)S(1)} all-to-all(f32[8,64,8,128]{3,2,1,0:T(8,128)S(1)} %broadcast_in_dim.22), channel_id=1, replica_groups={{0,4,128,132,68,64,196,192},{1,5,129,133,69,65,197,193},{2,6,130,134,70..., dimensions={0} | all-to-all | bytes 4194304 | tf_op jit(solution)/shard_map/all_to_all | solution.py:51
  56.7 1.9 %collective-permute-start = (f32[512,8,128]{2,1,0:T(8,128)S(1)}, f32[512,8,128]{2,1,0:T(8,128)S(1)}, u32[]{:S(2)}, u32[]{:S(2)}) collective-permute-start(f32[512,8,128]{2,1,0:T(8,128)S(1)} %bitcast.7), channel_id=1, source_target_pairs={{0,32},{1,33},{2,34},{3,35},{4,36},{5,37},{6,38},{7,39},{8,40},{9,... | collective-permute-start | bytes 6291464 | tf_op jit(solution)/shard_map/ppermute | solution.py:285
  58.6 0.0 copy-done.6
  58.6 0.0 copy-done
  58.6 0.0 copy-done.1
  58.7 0.0 copy-done.4
  58.7 0.0 copy-done.5
  58.7 2.9 %shard_map.85 = (s32[2,16]{1,0:T(2,128)S(1)}, f32[8,128]{1,0:T(8,128)S(1)}, s32[64]{0:T(128)S(1)}, f32[2,8,128]{2,1,0:T(8,128)S(1)}, bf16[16,2,128,256]{3,2,1,0:...) custom-call(s32[2,16]{1,0:T(2,128)S(1)} %copy-done.4, s32[64]{0:T(128)S(1)} %copy-done.5, s32[64]{0:T(128)S(1)} %copy-done.6, ...), custom_call_target="tpu_custom_call" | custom-call | flops 1073741824 | bytes 8388608 | tf_op jit(solution)/shard_map/pallas_call | solution.py:286
  61.6 1.1 collective-permute-done.other
  62.7 2.0 %shard_map.86 = f32[16,3,8,128]{3,2,1,0:T(8,128)S(1)} custom-call(s32[2,16]{1,0:T(2,128)S(1)} %get-tuple-element.15.base, f32[8,128]{1,0:T(8,128)S(1)} %get-tuple-element.16.bases, f32[512,8,128]{2,1,0:T(8,128)S(1)} %bitcast.8, f32[512,8,128]{2,1,0:T(8,128)S(1)} %collective-permute-done.other, bf16[16,2,128,256]{3,2,1,0:T(8,128)(2,1)S(1)} %get-tuple-element.17.lefts, ...), custom_call_target="tpu_custom_call" | custom-call | flops 1073741824 | bytes 1048576 | tf_op jit(solution)/shard_map/pallas_call | solution.py:308
  64.8 9.3 %all_to_all.32.parts = f32[16,3,8,128]{3,2,1,0:T(8,128)S(1)} all-to-all(f32[16,3,8,128]{3,2,1,0:T(8,128)S(1)} %shard_map.86), channel_id=1, replica_groups={{0,32,64,96,128,160,192,224,256,288,320,352,384,416,448,480},{1,33,65,9..., dimensions={0} | all-to-all | bytes 393216 | tf_op jit(solution)/shard_map/all_to_all | solution.py:51
  74.0 0.6 shard_map.87
  74.7 19.7 %all_to_all.33 = f32[32,2,8,128]{3,2,1,0:T(8,128)S(1)} all-to-all(f32[32,2,8,128]{3,2,1,0:T(8,128)S(1)} %get-tuple-element.20), channel_id=1, replica_groups={{0,8,16,24,324,332,340,348,1,9,17,25,325,333,341,349,2,10,18,26,326,334..., dimensions={0} | all-to-all | bytes 524288 | tf_op jit(solution)/shard_map/all_to_all | solution.py:51
  94.4 0.1 broadcast_in_dim.24
  94.5 23.5 %all_to_all.34 = f32[8,64,8,128]{3,2,1,0:T(8,128)S(1)} all-to-all(f32[8,64,8,128]{3,2,1,0:T(8,128)S(1)} %broadcast_in_dim.24), channel_id=1, replica_groups={{0,4,128,132,68,64,196,192},{1,5,129,133,69,65,197,193},{2,6,130,134,70..., dimensions={0} | all-to-all | bytes 4194304 | tf_op jit(solution)/shard_map/all_to_all | solution.py:51
  118.0 0.7 shard_map.88
  118.8 1.9 %collective-permute-start.1 = (f32[2,16,8,8,128]{4,3,2,1,0:T(8,128)S(1)}, f32[2,16,8,8,128]{4,3,2,1,0:T(8,128)S(1)}, u32[]{:S(2)}, u32[]{:S(2)}) collective-permute-start(f32[2,16,8,8,128]{4,3,2,1,0:T(8,128)S(1)} %shard_map.88), channel_id=1, source_target_pairs={{0,32},{1,33},{2,34},{3,35},{4,36},{5,37},{6,38},{7,39},{8,40},{9,... | collective-permute-start | bytes 3145736 | tf_op jit(solution)/shard_map/ppermute | solution.py:322
  120.7 0.9 shard_map.89.sums
  121.6 1.8 %collective-permute-done.1.packed = f32[2,16,8,8,128]{4,3,2,1,0:T(8,128)S(1)} collective-permute-done((f32[2,16,8,8,128]{4,3,2,1,0:T(8,128)S(1)}, f32[2,16,8,8,128]{4,3,2,1,0:T(8,128)S(1)}, u32[]{:S(2)}, u32[]{:S(2)}) %collective-permute-start.1) | collective-permute-done | bytes 1048608 | tf_op jit(solution)/shard_map/ppermute | solution.py:322
  123.3 2.0 %shard_map.90 = f32[16,3,8,128]{3,2,1,0:T(8,128)S(1)} custom-call(s32[2,16]{1,0:T(2,128)S(1)} %get-tuple-element.15.base, f32[512,8,128]{2,1,0:T(8,128)S(1)} %bitcast.6, f32[2,16,8,8,128]{4,3,2,1,0:T(8,128)S(1)} %collective-permute-done.1.packed, bf16[16,2,128,256]{3,2,1,0:T(8,128)(2,1)S(1)} %get-tuple-element.17.lefts, ...), custom_call_target="tpu_custom_call" | custom-call | flops 1073741824 | bytes 1048576 | tf_op jit(solution)/shard_map/pallas_call | solution.py:331
  125.4 9.3 %all_to_all.35.parts = f32[16,3,8,128]{3,2,1,0:T(8,128)S(1)} all-to-all(f32[16,3,8,128]{3,2,1,0:T(8,128)S(1)} %shard_map.90), channel_id=1, replica_groups={{0,32,64,96,128,160,192,224,256,288,320,352,384,416,448,480},{1,33,65,9..., dimensions={0} | all-to-all | bytes 393216 | tf_op jit(solution)/shard_map/all_to_all | solution.py:51
  134.6 0.0 copy-done.2
  134.6 0.0 copy-done.3
  134.6 0.7 shard_map.91
  (2 shorter events, 0.0 us)
Async XLA Ops:
  32.2 26.5 %copy-start.6 = (s32[64]{0:T(128)S(1)}, s32[64]{0:T(128)}, u32[]{:S(2)}) copy-start(s32[64]{0:T(128)} %sizes_hbm.1) | copy-start | bytes 772
  32.3 26.3 %copy-start = (f32[16,2,128,128]{3,2,1,0:T(8,128)S(1)}, f32[16,2,128,128]{3,2,1,0:T(8,128)}, u32[]{:S(2)}) copy-start(f32[16,2,128,128]{3,2,1,0:T(8,128)} %left.1) | copy-start | bytes 6291460
  32.3 26.3 %copy-start.1 = (f32[16,2,128,128]{3,2,1,0:T(8,128)S(1)}, f32[16,2,128,128]{3,2,1,0:T(8,128)}, u32[]{:S(2)}) copy-start(f32[16,2,128,128]{3,2,1,0:T(8,128)} %right.1) | copy-start | bytes 6291460
  32.3 26.3 %copy-start.4 = (s32[2,16]{1,0:T(2,128)S(1)}, s32[2,16]{1,0:T(2,128)}, u32[]{:S(2)}) copy-start(s32[2,16]{1,0:T(2,128)} %coupling_hbm.1) | copy-start | bytes 388
  32.3 26.3 %copy-start.5 = (s32[64]{0:T(128)S(1)}, s32[64]{0:T(128)}, u32[]{:S(2)}) copy-start(s32[64]{0:T(128)} %assign_hbm.1) | copy-start | bytes 772
  56.7 6.0 %collective-permute-start = (f32[512,8,128]{2,1,0:T(8,128)S(1)}, f32[512,8,128]{2,1,0:T(8,128)S(1)}, u32[]{:S(2)}, u32[]{:S(2)}) collective-permute-start(f32[512,8,128]{2,1,0:T(8,128)S(1)} %bitcast.7), channel_id=1, source_target_pairs={{0,32},{1,33},{2,34},{3,35},{4,36},{5,37},{6,38},{7,39},{8,40},{9,... | collective-permute-start | bytes 6291464 | tf_op jit(solution)/shard_map/ppermute | solution.py:285
  118.8 4.6 %collective-permute-start.1 = (f32[2,16,8,8,128]{4,3,2,1,0:T(8,128)S(1)}, f32[2,16,8,8,128]{4,3,2,1,0:T(8,128)S(1)}, u32[]{:S(2)}, u32[]{:S(2)}) collective-permute-start(f32[2,16,8,8,128]{4,3,2,1,0:T(8,128)S(1)} %shard_map.88), channel_id=1, source_target_pairs={{0,32},{1,33},{2,34},{3,35},{4,36},{5,37},{6,38},{7,39},{8,40},{9,... | collective-permute-start | bytes 3145736 | tf_op jit(solution)/shard_map/ppermute | solution.py:322
  121.6 13.0 %copy-start.2 = (f32[2,8,128]{2,1,0:T(8,128)S(1)}, f32[2,8,128]{2,1,0:T(8,128)}, u32[]{:S(2)}) copy-start(f32[2,8,128]{2,1,0:T(8,128)} %psi.1) | copy-start | bytes 24580
  121.6 13.0 %copy-start.3 = (f32[2,8,128]{2,1,0:T(8,128)S(1)}, f32[2,8,128]{2,1,0:T(8,128)}, u32[]{:S(2)}) copy-start(f32[2,8,128]{2,1,0:T(8,128)} %get-tuple-element.11.sigma) | copy-start | bytes 24580

commit v7 on v6

--- a/solution.py
+++ b/solution.py
@@ -32,11 +32,11 @@
 
 def cube(x, zl, core, y, zh):
     z = 2 * zh + zl
-    return (x - core) % 4 // 2, (y - core) % 8 // 2, (z - core) % 8 // 2, core
+    return (x + core - 1) % 4 // 2, (y - core) % 8 // 2, (z - core) % 8 // 2, core
 
 
 def kind(x, zl, core, y, zh):
-    return (x + 2 * zl) % 4 * 2 + (y + zl) % 2
+    return (x + 2 * zl) % 4 * 2 + y % 2
 
 
 SAME_SEC = groups(lambda x, zl, core, y, zh: (y, zh), lambda x, zl, core, y, zh: (x, zl, core))
@@ -152,8 +152,7 @@
 
 
 def own_rows(field, first):
-    starts = (first, first ^ 64)
-    return [field[starts[zl] + ((x + 2 * zl) % 4 * 128 + zl * 8)] for x in range(4) for zl in range(2)]
+    return [field[first + ((x + 2 * zl) % 4 * 128 + zl * 8)] for x in range(4) for zl in range(2)]
 
 
 def gathered_block(mine, other, first):
@@ -227,8 +226,7 @@
 
     def first(u, where, here):
         yl, zh, yh, t = where
-        y = yh * 2 + (yl + op // 2) % 2
-        size = size_of[y * 8 + zh * 2 + t]
+        size = size_of[(yh * 2 + yl) * 8 + zh * 2 + t]
         s = jnp.where((cols < size) & (rows < size - op * ROWS), start[here], 0.0)
         masked[u] = s
         return s * field[here], s * s

time: 136 us -> 136 us (level)
  starting transfers between devices: 3.83 us -> 9.28 us
  blocking collectives: 117 us -> 113 us
    all_to_all x6, blocking collectives: 117 us -> 113 us  [exchange(): return lax.all_to_all(parts, AXES, 0, 0, axis_index_groups=members)]
    ppermute x1, starting transfers between devices: 1.91 us -> 4.95 us  [on_device(): start_other = lax.ppermute(start_mine, AXES, OTHER_CORE)]
    ppermute x1, starting transfers between devices: 1.92 us -> 4.33 us  [on_device(): other = lax.ppermute(packed, AXES, OTHER_CORE)]
where the time goes in v7:
time: 136 us
  blocking collectives  113 us (83%)
  Pallas kernels  9.86 us (7%)
  starting transfers between devices  9.28 us (7%)
  waiting for transfers between devices  2.16 us (2%)
    all_to_all x6, blocking collectives, exchange(): return lax.all_to_all(parts, AXES, 0, 0, axis_index_groups=members)  113 us
    ppermute x1, starting transfers between devices, on_device(): start_other = lax.ppermute(start_mine, AXES, OTHER_CORE)  4.95 us
    ppermute x1, starting transfers between devices, on_device(): other = lax.ppermute(packed, AXES, OTHER_CORE)  4.33 us
    pallas_call x1, Pallas kernels, on_device(): call(prepare, (shape(SLOTS, LOCAL_TERMS, dtype=ints), chunk, shape(SECTOR...  2.93 us
  transfers between devices with their start and end apart: 2, of which 2 were waited for; matrix products, arithmetic and copies ran while one was open for 0% of the time, Pallas kernels for 3%

profile of v7, /device:TPU:1, one launch (start us, length us, event | category | flops | bytes accessed | tf_op | source)
XLA Modules:
  0.0 135.7 jit_solution(13093557696000646920)
XLA Ops:
  0.6 0.7 broadcast_in_dim.20
  1.3 32.7 %all_to_all.30 = f32[32,2,8,128]{3,2,1,0:T(8,128)S(1)} all-to-all(f32[32,2,8,128]{3,2,1,0:T(8,128)S(1)} %broadcast_in_dim.20), channel_id=1, replica_groups={{0,8,16,24,320,328,336,344,1,9,17,25,321,329,337,345,2,10,18,26,322,330..., dimensions={0} | all-to-all | bytes 524288 | tf_op jit(solution)/shard_map/all_to_all | solution.py:51
  34.0 0.0 copy-start.6
  34.0 0.1 broadcast_in_dim.22
  34.2 0.0 copy-start
  34.2 0.0 copy-start.1
  34.2 0.0 copy-start.4
  34.2 0.0 copy-start.5
  34.2 20.8 %all_to_all.31 = f32[8,64,8,128]{3,2,1,0:T(8,128)S(1)} all-to-all(f32[8,64,8,128]{3,2,1,0:T(8,128)S(1)} %broadcast_in_dim.22), channel_id=1, replica_groups={{0,4,448,452,64,68,384,388},{1,5,449,453,65,69,385,389},{2,6,450,454,66..., dimensions={0} | all-to-all | bytes 4194304 | tf_op jit(solution)/shard_map/all_to_all | solution.py:51
  55.0 5.0 %collective-permute-start = (f32[512,8,128]{2,1,0:T(8,128)S(1)}, f32[512,8,128]{2,1,0:T(8,128)S(1)}, u32[]{:S(2)}, u32[]{:S(2)}) collective-permute-start(f32[512,8,128]{2,1,0:T(8,128)S(1)} %bitcast.7), channel_id=1, source_target_pairs={{0,32},{1,33},{2,34},{3,35},{4,36},{5,37},{6,38},{7,39},{8,40},{9,... | collective-permute-start | bytes 6291464 | tf_op jit(solution)/shard_map/ppermute | solution.py:283
  60.0 0.0 copy-done.6
  60.0 0.0 copy-done
  60.0 0.0 copy-done.1
  60.0 0.0 copy-done.4
  60.0 0.0 copy-done.5
  60.0 2.9 %shard_map.85 = (s32[2,16]{1,0:T(2,128)S(1)}, f32[8,128]{1,0:T(8,128)S(1)}, s32[64]{0:T(128)S(1)}, f32[2,8,128]{2,1,0:T(8,128)S(1)}, bf16[16,2,128,256]{3,2,1,0:...) custom-call(s32[2,16]{1,0:T(2,128)S(1)} %copy-done.4, s32[64]{0:T(128)S(1)} %copy-done.5, s32[64]{0:T(128)S(1)} %copy-done.6, ...), custom_call_target="tpu_custom_call" | custom-call | flops 1073741824 | bytes 8388608 | tf_op jit(solution)/shard_map/pallas_call | solution.py:284
  62.9 0.8 collective-permute-done.other
  63.7 2.0 %shard_map.86 = f32[16,3,8,128]{3,2,1,0:T(8,128)S(1)} custom-call(s32[2,16]{1,0:T(2,128)S(1)} %get-tuple-element.15.base, f32[8,128]{1,0:T(8,128)S(1)} %get-tuple-element.16.bases, f32[512,8,128]{2,1,0:T(8,128)S(1)} %bitcast.8, f32[512,8,128]{2,1,0:T(8,128)S(1)} %collective-permute-done.other, bf16[16,2,128,256]{3,2,1,0:T(8,128)(2,1)S(1)} %get-tuple-element.17.lefts, ...), custom_call_target="tpu_custom_call" | custom-call | flops 1073741824 | bytes 1048576 | tf_op jit(solution)/shard_map/pallas_call | solution.py:306
  65.7 9.5 %all_to_all.32.parts = f32[16,3,8,128]{3,2,1,0:T(8,128)S(1)} all-to-all(f32[16,3,8,128]{3,2,1,0:T(8,128)S(1)} %shard_map.86), channel_id=1, replica_groups={{0,32,64,96,128,160,192,224,256,288,320,352,384,416,448,480},{1,33,65,9..., dimensions={0} | all-to-all | bytes 393216 | tf_op jit(solution)/shard_map/all_to_all | solution.py:51
  75.2 0.6 shard_map.87
  75.9 19.2 %all_to_all.33 = f32[32,2,8,128]{3,2,1,0:T(8,128)S(1)} all-to-all(f32[32,2,8,128]{3,2,1,0:T(8,128)S(1)} %get-tuple-element.20), channel_id=1, replica_groups={{0,8,16,24,320,328,336,344,1,9,17,25,321,329,337,345,2,10,18,26,322,330..., dimensions={0} | all-to-all | bytes 524288 | tf_op jit(solution)/shard_map/all_to_all | solution.py:51
  95.0 0.1 broadcast_in_dim.24
  95.2 21.0 %all_to_all.34 = f32[8,64,8,128]{3,2,1,0:T(8,128)S(1)} all-to-all(f32[8,64,8,128]{3,2,1,0:T(8,128)S(1)} %broadcast_in_dim.24), channel_id=1, replica_groups={{0,4,448,452,64,68,384,388},{1,5,449,453,65,69,385,389},{2,6,450,454,66..., dimensions={0} | all-to-all | bytes 4194304 | tf_op jit(solution)/shard_map/all_to_all | solution.py:51
  116.1 0.7 shard_map.88
  116.9 4.3 %collective-permute-start.1 = (f32[2,16,8,8,128]{4,3,2,1,0:T(8,128)S(1)}, f32[2,16,8,8,128]{4,3,2,1,0:T(8,128)S(1)}, u32[]{:S(2)}, u32[]{:S(2)}) collective-permute-start(f32[2,16,8,8,128]{4,3,2,1,0:T(8,128)S(1)} %shard_map.88), channel_id=1, source_target_pairs={{0,32},{1,33},{2,34},{3,35},{4,36},{5,37},{6,38},{7,39},{8,40},{9,... | collective-permute-start | bytes 3145736 | tf_op jit(solution)/shard_map/ppermute | solution.py:320
  121.2 0.9 shard_map.89.sums
  122.1 1.4 %collective-permute-done.1.packed = f32[2,16,8,8,128]{4,3,2,1,0:T(8,128)S(1)} collective-permute-done((f32[2,16,8,8,128]{4,3,2,1,0:T(8,128)S(1)}, f32[2,16,8,8,128]{4,3,2,1,0:T(8,128)S(1)}, u32[]{:S(2)}, u32[]{:S(2)}) %collective-permute-start.1) | collective-permute-done | bytes 1048608 | tf_op jit(solution)/shard_map/ppermute | solution.py:320
  123.5 2.0 %shard_map.90 = f32[16,3,8,128]{3,2,1,0:T(8,128)S(1)} custom-call(s32[2,16]{1,0:T(2,128)S(1)} %get-tuple-element.15.base, f32[512,8,128]{2,1,0:T(8,128)S(1)} %bitcast.6, f32[2,16,8,8,128]{4,3,2,1,0:T(8,128)S(1)} %collective-permute-done.1.packed, bf16[16,2,128,256]{3,2,1,0:T(8,128)(2,1)S(1)} %get-tuple-element.17.lefts, ...), custom_call_target="tpu_custom_call" | custom-call | flops 1073741824 | bytes 1048576 | tf_op jit(solution)/shard_map/pallas_call | solution.py:329
  125.5 9.5 %all_to_all.35.parts = f32[16,3,8,128]{3,2,1,0:T(8,128)S(1)} all-to-all(f32[16,3,8,128]{3,2,1,0:T(8,128)S(1)} %shard_map.90), channel_id=1, replica_groups={{0,32,64,96,128,160,192,224,256,288,320,352,384,416,448,480},{1,33,65,9..., dimensions={0} | all-to-all | bytes 393216 | tf_op jit(solution)/shard_map/all_to_all | solution.py:51
  135.0 0.0 copy-done.2
  135.0 0.0 copy-done.3
  135.0 0.7 shard_map.91
  (2 shorter events, 0.0 us)
Async XLA Ops:
  34.0 25.9 %copy-start.6 = (s32[64]{0:T(128)S(1)}, s32[64]{0:T(128)}, u32[]{:S(2)}) copy-start(s32[64]{0:T(128)} %sizes_hbm.1) | copy-start | bytes 772
  34.2 25.8 %copy-start = (f32[16,2,128,128]{3,2,1,0:T(8,128)S(1)}, f32[16,2,128,128]{3,2,1,0:T(8,128)}, u32[]{:S(2)}) copy-start(f32[16,2,128,128]{3,2,1,0:T(8,128)} %left.1) | copy-start | bytes 6291460
  34.2 25.8 %copy-start.1 = (f32[16,2,128,128]{3,2,1,0:T(8,128)S(1)}, f32[16,2,128,128]{3,2,1,0:T(8,128)}, u32[]{:S(2)}) copy-start(f32[16,2,128,128]{3,2,1,0:T(8,128)} %right.1) | copy-start | bytes 6291460
  34.2 25.8 %copy-start.4 = (s32[2,16]{1,0:T(2,128)S(1)}, s32[2,16]{1,0:T(2,128)}, u32[]{:S(2)}) copy-start(s32[2,16]{1,0:T(2,128)} %coupling_hbm.1) | copy-start | bytes 388
  34.2 25.8 %copy-start.5 = (s32[64]{0:T(128)S(1)}, s32[64]{0:T(128)}, u32[]{:S(2)}) copy-start(s32[64]{0:T(128)} %assign_hbm.1) | copy-start | bytes 772
  55.0 8.7 %collective-permute-start = (f32[512,8,128]{2,1,0:T(8,128)S(1)}, f32[512,8,128]{2,1,0:T(8,128)S(1)}, u32[]{:S(2)}, u32[]{:S(2)}) collective-permute-start(f32[512,8,128]{2,1,0:T(8,128)S(1)} %bitcast.7), channel_id=1, source_target_pairs={{0,32},{1,33},{2,34},{3,35},{4,36},{5,37},{6,38},{7,39},{8,40},{9,... | collective-permute-start | bytes 6291464 | tf_op jit(solution)/shard_map/ppermute | solution.py:283
  116.9 6.6 %collective-permute-start.1 = (f32[2,16,8,8,128]{4,3,2,1,0:T(8,128)S(1)}, f32[2,16,8,8,128]{4,3,2,1,0:T(8,128)S(1)}, u32[]{:S(2)}, u32[]{:S(2)}) collective-permute-start(f32[2,16,8,8,128]{4,3,2,1,0:T(8,128)S(1)} %shard_map.88), channel_id=1, source_target_pairs={{0,32},{1,33},{2,34},{3,35},{4,36},{5,37},{6,38},{7,39},{8,40},{9,... | collective-permute-start | bytes 3145736 | tf_op jit(solution)/shard_map/ppermute | solution.py:320
  122.1 12.9 %copy-start.2 = (f32[2,8,128]{2,1,0:T(8,128)S(1)}, f32[2,8,128]{2,1,0:T(8,128)}, u32[]{:S(2)}) copy-start(f32[2,8,128]{2,1,0:T(8,128)} %psi.1) | copy-start | bytes 24580
  122.1 12.9 %copy-start.3 = (f32[2,8,128]{2,1,0:T(8,128)S(1)}, f32[2,8,128]{2,1,0:T(8,128)}, u32[]{:S(2)}) copy-start(f32[2,8,128]{2,1,0:T(8,128)} %get-tuple-element.11.sigma) | copy-start | bytes 24580

commit v8 on v6

--- a/solution.py
+++ b/solution.py
@@ -32,7 +32,7 @@
 
 def cube(x, zl, core, y, zh):
     z = 2 * zh + zl
-    return (x - core) % 4 // 2, (y - core) % 8 // 2, (z - core) % 8 // 2, core
+    return (x + core - 1) % 4 // 2, (y - core) % 8 // 2, (z - core) % 8 // 2, core
 
 
 def kind(x, zl, core, y, zh):
@@ -187,7 +187,8 @@
         sigma[t] = total
         for i in range(SECS):
             copies[i, t] = total
-    other_base[...] = parts[op + 1 - 2 * (op % 2), SLOTS].astype(jnp.int32)
+    numbers = parts[op + 1 - 2 * (op % 2), SLOTS]
+    other_base[...] = numbers[:SLOTS, :LOCAL_TERMS].astype(jnp.int32)
 
 
 def pack(other_base, mine, packed):
@@ -311,7 +312,7 @@
     parts = exchange(parts, SAME_SEC)
     sigma_first, copies, other_base = call(
         finish_first,
-        (vec, shape(SECS, SLOTS, ROWS, WIDTH), shape(ROWS, WIDTH, dtype=ints)),
+        (vec, shape(SECS, SLOTS, ROWS, WIDTH), shape(SLOTS, LOCAL_TERMS, dtype=ints)),
         (VMEM,) * 3,
         (VMEM, VMEM),
     )(masks, parts)

time: 136 us -> 135 us (level)
  starting transfers between devices: 3.83 us -> 8.43 us
  blocking collectives: 117 us -> 113 us
    all_to_all x6, blocking collectives: 117 us -> 113 us  [exchange(): return lax.all_to_all(parts, AXES, 0, 0, axis_index_groups=members)]
    ppermute x1, starting transfers between devices: 1.91 us -> 5.04 us  [on_device(): start_other = lax.ppermute(start_mine, AXES, OTHER_CORE)]
    ppermute x1, starting transfers between devices: 1.92 us -> 3.39 us  [on_device(): other = lax.ppermute(packed, AXES, OTHER_CORE)]
where the time goes in v8:
time: 135 us
  blocking collectives  113 us (84%)
  Pallas kernels  9.81 us (7%)
  starting transfers between devices  8.43 us (6%)
  waiting for transfers between devices  2.17 us (2%)
    all_to_all x6, blocking collectives, exchange(): return lax.all_to_all(parts, AXES, 0, 0, axis_index_groups=members)  113 us
    ppermute x1, starting transfers between devices, on_device(): start_other = lax.ppermute(start_mine, AXES, OTHER_CORE)  5.04 us
    ppermute x1, starting transfers between devices, on_device(): other = lax.ppermute(packed, AXES, OTHER_CORE)  3.39 us
    pallas_call x1, Pallas kernels, on_device(): call(prepare, (shape(SLOTS, LOCAL_TERMS, dtype=ints), chunk, shape(SECTOR...  2.93 us
  transfers between devices with their start and end apart: 2, of which 2 were waited for; matrix products, arithmetic and copies ran while one was open for 0% of the time, Pallas kernels for 3%

profile of v8, /device:TPU:1, one launch (start us, length us, event | category | flops | bytes accessed | tf_op | source)
XLA Modules:
  0.0 134.9 jit_solution(13587307186377735665)
XLA Ops:
  0.6 0.7 broadcast_in_dim.20
  1.3 30.8 %all_to_all.30 = f32[32,2,8,128]{3,2,1,0:T(8,128)S(1)} all-to-all(f32[32,2,8,128]{3,2,1,0:T(8,128)S(1)} %broadcast_in_dim.20), channel_id=1, replica_groups={{0,8,16,24,324,332,340,348,1,9,17,25,325,333,341,349,2,10,18,26,326,334..., dimensions={0} | all-to-all | bytes 524288 | tf_op jit(solution)/shard_map/all_to_all | solution.py:51
  32.2 0.0 copy-start.6
  32.2 0.1 broadcast_in_dim.22
  32.3 0.0 copy-start
  32.3 0.0 copy-start.1
  32.3 0.0 copy-start.4
  32.3 0.0 copy-start.5
  32.3 21.9 %all_to_all.31 = f32[8,64,8,128]{3,2,1,0:T(8,128)S(1)} all-to-all(f32[8,64,8,128]{3,2,1,0:T(8,128)S(1)} %broadcast_in_dim.22), channel_id=1, replica_groups={{0,4,452,448,68,64,384,388},{1,5,453,449,69,65,385,389},{2,6,454,450,70..., dimensions={0} | all-to-all | bytes 4194304 | tf_op jit(solution)/shard_map/all_to_all | solution.py:51
  54.2 5.0 %collective-permute-start = (f32[512,8,128]{2,1,0:T(8,128)S(1)}, f32[512,8,128]{2,1,0:T(8,128)S(1)}, u32[]{:S(2)}, u32[]{:S(2)}) collective-permute-start(f32[512,8,128]{2,1,0:T(8,128)S(1)} %bitcast.7), channel_id=1, source_target_pairs={{0,32},{1,33},{2,34},{3,35},{4,36},{5,37},{6,38},{7,39},{8,40},{9,... | collective-permute-start | bytes 6291464 | tf_op jit(solution)/shard_map/ppermute | solution.py:286
  59.3 0.0 copy-done.6
  59.3 0.0 copy-done
  59.3 0.0 copy-done.1
  59.3 0.0 copy-done.4
  59.3 0.0 copy-done.5
  59.3 2.9 %shard_map.85 = (s32[2,16]{1,0:T(2,128)S(1)}, f32[8,128]{1,0:T(8,128)S(1)}, s32[64]{0:T(128)S(1)}, f32[2,8,128]{2,1,0:T(8,128)S(1)}, bf16[16,2,128,256]{3,2,1,0:...) custom-call(s32[2,16]{1,0:T(2,128)S(1)} %copy-done.4, s32[64]{0:T(128)S(1)} %copy-done.5, s32[64]{0:T(128)S(1)} %copy-done.6, ...), custom_call_target="tpu_custom_call" | custom-call | flops 1073741824 | bytes 8388608 | tf_op jit(solution)/shard_map/pallas_call | solution.py:287
  62.3 0.8 collective-permute-done.other
  63.1 2.0 %shard_map.86 = f32[16,3,8,128]{3,2,1,0:T(8,128)S(1)} custom-call(s32[2,16]{1,0:T(2,128)S(1)} %get-tuple-element.15.base, f32[8,128]{1,0:T(8,128)S(1)} %get-tuple-element.16.bases, f32[512,8,128]{2,1,0:T(8,128)S(1)} %bitcast.8, f32[512,8,128]{2,1,0:T(8,128)S(1)} %collective-permute-done.other, bf16[16,2,128,256]{3,2,1,0:T(8,128)(2,1)S(1)} %get-tuple-element.17.lefts, ...), custom_call_target="tpu_custom_call" | custom-call | flops 1073741824 | bytes 1048576 | tf_op jit(solution)/shard_map/pallas_call | solution.py:309
  65.1 9.5 %all_to_all.32.parts = f32[16,3,8,128]{3,2,1,0:T(8,128)S(1)} all-to-all(f32[16,3,8,128]{3,2,1,0:T(8,128)S(1)} %shard_map.86), channel_id=1, replica_groups={{0,32,64,96,128,160,192,224,256,288,320,352,384,416,448,480},{1,33,65,9..., dimensions={0} | all-to-all | bytes 393216 | tf_op jit(solution)/shard_map/all_to_all | solution.py:51
  74.6 0.6 shard_map.87
  75.2 16.8 %all_to_all.33 = f32[32,2,8,128]{3,2,1,0:T(8,128)S(1)} all-to-all(f32[32,2,8,128]{3,2,1,0:T(8,128)S(1)} %get-tuple-element.20), channel_id=1, replica_groups={{0,8,16,24,324,332,340,348,1,9,17,25,325,333,341,349,2,10,18,26,326,334..., dimensions={0} | all-to-all | bytes 524288 | tf_op jit(solution)/shard_map/all_to_all | solution.py:51
  92.0 0.1 broadcast_in_dim.24
  92.1 24.2 %all_to_all.34 = f32[8,64,8,128]{3,2,1,0:T(8,128)S(1)} all-to-all(f32[8,64,8,128]{3,2,1,0:T(8,128)S(1)} %broadcast_in_dim.24), channel_id=1, replica_groups={{0,4,452,448,68,64,384,388},{1,5,453,449,69,65,385,389},{2,6,454,450,70..., dimensions={0} | all-to-all | bytes 4194304 | tf_op jit(solution)/shard_map/all_to_all | solution.py:51
  116.3 0.7 shard_map.88
  117.0 3.4 %collective-permute-start.1 = (f32[2,16,8,8,128]{4,3,2,1,0:T(8,128)S(1)}, f32[2,16,8,8,128]{4,3,2,1,0:T(8,128)S(1)}, u32[]{:S(2)}, u32[]{:S(2)}) collective-permute-start(f32[2,16,8,8,128]{4,3,2,1,0:T(8,128)S(1)} %shard_map.88), channel_id=1, source_target_pairs={{0,32},{1,33},{2,34},{3,35},{4,36},{5,37},{6,38},{7,39},{8,40},{9,... | collective-permute-start | bytes 3145736 | tf_op jit(solution)/shard_map/ppermute | solution.py:323
  120.4 0.9 shard_map.89.sums
  121.3 1.4 %collective-permute-done.1.packed = f32[2,16,8,8,128]{4,3,2,1,0:T(8,128)S(1)} collective-permute-done((f32[2,16,8,8,128]{4,3,2,1,0:T(8,128)S(1)}, f32[2,16,8,8,128]{4,3,2,1,0:T(8,128)S(1)}, u32[]{:S(2)}, u32[]{:S(2)}) %collective-permute-start.1) | collective-permute-done | bytes 1048608 | tf_op jit(solution)/shard_map/ppermute | solution.py:323
  122.7 2.0 %shard_map.90 = f32[16,3,8,128]{3,2,1,0:T(8,128)S(1)} custom-call(s32[2,16]{1,0:T(2,128)S(1)} %get-tuple-element.15.base, f32[512,8,128]{2,1,0:T(8,128)S(1)} %bitcast.6, f32[2,16,8,8,128]{4,3,2,1,0:T(8,128)S(1)} %collective-permute-done.1.packed, bf16[16,2,128,256]{3,2,1,0:T(8,128)(2,1)S(1)} %get-tuple-element.17.lefts, ...), custom_call_target="tpu_custom_call" | custom-call | flops 1073741824 | bytes 1048576 | tf_op jit(solution)/shard_map/pallas_call | solution.py:332
  124.7 9.5 %all_to_all.35.parts = f32[16,3,8,128]{3,2,1,0:T(8,128)S(1)} all-to-all(f32[16,3,8,128]{3,2,1,0:T(8,128)S(1)} %shard_map.90), channel_id=1, replica_groups={{0,32,64,96,128,160,192,224,256,288,320,352,384,416,448,480},{1,33,65,9..., dimensions={0} | all-to-all | bytes 393216 | tf_op jit(solution)/shard_map/all_to_all | solution.py:51
  134.2 0.0 copy-done.2
  134.2 0.0 copy-done.3
  134.2 0.7 shard_map.91
  (2 shorter events, 0.0 us)
Async XLA Ops:
  32.2 27.1 %copy-start.6 = (s32[64]{0:T(128)S(1)}, s32[64]{0:T(128)}, u32[]{:S(2)}) copy-start(s32[64]{0:T(128)} %sizes_hbm.1) | copy-start | bytes 772
  32.3 27.0 %copy-start = (f32[16,2,128,128]{3,2,1,0:T(8,128)S(1)}, f32[16,2,128,128]{3,2,1,0:T(8,128)}, u32[]{:S(2)}) copy-start(f32[16,2,128,128]{3,2,1,0:T(8,128)} %left.1) | copy-start | bytes 6291460
  32.3 27.0 %copy-start.1 = (f32[16,2,128,128]{3,2,1,0:T(8,128)S(1)}, f32[16,2,128,128]{3,2,1,0:T(8,128)}, u32[]{:S(2)}) copy-start(f32[16,2,128,128]{3,2,1,0:T(8,128)} %right.1) | copy-start | bytes 6291460
  32.3 27.0 %copy-start.4 = (s32[2,16]{1,0:T(2,128)S(1)}, s32[2,16]{1,0:T(2,128)}, u32[]{:S(2)}) copy-start(s32[2,16]{1,0:T(2,128)} %coupling_hbm.1) | copy-start | bytes 388
  32.3 27.0 %copy-start.5 = (s32[64]{0:T(128)S(1)}, s32[64]{0:T(128)}, u32[]{:S(2)}) copy-start(s32[64]{0:T(128)} %assign_hbm.1) | copy-start | bytes 772
  54.2 8.8 %collective-permute-start = (f32[512,8,128]{2,1,0:T(8,128)S(1)}, f32[512,8,128]{2,1,0:T(8,128)S(1)}, u32[]{:S(2)}, u32[]{:S(2)}) collective-permute-start(f32[512,8,128]{2,1,0:T(8,128)S(1)} %bitcast.7), channel_id=1, source_target_pairs={{0,32},{1,33},{2,34},{3,35},{4,36},{5,37},{6,38},{7,39},{8,40},{9,... | collective-permute-start | bytes 6291464 | tf_op jit(solution)/shard_map/ppermute | solution.py:286
  117.0 5.7 %collective-permute-start.1 = (f32[2,16,8,8,128]{4,3,2,1,0:T(8,128)S(1)}, f32[2,16,8,8,128]{4,3,2,1,0:T(8,128)S(1)}, u32[]{:S(2)}, u32[]{:S(2)}) collective-permute-start(f32[2,16,8,8,128]{4,3,2,1,0:T(8,128)S(1)} %shard_map.88), channel_id=1, source_target_pairs={{0,32},{1,33},{2,34},{3,35},{4,36},{5,37},{6,38},{7,39},{8,40},{9,... | collective-permute-start | bytes 3145736 | tf_op jit(solution)/shard_map/ppermute | solution.py:323
  121.3 12.9 %copy-start.2 = (f32[2,8,128]{2,1,0:T(8,128)S(1)}, f32[2,8,128]{2,1,0:T(8,128)}, u32[]{:S(2)}) copy-start(f32[2,8,128]{2,1,0:T(8,128)} %psi.1) | copy-start | bytes 24580
  121.3 12.9 %copy-start.3 = (f32[2,8,128]{2,1,0:T(8,128)S(1)}, f32[2,8,128]{2,1,0:T(8,128)}, u32[]{:S(2)}) copy-start(f32[2,8,128]{2,1,0:T(8,128)} %get-tuple-element.11.sigma) | copy-start | bytes 24580

commit v9 on v8

--- a/solution.py
+++ b/solution.py
@@ -115,14 +115,15 @@
     row = lax.broadcasted_iota(jnp.int32, (WIDTH, WIDTH), 0)
     col = lax.broadcasted_iota(jnp.int32, (WIDTH, WIDTH), 1)
     other = (row // 8 % 2 != op % 2).astype(jnp.int32)
-    order = (col == other * 64 + row // 16 * 8 + row % 8).astype(F32).astype(BF16)
+    spot = other * 128 + row // 16 * 8 + row % 8
+    lanes = lax.broadcasted_iota(jnp.int32, (WIDTH, 2 * WIDTH), 1)
+    spots = jnp.concatenate([spot, spot], axis=1)
+    order = jnp.concatenate([lanes == spots, lanes == spots + 64], axis=0).astype(F32).astype(BF16)
     for k in range(LOCAL_TERMS):
         for t in range(SLOTS):
             size = sizes[coupling[t, k]]
             high, low = halves(jnp.where(col < size, left[k, t], 0.0))
-            moved = matmul(jnp.concatenate([high, low], axis=0), order).astype(BF16)
-            lefts[k, t, :, :WIDTH] = moved[:WIDTH]
-            lefts[k, t, :, WIDTH:] = moved[WIDTH:]
+            lefts[k, t] = matmul(jnp.concatenate([high, low], axis=1), order).astype(BF16)
             high, low = halves(jnp.where(col < size, right[k, t], 0.0).T)
             rights[k, t, :, :WIDTH] = high
             rights[k, t, :, WIDTH:] = low
@@ -132,23 +133,31 @@
     return lax.dot_general(a, b, (((1,), (0,)), ((), ())), preferred_element_type=F32)
 
 
-def products(block_of, lefts, rights, store):
-    results = []
+def part_product(columns, chunks):
+    high, low = halves(jnp.concatenate(chunks, axis=0))
+    pair = jnp.concatenate([high, low], axis=1)
+    result = matmul(columns, jnp.concatenate([pair, pair], axis=0))
+    return result[:, :WIDTH] + result[:, WIDTH:]
+
+
+def own_products(base, mine, lefts, inner):
+    for t in range(SLOTS):
+        for k in range(LOCAL_TERMS):
+            inner[t, k] = part_product(lefts[k, t, :, :WIDTH], own_rows(mine, base[t, k]))
+
+
+def products(other_rows, inner, lefts, rights, out):
     for t in range(SLOTS):
         total = jnp.zeros((WIDTH, 2 * WIDTH), F32)
         for k in range(LOCAL_TERMS):
-            high, low = halves(block_of(t, k))
-            pair = jnp.concatenate([high, low], axis=1)
-            inner = matmul(lefts[k, t], jnp.concatenate([pair, pair], axis=0))
-            high, low = halves(inner[:, :WIDTH] + inner[:, WIDTH:])
+            high, low = halves(inner[t, k] + part_product(lefts[k, t, :, WIDTH:], other_rows(t, k)))
             rows = rights[k, t]
             total = total + matmul(
                 jnp.concatenate([high, low], axis=1), jnp.concatenate([rows, rows], axis=0)
             )
-        results.append(total[:, :WIDTH] + total[:, WIDTH:])
-    for t in range(SLOTS):
+        result = total[:, :WIDTH] + total[:, WIDTH:]
         for i in range(OPS):
-            store(i, t, results[t][i * ROWS : (i + 1) * ROWS])
+            out[i, t] = result[i * ROWS : (i + 1) * ROWS]
 
 
 def own_rows(field, first):
@@ -156,19 +165,8 @@
     return [field[starts[zl] + ((x + 2 * zl) % 4 * 128 + zl * 8)] for x in range(4) for zl in range(2)]
 
 
-def gathered_block(mine, other, first):
-    return jnp.concatenate(own_rows(mine, first) + own_rows(other, first), axis=0)
-
-
-def store_in(out):
-    def store(i, t, rows):
-        out[i, t] = rows
-
-    return store
-
-
-def apply_first(base, bases, mine, other, lefts, rights, out):
-    products(lambda t, k: gathered_block(mine, other, base[t, k]), lefts, rights, store_in(out))
+def apply_first(base, bases, inner, other, lefts, rights, out):
+    products(lambda t, k: own_rows(other, base[t, k]), inner, lefts, rights, out)
     for i in range(OPS):
         out[i, SLOTS] = bases[...]
 
@@ -245,12 +243,8 @@
     sums[...] = jnp.where(rows == 0, cross, jnp.where(rows == 1, square, left))
 
 
-def apply_next(base, mine, packed, lefts, rights, sums, out):
-    def block(t, k):
-        other = [packed[t, k, n] for n in range(OPS // 2)]
-        return jnp.concatenate(own_rows(mine, base[t, k]) + other, axis=0)
-
-    products(block, lefts, rights, store_in(out))
+def apply_next(inner, packed, lefts, rights, sums, out):
+    products(lambda t, k: [packed[t, k, n] for n in range(OPS // 2)], inner, lefts, rights, out)
     for i in range(OPS):
         out[i, SLOTS] = sums[...]
 
@@ -306,8 +300,10 @@
         flops=flops,
         moved=8 << 20,
     )(coupling, assign, sizes, left_env, right_env)
+    inner_shape = shape(SLOTS, LOCAL_TERMS, WIDTH, WIDTH)
+    own = call(own_products, inner_shape, VMEM, (SMEM, VMEM, VMEM), flops=flops // 2)
     parts = call(apply_first, parts_shape, VMEM, (SMEM,) + (VMEM,) * 5, flops=flops)(
-        base, bases, start_mine, start_other, lefts, rights
+        base, bases, own(base, start_mine, lefts), start_other, lefts, rights
     )
     parts = exchange(parts, SAME_SEC)
     sigma_first, copies, other_base = call(
@@ -329,8 +325,8 @@
         scratch=(pltpu.VMEM((SECTORS, ROWS, WIDTH), F32),),
         flops=flops,
     )(size_of, start_mine, mine)
-    parts = call(apply_next, parts_shape, VMEM, (SMEM,) + (VMEM,) * 5, flops=flops)(
-        base, mine, other, lefts, rights, sums
+    parts = call(apply_next, parts_shape, VMEM, (VMEM,) * 5, flops=flops)(
+        own(base, mine, lefts), other, lefts, rights, sums
     )
     parts = exchange(parts, SAME_SEC)
     next_vector, sigma_next = call(finish_next, (vec, vec), (VMEM, VMEM), (VMEM,) * 4)(

time: 135 us -> 135 us (level)
  waiting for transfers between devices: 2.17 us -> 0.13 us
  Pallas kernels: 9.81 us -> 11.8 us
    pallas_call x1 -> x3, Pallas kernels: 2.01 us -> 4 us  [the longest x1 1.49 us: on_device(): call(apply_next, parts_shape, VMEM, (VMEM,) * 5, flops=flops)]
  transfers between devices with their start and end apart: 2 -> 2, of which waited for: 2 -> 1; matrix products, arithmetic and copies ran while one was open for 0% -> 0% of each run, Pallas kernels for 3% -> 5%
where the time goes in v9:
time: 135 us
  blocking collectives  112 us (83%)
  Pallas kernels  11.8 us (9%)
  starting transfers between devices  8.92 us (7%)
    all_to_all x6, blocking collectives, exchange(): return lax.all_to_all(parts, AXES, 0, 0, axis_index_groups=members)  112 us
    ppermute x1, starting transfers between devices, on_device(): start_other = lax.ppermute(start_mine, AXES, OTHER_CORE)  5.04 us
    ppermute x1, starting transfers between devices, on_device(): other = lax.ppermute(packed, AXES, OTHER_CORE)  3.87 us
    pallas_call x1, Pallas kernels, on_device(): call(prepare, (shape(SLOTS, LOCAL_TERMS, dtype=ints), chunk, shape(SECTOR...  2.89 us
  transfers between devices with their start and end apart: 2, of which 1 were waited for; matrix products, arithmetic and copies ran while one was open for 0% of the time, Pallas kernels for 5%

profile of v9, /device:TPU:1, one launch (start us, length us, event | category | flops | bytes accessed | tf_op | source)
XLA Modules:
  0.0 134.5 jit_solution(5155794553423875464)
XLA Ops:
  0.6 0.7 broadcast_in_dim.20
  1.3 30.8 %all_to_all.30 = f32[32,2,8,128]{3,2,1,0:T(8,128)S(1)} all-to-all(f32[32,2,8,128]{3,2,1,0:T(8,128)S(1)} %broadcast_in_dim.20), channel_id=1, replica_groups={{0,8,16,24,324,332,340,348,1,9,17,25,325,333,341,349,2,10,18,26,326,334..., dimensions={0} | all-to-all | bytes 524288 | tf_op jit(solution)/shard_map/all_to_all | solution.py:51
  32.2 0.1 broadcast_in_dim.22
  32.3 0.0 copy-start
  32.3 0.0 copy-start.1
  32.3 0.0 copy-start.4
  32.3 0.0 copy-start.5
  32.3 21.9 %all_to_all.31 = f32[8,64,8,128]{3,2,1,0:T(8,128)S(1)} all-to-all(f32[8,64,8,128]{3,2,1,0:T(8,128)S(1)} %broadcast_in_dim.22), channel_id=1, replica_groups={{0,4,452,448,68,64,384,388},{1,5,453,449,69,65,385,389},{2,6,454,450,70..., dimensions={0} | all-to-all | bytes 4194304 | tf_op jit(solution)/shard_map/all_to_all | solution.py:51
  54.2 5.0 %collective-permute-start = (f32[512,8,128]{2,1,0:T(8,128)S(1)}, f32[512,8,128]{2,1,0:T(8,128)S(1)}, u32[]{:S(2)}, u32[]{:S(2)}) collective-permute-start(f32[512,8,128]{2,1,0:T(8,128)S(1)} %bitcast.7), channel_id=1, source_target_pairs={{0,32},{1,33},{2,34},{3,35},{4,36},{5,37},{6,38},{7,39},{8,40},{9,... | collective-permute-start | bytes 6291464 | tf_op jit(solution)/shard_map/ppermute | solution.py:280
  59.3 0.0 copy-done.6
  59.3 0.0 copy-done
  59.3 0.0 copy-done.1
  59.3 0.0 copy-done.4
  59.3 0.0 copy-done.5
  59.3 2.9 %shard_map.85 = (s32[2,16]{1,0:T(2,128)S(1)}, f32[8,128]{1,0:T(8,128)S(1)}, s32[64]{0:T(128)S(1)}, f32[2,8,128]{2,1,0:T(8,128)S(1)}, bf16[16,2,128,256]{3,2,1,0:...) custom-call(s32[2,16]{1,0:T(2,128)S(1)} %copy-done.4, s32[64]{0:T(128)S(1)} %copy-done.5, s32[64]{0:T(128)S(1)} %copy-done.6, ...), custom_call_target="tpu_custom_call" | custom-call | flops 1073741824 | bytes 8388608 | tf_op jit(solution)/shard_map/pallas_call | solution.py:281
  62.2 1.3 shard_map.86.inner
  63.5 0.0 collective-permute-done.other
  63.5 2.1 %shard_map.87 = f32[16,3,8,128]{3,2,1,0:T(8,128)S(1)} custom-call(s32[2,16]{1,0:T(2,128)S(1)} %get-tuple-element.15.base, f32[8,128]{1,0:T(8,128)S(1)} %get-tuple-element.16.bases, f32[2,16,128,128]{3,2,1,0:T(8,128)S(1)} %shard_map.86.inner, f32[512,8,128]{2,1,0:T(8,128)S(1)} %collective-permute-done.other, ...), custom_call_target="tpu_custom_call" | custom-call | flops 1073741824 | bytes 1048576 | tf_op jit(solution)/shard_map/pallas_call | solution.py:305
  65.6 9.1 %all_to_all.32.parts = f32[16,3,8,128]{3,2,1,0:T(8,128)S(1)} all-to-all(f32[16,3,8,128]{3,2,1,0:T(8,128)S(1)} %shard_map.87), channel_id=1, replica_groups={{0,32,64,96,128,160,192,224,256,288,320,352,384,416,448,480},{1,33,65,9..., dimensions={0} | all-to-all | bytes 393216 | tf_op jit(solution)/shard_map/all_to_all | solution.py:51
  74.7 0.6 shard_map.88
  75.4 16.8 %all_to_all.33 = f32[32,2,8,128]{3,2,1,0:T(8,128)S(1)} all-to-all(f32[32,2,8,128]{3,2,1,0:T(8,128)S(1)} %get-tuple-element.20), channel_id=1, replica_groups={{0,8,16,24,324,332,340,348,1,9,17,25,325,333,341,349,2,10,18,26,326,334..., dimensions={0} | all-to-all | bytes 524288 | tf_op jit(solution)/shard_map/all_to_all | solution.py:51
  92.1 0.1 broadcast_in_dim.24
  92.3 23.8 %all_to_all.34 = f32[8,64,8,128]{3,2,1,0:T(8,128)S(1)} all-to-all(f32[8,64,8,128]{3,2,1,0:T(8,128)S(1)} %broadcast_in_dim.24), channel_id=1, replica_groups={{0,4,452,448,68,64,384,388},{1,5,453,449,69,65,385,389},{2,6,454,450,70..., dimensions={0} | all-to-all | bytes 4194304 | tf_op jit(solution)/shard_map/all_to_all | solution.py:51
  116.0 0.7 shard_map.90
  116.7 3.9 %collective-permute-start.1 = (f32[2,16,8,8,128]{4,3,2,1,0:T(8,128)S(1)}, f32[2,16,8,8,128]{4,3,2,1,0:T(8,128)S(1)}, u32[]{:S(2)}, u32[]{:S(2)}) collective-permute-start(f32[2,16,8,8,128]{4,3,2,1,0:T(8,128)S(1)} %shard_map.90), channel_id=1, source_target_pairs={{0,32},{1,33},{2,34},{3,35},{4,36},{5,37},{6,38},{7,39},{8,40},{9,... | collective-permute-start | bytes 3145736 | tf_op jit(solution)/shard_map/ppermute | solution.py:319
  120.6 1.3 shard_map.89.inner
  121.9 0.9 shard_map.91.sums
  122.7 0.1 collective-permute-done.1.packed
  122.9 1.5 %shard_map.92 = f32[16,3,8,128]{3,2,1,0:T(8,128)S(1)} custom-call(f32[2,16,128,128]{3,2,1,0:T(8,128)S(1)} %shard_map.89.inner, f32[2,16,8,8,128]{4,3,2,1,0:T(8,128)S(1)} %collective-permute-done.1.packed, bf16[16,2,128,256]{3,2,1,0:T(8,128)(2,1)S(1)} %get-tuple-element.17.lefts, bf16[16,2,128,256]{3,2,1,0:T(8,128)(2,1)S(1)} %get-tuple-element.18.rights, ...), custom_call_target="tpu_custom_call" | custom-call | flops 1073741824 | bytes 1048576 | tf_op jit(solution)/shard_map/pallas_call | solution.py:328
  124.4 9.5 %all_to_all.35.parts = f32[16,3,8,128]{3,2,1,0:T(8,128)S(1)} all-to-all(f32[16,3,8,128]{3,2,1,0:T(8,128)S(1)} %shard_map.92), channel_id=1, replica_groups={{0,32,64,96,128,160,192,224,256,288,320,352,384,416,448,480},{1,33,65,9..., dimensions={0} | all-to-all | bytes 393216 | tf_op jit(solution)/shard_map/all_to_all | solution.py:51
  133.9 0.0 copy-done.2
  133.9 0.7 shard_map.93
  (4 shorter events, 0.0 us)
Async XLA Ops:
  32.2 27.1 %copy-start.6 = (s32[64]{0:T(128)S(1)}, s32[64]{0:T(128)}, u32[]{:S(2)}) copy-start(s32[64]{0:T(128)} %sizes_hbm.1) | copy-start | bytes 772
  32.3 27.0 %copy-start = (f32[16,2,128,128]{3,2,1,0:T(8,128)S(1)}, f32[16,2,128,128]{3,2,1,0:T(8,128)}, u32[]{:S(2)}) copy-start(f32[16,2,128,128]{3,2,1,0:T(8,128)} %left.1) | copy-start | bytes 6291460
  32.3 27.0 %copy-start.1 = (f32[16,2,128,128]{3,2,1,0:T(8,128)S(1)}, f32[16,2,128,128]{3,2,1,0:T(8,128)}, u32[]{:S(2)}) copy-start(f32[16,2,128,128]{3,2,1,0:T(8,128)} %right.1) | copy-start | bytes 6291460
  32.3 27.0 %copy-start.4 = (s32[2,16]{1,0:T(2,128)S(1)}, s32[2,16]{1,0:T(2,128)}, u32[]{:S(2)}) copy-start(s32[2,16]{1,0:T(2,128)} %coupling_hbm.1) | copy-start | bytes 388
  32.3 27.0 %copy-start.5 = (s32[64]{0:T(128)S(1)}, s32[64]{0:T(128)}, u32[]{:S(2)}) copy-start(s32[64]{0:T(128)} %assign_hbm.1) | copy-start | bytes 772
  54.2 9.3 %collective-permute-start = (f32[512,8,128]{2,1,0:T(8,128)S(1)}, f32[512,8,128]{2,1,0:T(8,128)S(1)}, u32[]{:S(2)}, u32[]{:S(2)}) collective-permute-start(f32[512,8,128]{2,1,0:T(8,128)S(1)} %bitcast.7), channel_id=1, source_target_pairs={{0,32},{1,33},{2,34},{3,35},{4,36},{5,37},{6,38},{7,39},{8,40},{9,... | collective-permute-start | bytes 6291464 | tf_op jit(solution)/shard_map/ppermute | solution.py:280
  116.7 6.1 %collective-permute-start.1 = (f32[2,16,8,8,128]{4,3,2,1,0:T(8,128)S(1)}, f32[2,16,8,8,128]{4,3,2,1,0:T(8,128)S(1)}, u32[]{:S(2)}, u32[]{:S(2)}) collective-permute-start(f32[2,16,8,8,128]{4,3,2,1,0:T(8,128)S(1)} %shard_map.90), channel_id=1, source_target_pairs={{0,32},{1,33},{2,34},{3,35},{4,36},{5,37},{6,38},{7,39},{8,40},{9,... | collective-permute-start | bytes 3145736 | tf_op jit(solution)/shard_map/ppermute | solution.py:319
  122.7 11.1 %copy-start.2 = (f32[2,8,128]{2,1,0:T(8,128)S(1)}, f32[2,8,128]{2,1,0:T(8,128)}, u32[]{:S(2)}) copy-start(f32[2,8,128]{2,1,0:T(8,128)} %psi.1) | copy-start | bytes 24580
  122.7 11.1 %copy-start.3 = (f32[2,8,128]{2,1,0:T(8,128)S(1)}, f32[2,8,128]{2,1,0:T(8,128)}, u32[]{:S(2)}) copy-start(f32[2,8,128]{2,1,0:T(8,128)} %get-tuple-element.11.sigma) | copy-start | bytes 24580

commit v10 on v9

--- a/solution.py
+++ b/solution.py
@@ -146,11 +146,11 @@
             inner[t, k] = part_product(lefts[k, t, :, :WIDTH], own_rows(mine, base[t, k]))
 
 
-def products(other_rows, inner, lefts, rights, out):
+def products(inner, rights, out):
     for t in range(SLOTS):
         total = jnp.zeros((WIDTH, 2 * WIDTH), F32)
         for k in range(LOCAL_TERMS):
-            high, low = halves(inner[t, k] + part_product(lefts[k, t, :, WIDTH:], other_rows(t, k)))
+            high, low = halves(inner(t, k))
             rows = rights[k, t]
             total = total + matmul(
                 jnp.concatenate([high, low], axis=1), jnp.concatenate([rows, rows], axis=0)
@@ -165,8 +165,16 @@
     return [field[starts[zl] + ((x + 2 * zl) % 4 * 128 + zl * 8)] for x in range(4) for zl in range(2)]
 
 
-def apply_first(base, bases, inner, other, lefts, rights, out):
-    products(lambda t, k: own_rows(other, base[t, k]), inner, lefts, rights, out)
+def apply_first(base, bases, mine, other, lefts, rights, out):
+    def inner(t, k):
+        pairs = []
+        for field in (mine, other):
+            high, low = halves(jnp.concatenate(own_rows(field, base[t, k]), axis=0))
+            pairs += [jnp.concatenate([high, low], axis=1)] * 2
+        result = matmul(lefts[k, t], jnp.concatenate(pairs, axis=0))
+        return result[:, :WIDTH] + result[:, WIDTH:]
+
+    products(inner, rights, out)
     for i in range(OPS):
         out[i, SLOTS] = bases[...]
 
@@ -243,8 +251,12 @@
     sums[...] = jnp.where(rows == 0, cross, jnp.where(rows == 1, square, left))
 
 
-def apply_next(inner, packed, lefts, rights, sums, out):
-    products(lambda t, k: [packed[t, k, n] for n in range(OPS // 2)], inner, lefts, rights, out)
+def apply_next(own, packed, lefts, rights, sums, out):
+    def inner(t, k):
+        other = [packed[t, k, n] for n in range(OPS // 2)]
+        return own[t, k] + part_product(lefts[k, t, :, WIDTH:], other)
+
+    products(inner, rights, out)
     for i in range(OPS):
         out[i, SLOTS] = sums[...]
 
@@ -300,10 +312,8 @@
         flops=flops,
         moved=8 << 20,
     )(coupling, assign, sizes, left_env, right_env)
-    inner_shape = shape(SLOTS, LOCAL_TERMS, WIDTH, WIDTH)
-    own = call(own_products, inner_shape, VMEM, (SMEM, VMEM, VMEM), flops=flops // 2)
     parts = call(apply_first, parts_shape, VMEM, (SMEM,) + (VMEM,) * 5, flops=flops)(
-        base, bases, own(base, start_mine, lefts), start_other, lefts, rights
+        base, bases, start_mine, start_other, lefts, rights
     )
     parts = exchange(parts, SAME_SEC)
     sigma_first, copies, other_base = call(
@@ -325,9 +335,10 @@
         scratch=(pltpu.VMEM((SECTORS, ROWS, WIDTH), F32),),
         flops=flops,
     )(size_of, start_mine, mine)
-    parts = call(apply_next, parts_shape, VMEM, (VMEM,) * 5, flops=flops)(
-        own(base, mine, lefts), other, lefts, rights, sums
-    )
+    own = call(
+        own_products, shape(SLOTS, LOCAL_TERMS, WIDTH, WIDTH), VMEM, (SMEM, VMEM, VMEM), flops=flops // 2
+    )(base, mine, lefts)
+    parts = call(apply_next, parts_shape, VMEM, (VMEM,) * 5, flops=flops)(own, other, lefts, rights, sums)
     parts = exchange(parts, SAME_SEC)
     next_vector, sigma_next = call(finish_next, (vec, vec), (VMEM, VMEM), (VMEM,) * 4)(
         masks, parts, psi, sigma_first

time: 135 us -> 135 us (level)
  Pallas kernels: 11.8 us -> 10.4 us
  transfers between devices with their start and end apart: 2 -> 2, of which waited for: 1 -> 2; matrix products, arithmetic and copies ran while one was open for 0% -> 0% of each run, Pallas kernels for 5% -> 4%
where the time goes in v10:
time: 135 us; the launch traced here: 134 us
  blocking collectives  113 us (84%)
  Pallas kernels  10.4 us (8%)
  starting transfers between devices  8.37 us (6%)
    all_to_all x6, blocking collectives, exchange(): return lax.all_to_all(parts, AXES, 0, 0, axis_index_groups=members)  113 us
    ppermute x1, starting transfers between devices, on_device(): start_other = lax.ppermute(start_mine, AXES, OTHER_CORE)  5.04 us
    ppermute x1, starting transfers between devices, on_device(): other = lax.ppermute(packed, AXES, OTHER_CORE)  3.33 us
    pallas_call x1, Pallas kernels, on_device(): call(prepare, (shape(SLOTS, LOCAL_TERMS, dtype=ints), chunk, shape(SECTOR...  2.89 us
  transfers between devices with their start and end apart: 2, of which 2 were waited for; matrix products, arithmetic and copies ran while one was open for 0% of the time, Pallas kernels for 4%

profile of v10, /device:TPU:1, one launch (start us, length us, event | category | flops | bytes accessed | tf_op | source)
XLA Modules:
  0.0 134.2 jit_solution(3651140905053354640)
XLA Ops:
  0.6 0.7 broadcast_in_dim.20
  1.3 30.8 %all_to_all.30 = f32[32,2,8,128]{3,2,1,0:T(8,128)S(1)} all-to-all(f32[32,2,8,128]{3,2,1,0:T(8,128)S(1)} %broadcast_in_dim.20), channel_id=1, replica_groups={{0,8,16,24,324,332,340,348,1,9,17,25,325,333,341,349,2,10,18,26,326,334..., dimensions={0} | all-to-all | bytes 524288 | tf_op jit(solution)/shard_map/all_to_all | solution.py:51
  32.2 0.1 broadcast_in_dim.22
  32.3 0.0 copy-start
  32.3 0.0 copy-start.1
  32.3 0.0 copy-start.4
  32.3 0.0 copy-start.5
  32.3 21.9 %all_to_all.31 = f32[8,64,8,128]{3,2,1,0:T(8,128)S(1)} all-to-all(f32[8,64,8,128]{3,2,1,0:T(8,128)S(1)} %broadcast_in_dim.22), channel_id=1, replica_groups={{0,4,452,448,68,64,384,388},{1,5,453,449,69,65,385,389},{2,6,454,450,70..., dimensions={0} | all-to-all | bytes 4194304 | tf_op jit(solution)/shard_map/all_to_all | solution.py:51
  54.2 5.0 %collective-permute-start = (f32[512,8,128]{2,1,0:T(8,128)S(1)}, f32[512,8,128]{2,1,0:T(8,128)S(1)}, u32[]{:S(2)}, u32[]{:S(2)}) collective-permute-start(f32[512,8,128]{2,1,0:T(8,128)S(1)} %bitcast.7), channel_id=1, source_target_pairs={{0,32},{1,33},{2,34},{3,35},{4,36},{5,37},{6,38},{7,39},{8,40},{9,... | collective-permute-start | bytes 6291464 | tf_op jit(solution)/shard_map/ppermute | solution.py:292
  59.3 0.0 copy-done.6
  59.3 0.0 copy-done
  59.3 0.0 copy-done.1
  59.3 0.0 copy-done.4
  59.3 0.0 copy-done.5
  59.3 2.9 %shard_map.85 = (s32[2,16]{1,0:T(2,128)S(1)}, f32[8,128]{1,0:T(8,128)S(1)}, s32[64]{0:T(128)S(1)}, f32[2,8,128]{2,1,0:T(8,128)S(1)}, bf16[16,2,128,256]{3,2,1,0:...) custom-call(s32[2,16]{1,0:T(2,128)S(1)} %copy-done.4, s32[64]{0:T(128)S(1)} %copy-done.5, s32[64]{0:T(128)S(1)} %copy-done.6, ...), custom_call_target="tpu_custom_call" | custom-call | flops 1073741824 | bytes 8388608 | tf_op jit(solution)/shard_map/pallas_call | solution.py:293
  62.2 0.8 collective-permute-done.other
  63.1 2.0 %shard_map.86 = f32[16,3,8,128]{3,2,1,0:T(8,128)S(1)} custom-call(s32[2,16]{1,0:T(2,128)S(1)} %get-tuple-element.15.base, f32[8,128]{1,0:T(8,128)S(1)} %get-tuple-element.16.bases, f32[512,8,128]{2,1,0:T(8,128)S(1)} %bitcast.8, f32[512,8,128]{2,1,0:T(8,128)S(1)} %collective-permute-done.other, bf16[16,2,128,256]{3,2,1,0:T(8,128)(2,1)S(1)} %get-tuple-element.17.lefts, ...), custom_call_target="tpu_custom_call" | custom-call | flops 1073741824 | bytes 1048576 | tf_op jit(solution)/shard_map/pallas_call | solution.py:315
  65.0 9.5 %all_to_all.32.parts = f32[16,3,8,128]{3,2,1,0:T(8,128)S(1)} all-to-all(f32[16,3,8,128]{3,2,1,0:T(8,128)S(1)} %shard_map.86), channel_id=1, replica_groups={{0,32,64,96,128,160,192,224,256,288,320,352,384,416,448,480},{1,33,65,9..., dimensions={0} | all-to-all | bytes 393216 | tf_op jit(solution)/shard_map/all_to_all | solution.py:51
  74.5 0.6 shard_map.87
  75.2 16.8 %all_to_all.33 = f32[32,2,8,128]{3,2,1,0:T(8,128)S(1)} all-to-all(f32[32,2,8,128]{3,2,1,0:T(8,128)S(1)} %get-tuple-element.20), channel_id=1, replica_groups={{0,8,16,24,324,332,340,348,1,9,17,25,325,333,341,349,2,10,18,26,326,334..., dimensions={0} | all-to-all | bytes 524288 | tf_op jit(solution)/shard_map/all_to_all | solution.py:51
  91.9 0.1 broadcast_in_dim.24
  92.1 24.2 %all_to_all.34 = f32[8,64,8,128]{3,2,1,0:T(8,128)S(1)} all-to-all(f32[8,64,8,128]{3,2,1,0:T(8,128)S(1)} %broadcast_in_dim.24), channel_id=1, replica_groups={{0,4,452,448,68,64,384,388},{1,5,453,449,69,65,385,389},{2,6,454,450,70..., dimensions={0} | all-to-all | bytes 4194304 | tf_op jit(solution)/shard_map/all_to_all | solution.py:51
  116.3 0.7 shard_map.89
  117.0 3.3 %collective-permute-start.1 = (f32[2,16,8,8,128]{4,3,2,1,0:T(8,128)S(1)}, f32[2,16,8,8,128]{4,3,2,1,0:T(8,128)S(1)}, u32[]{:S(2)}, u32[]{:S(2)}) collective-permute-start(f32[2,16,8,8,128]{4,3,2,1,0:T(8,128)S(1)} %shard_map.89), channel_id=1, source_target_pairs={{0,32},{1,33},{2,34},{3,35},{4,36},{5,37},{6,38},{7,39},{8,40},{9,... | collective-permute-start | bytes 3145736 | tf_op jit(solution)/shard_map/ppermute | solution.py:329
  120.3 1.3 shard_map.88.own
  121.6 0.9 shard_map.90.sums
  122.5 0.1 collective-permute-done.1.packed
  122.6 1.5 %shard_map.91 = f32[16,3,8,128]{3,2,1,0:T(8,128)S(1)} custom-call(f32[2,16,128,128]{3,2,1,0:T(8,128)S(1)} %shard_map.88.own, f32[2,16,8,8,128]{4,3,2,1,0:T(8,128)S(1)} %collective-permute-done.1.packed, bf16[16,2,128,256]{3,2,1,0:T(8,128)(2,1)S(1)} %get-tuple-element.17.lefts, bf16[16,2,128,256]{3,2,1,0:T(8,128)(2,1)S(1)} %get-tuple-element.18.rights, ...), custom_call_target="tpu_custom_call" | custom-call | flops 1073741824 | bytes 1048576 | tf_op jit(solution)/shard_map/pallas_call | solution.py:341
  124.1 9.5 %all_to_all.35.parts = f32[16,3,8,128]{3,2,1,0:T(8,128)S(1)} all-to-all(f32[16,3,8,128]{3,2,1,0:T(8,128)S(1)} %shard_map.91), channel_id=1, replica_groups={{0,32,64,96,128,160,192,224,256,288,320,352,384,416,448,480},{1,33,65,9..., dimensions={0} | all-to-all | bytes 393216 | tf_op jit(solution)/shard_map/all_to_all | solution.py:51
  133.6 0.0 copy-done.2
  133.6 0.0 copy-done.3
  133.6 0.7 shard_map.92
  (3 shorter events, 0.0 us)
Async XLA Ops:
  32.2 27.1 %copy-start.6 = (s32[64]{0:T(128)S(1)}, s32[64]{0:T(128)}, u32[]{:S(2)}) copy-start(s32[64]{0:T(128)} %sizes_hbm.1) | copy-start | bytes 772
  32.3 27.0 %copy-start = (f32[16,2,128,128]{3,2,1,0:T(8,128)S(1)}, f32[16,2,128,128]{3,2,1,0:T(8,128)}, u32[]{:S(2)}) copy-start(f32[16,2,128,128]{3,2,1,0:T(8,128)} %left.1) | copy-start | bytes 6291460
  32.3 27.0 %copy-start.1 = (f32[16,2,128,128]{3,2,1,0:T(8,128)S(1)}, f32[16,2,128,128]{3,2,1,0:T(8,128)}, u32[]{:S(2)}) copy-start(f32[16,2,128,128]{3,2,1,0:T(8,128)} %right.1) | copy-start | bytes 6291460
  32.3 27.0 %copy-start.4 = (s32[2,16]{1,0:T(2,128)S(1)}, s32[2,16]{1,0:T(2,128)}, u32[]{:S(2)}) copy-start(s32[2,16]{1,0:T(2,128)} %coupling_hbm.1) | copy-start | bytes 388
  32.3 27.0 %copy-start.5 = (s32[64]{0:T(128)S(1)}, s32[64]{0:T(128)}, u32[]{:S(2)}) copy-start(s32[64]{0:T(128)} %assign_hbm.1) | copy-start | bytes 772
  54.2 8.8 %collective-permute-start = (f32[512,8,128]{2,1,0:T(8,128)S(1)}, f32[512,8,128]{2,1,0:T(8,128)S(1)}, u32[]{:S(2)}, u32[]{:S(2)}) collective-permute-start(f32[512,8,128]{2,1,0:T(8,128)S(1)} %bitcast.7), channel_id=1, source_target_pairs={{0,32},{1,33},{2,34},{3,35},{4,36},{5,37},{6,38},{7,39},{8,40},{9,... | collective-permute-start | bytes 6291464 | tf_op jit(solution)/shard_map/ppermute | solution.py:292
  117.0 5.6 %collective-permute-start.1 = (f32[2,16,8,8,128]{4,3,2,1,0:T(8,128)S(1)}, f32[2,16,8,8,128]{4,3,2,1,0:T(8,128)S(1)}, u32[]{:S(2)}, u32[]{:S(2)}) collective-permute-start(f32[2,16,8,8,128]{4,3,2,1,0:T(8,128)S(1)} %shard_map.89), channel_id=1, source_target_pairs={{0,32},{1,33},{2,34},{3,35},{4,36},{5,37},{6,38},{7,39},{8,40},{9,... | collective-permute-start | bytes 3145736 | tf_op jit(solution)/shard_map/ppermute | solution.py:329
  122.4 11.1 %copy-start.2 = (f32[2,8,128]{2,1,0:T(8,128)S(1)}, f32[2,8,128]{2,1,0:T(8,128)}, u32[]{:S(2)}) copy-start(f32[2,8,128]{2,1,0:T(8,128)} %psi.1) | copy-start | bytes 24580
  122.4 11.1 %copy-start.3 = (f32[2,8,128]{2,1,0:T(8,128)S(1)}, f32[2,8,128]{2,1,0:T(8,128)}, u32[]{:S(2)}) copy-start(f32[2,8,128]{2,1,0:T(8,128)} %get-tuple-element.11.sigma) | copy-start | bytes 24580

commit v11 on v9

--- a/solution.py
+++ b/solution.py
@@ -92,7 +92,7 @@
 
 
 def prepare(
-    coupling_hbm, assign_hbm, sizes_hbm, left, right, base, bases, size_of, masks, lefts, rights, coupling, assign, sizes, slot_of, done
+    coupling_hbm, assign_hbm, sizes_hbm, left, right, bases, size_of, masks, lefts, rights, coupling, assign, sizes, slot_of, done
 ):
     fetch([(coupling_hbm, coupling), (assign_hbm, assign), (sizes_hbm, sizes)], done)
     op = lax.axis_index("op")
@@ -108,7 +108,6 @@
             p = slot_of[coupling[t, k]]
             y = p // 8
             first = y % 2 * 64 + p % 8 // 2 * 16 + y // 2 * 2 + p % 2
-            base[t, k] = first
             table = jnp.where((sub == t) & (lane == k), first, table)
         masks[t] = inside(size_of[lax.axis_index("sec") * SLOTS + t], op * ROWS).astype(F32)
     bases[...] = table.astype(F32)
@@ -140,7 +139,8 @@
     return result[:, :WIDTH] + result[:, WIDTH:]
 
 
-def own_products(base, mine, lefts, inner):
+def own_products(bases, mine, lefts, inner):
+    base = bases[...].astype(jnp.int32)
     for t in range(SLOTS):
         for k in range(LOCAL_TERMS):
             inner[t, k] = part_product(lefts[k, t, :, :WIDTH], own_rows(mine, base[t, k]))
@@ -165,7 +165,8 @@
     return [field[starts[zl] + ((x + 2 * zl) % 4 * 128 + zl * 8)] for x in range(4) for zl in range(2)]
 
 
-def apply_first(base, bases, inner, other, lefts, rights, out):
+def apply_first(bases, inner, other, lefts, rights, out):
+    base = bases[...].astype(jnp.int32)
     products(lambda t, k: own_rows(other, base[t, k]), inner, lefts, rights, out)
     for i in range(OPS):
         out[i, SLOTS] = bases[...]
@@ -190,9 +191,10 @@
 
 
 def pack(other_base, mine, packed):
+    base = other_base[...]
     for t in range(SLOTS):
         for k in range(LOCAL_TERMS):
-            for n, chunk in enumerate(own_rows(mine, other_base[t, k])):
+            for n, chunk in enumerate(own_rows(mine, base[t, k])):
                 packed[t, k, n] = chunk
 
 
@@ -278,17 +280,16 @@
 
     start_mine = gather(jnp.broadcast_to(psi[None], (SECS,) + psi.shape))
     start_other = lax.ppermute(start_mine, AXES, OTHER_CORE)
-    base, bases, size_of, masks, lefts, rights = call(
+    bases, size_of, masks, lefts, rights = call(
         prepare,
         (
-            shape(SLOTS, LOCAL_TERMS, dtype=ints),
             chunk,
             shape(SECTORS, dtype=ints),
             vec,
             env_shape,
             env_shape,
         ),
-        (SMEM, VMEM, SMEM, VMEM, VMEM, VMEM),
+        (VMEM, SMEM, VMEM, VMEM, VMEM),
         (HBM,) * 3 + (VMEM,) * 2,
         scratch=(
             pltpu.SMEM((SLOTS, LOCAL_TERMS), ints),
@@ -301,9 +302,9 @@
         moved=8 << 20,
     )(coupling, assign, sizes, left_env, right_env)
     inner_shape = shape(SLOTS, LOCAL_TERMS, WIDTH, WIDTH)
-    own = call(own_products, inner_shape, VMEM, (SMEM, VMEM, VMEM), flops=flops // 2)
-    parts = call(apply_first, parts_shape, VMEM, (SMEM,) + (VMEM,) * 5, flops=flops)(
-        base, bases, own(base, start_mine, lefts), start_other, lefts, rights
+    own = call(own_products, inner_shape, VMEM, (VMEM,) * 3, flops=flops // 2)
+    parts = call(apply_first, parts_shape, VMEM, (VMEM,) * 5, flops=flops)(
+        bases, own(bases, start_mine, lefts), start_other, lefts, rights
     )
     parts = exchange(parts, SAME_SEC)
     sigma_first, copies, other_base = call(
@@ -313,7 +314,7 @@
         (VMEM, VMEM),
     )(masks, parts)
     mine = gather(copies)
-    packed = call(pack, shape(SLOTS, LOCAL_TERMS, OPS // 2, ROWS, WIDTH), VMEM, (SMEM, VMEM))(
+    packed = call(pack, shape(SLOTS, LOCAL_TERMS, OPS // 2, ROWS, WIDTH), VMEM, (VMEM, VMEM))(
         other_base, mine
     )
     other = lax.ppermute(packed, AXES, OTHER_CORE)
@@ -326,7 +327,7 @@
         flops=flops,
     )(size_of, start_mine, mine)
     parts = call(apply_next, parts_shape, VMEM, (VMEM,) * 5, flops=flops)(
-        own(base, mine, lefts), other, lefts, rights, sums
+        own(bases, mine, lefts), other, lefts, rights, sums
     )
     parts = exchange(parts, SAME_SEC)
     next_vector, sigma_next = call(finish_next, (vec, vec), (VMEM, VMEM), (VMEM,) * 4)(

time: 135 us -> 134 us (level)
  Pallas kernels: 11.8 us -> 10 us
    pallas_call x5, Pallas kernels: 8.15 us -> 6.38 us  [the longest x1 2.66 us: on_device(): call(prepare, (chunk, shape(SECTORS, dtype=ints), vec, env_shape, env_sha...]
  transfers between devices with their start and end apart: 2 -> 2, of which waited for: 1 -> 2; matrix products, arithmetic and copies ran while one was open for 0% -> 0% of each run, Pallas kernels for 5% -> 4%
where the time goes in v11:
time: 134 us
  blocking collectives  113 us (84%)
  Pallas kernels  10 us (7%)
  starting transfers between devices  8.36 us (6%)
    all_to_all x6, blocking collectives, exchange(): return lax.all_to_all(parts, AXES, 0, 0, axis_index_groups=members)  113 us
    ppermute x1, starting transfers between devices, on_device(): start_other = lax.ppermute(start_mine, AXES, OTHER_CORE)  5.04 us
    ppermute x1, starting transfers between devices, on_device(): other = lax.ppermute(packed, AXES, OTHER_CORE)  3.31 us
  transfers between devices with their start and end apart: 2, of which 2 were waited for; matrix products, arithmetic and copies ran while one was open for 0% of the time, Pallas kernels for 4%

profile of v11, /device:TPU:1, one launch (start us, length us, event | category | flops | bytes accessed | tf_op | source)
XLA Modules:
  0.0 133.5 jit_solution(11972017162772818694)
XLA Ops:
  0.6 0.7 broadcast_in_dim.20
  1.3 30.8 %all_to_all.30 = f32[32,2,8,128]{3,2,1,0:T(8,128)S(1)} all-to-all(f32[32,2,8,128]{3,2,1,0:T(8,128)S(1)} %broadcast_in_dim.20), channel_id=1, replica_groups={{0,8,16,24,324,332,340,348,1,9,17,25,325,333,341,349,2,10,18,26,326,334..., dimensions={0} | all-to-all | bytes 524288 | tf_op jit(solution)/shard_map/all_to_all | solution.py:51
  32.2 0.1 broadcast_in_dim.22
  32.3 0.0 copy-start
  32.3 0.0 copy-start.1
  32.3 0.0 copy-start.4
  32.3 0.0 copy-start.5
  32.3 21.9 %all_to_all.31 = f32[8,64,8,128]{3,2,1,0:T(8,128)S(1)} all-to-all(f32[8,64,8,128]{3,2,1,0:T(8,128)S(1)} %broadcast_in_dim.22), channel_id=1, replica_groups={{0,4,452,448,68,64,384,388},{1,5,453,449,69,65,385,389},{2,6,454,450,70..., dimensions={0} | all-to-all | bytes 4194304 | tf_op jit(solution)/shard_map/all_to_all | solution.py:51
  54.2 5.0 %collective-permute-start = (f32[512,8,128]{2,1,0:T(8,128)S(1)}, f32[512,8,128]{2,1,0:T(8,128)S(1)}, u32[]{:S(2)}, u32[]{:S(2)}) collective-permute-start(f32[512,8,128]{2,1,0:T(8,128)S(1)} %bitcast.7), channel_id=1, source_target_pairs={{0,32},{1,33},{2,34},{3,35},{4,36},{5,37},{6,38},{7,39},{8,40},{9,... | collective-permute-start | bytes 6291464 | tf_op jit(solution)/shard_map/ppermute | solution.py:282
  59.3 0.0 copy-done.6
  59.3 0.0 copy-done
  59.3 0.0 copy-done.1
  59.3 0.0 copy-done.4
  59.3 0.0 copy-done.5
  59.3 2.7 %shard_map.85 = (f32[8,128]{1,0:T(8,128)S(1)}, s32[64]{0:T(128)S(1)}, f32[2,8,128]{2,1,0:T(8,128)S(1)}, bf16[16,2,128,256]{3,2,1,0:T(8,128)(2,1)S(1)}, bf16[16,2,128,256]{3,2,1,0:T(8,128)(2,1)S(1)}) custom-call(s32[2,16]{1,0:T(2,128)S(1)} %copy-done.4, s32[64]{0:T(128)S(1)} %copy-done.5, s32[64]{0:T(128)S(1)} %copy-done.6, f32[16,2,128,128]{3,2,1,0:T(8,128)S(1)} %copy-done, ...), custom_call_target="tpu_custom_call" | custom-call | flops 1073741824 | bytes 8388608 | tf_op jit(solution)/shard_map/pallas_call | solution.py:283
  62.0 0.9 shard_map.86.inner
  62.9 0.2 collective-permute-done.other
  63.1 1.7 %shard_map.87 = f32[16,3,8,128]{3,2,1,0:T(8,128)S(1)} custom-call(f32[8,128]{1,0:T(8,128)S(1)} %get-tuple-element.14.bases, f32[2,16,128,128]{3,2,1,0:T(8,128)S(1)} %shard_map.86.inner, f32[512,8,128]{2,1,0:T(8,128)S(1)} %collective-permute-done.other, bf16[16,2,128,256]{3,2,1,0:T(8,128)(2,1)S(1)} %get-tuple-element.15.lefts, ...), custom_call_target="tpu_custom_call" | custom-call | flops 1073741824 | bytes 1048576 | tf_op jit(solution)/shard_map/pallas_call | solution.py:306
  64.8 9.5 %all_to_all.32.parts = f32[16,3,8,128]{3,2,1,0:T(8,128)S(1)} all-to-all(f32[16,3,8,128]{3,2,1,0:T(8,128)S(1)} %shard_map.87), channel_id=1, replica_groups={{0,32,64,96,128,160,192,224,256,288,320,352,384,416,448,480},{1,33,65,9..., dimensions={0} | all-to-all | bytes 393216 | tf_op jit(solution)/shard_map/all_to_all | solution.py:51
  74.3 0.6 shard_map.88
  74.9 16.8 %all_to_all.33 = f32[32,2,8,128]{3,2,1,0:T(8,128)S(1)} all-to-all(f32[32,2,8,128]{3,2,1,0:T(8,128)S(1)} %get-tuple-element.18), channel_id=1, replica_groups={{0,8,16,24,324,332,340,348,1,9,17,25,325,333,341,349,2,10,18,26,326,334..., dimensions={0} | all-to-all | bytes 524288 | tf_op jit(solution)/shard_map/all_to_all | solution.py:51
  91.7 0.1 broadcast_in_dim.24
  91.8 24.2 %all_to_all.34 = f32[8,64,8,128]{3,2,1,0:T(8,128)S(1)} all-to-all(f32[8,64,8,128]{3,2,1,0:T(8,128)S(1)} %broadcast_in_dim.24), channel_id=1, replica_groups={{0,4,452,448,68,64,384,388},{1,5,453,449,69,65,385,389},{2,6,454,450,70..., dimensions={0} | all-to-all | bytes 4194304 | tf_op jit(solution)/shard_map/all_to_all | solution.py:51
  116.0 0.2 shard_map.90
  116.3 3.3 %collective-permute-start.1 = (f32[2,16,8,8,128]{4,3,2,1,0:T(8,128)S(1)}, f32[2,16,8,8,128]{4,3,2,1,0:T(8,128)S(1)}, u32[]{:S(2)}, u32[]{:S(2)}) collective-permute-start(f32[2,16,8,8,128]{4,3,2,1,0:T(8,128)S(1)} %shard_map.90), channel_id=1, source_target_pairs={{0,32},{1,33},{2,34},{3,35},{4,36},{5,37},{6,38},{7,39},{8,40},{9,... | collective-permute-start | bytes 3145736 | tf_op jit(solution)/shard_map/ppermute | solution.py:320
  119.6 0.9 shard_map.89.inner
  120.5 0.9 shard_map.91.sums
  121.4 0.5 collective-permute-done.1.packed
  121.9 1.5 %shard_map.92 = f32[16,3,8,128]{3,2,1,0:T(8,128)S(1)} custom-call(f32[2,16,128,128]{3,2,1,0:T(8,128)S(1)} %shard_map.89.inner, f32[2,16,8,8,128]{4,3,2,1,0:T(8,128)S(1)} %collective-permute-done.1.packed, bf16[16,2,128,256]{3,2,1,0:T(8,128)(2,1)S(1)} %get-tuple-element.15.lefts, bf16[16,2,128,256]{3,2,1,0:T(8,128)(2,1)S(1)} %get-tuple-element.16.rights, ...), custom_call_target="tpu_custom_call" | custom-call | flops 1073741824 | bytes 1048576 | tf_op jit(solution)/shard_map/pallas_call | solution.py:329
  123.4 9.5 %all_to_all.35.parts = f32[16,3,8,128]{3,2,1,0:T(8,128)S(1)} all-to-all(f32[16,3,8,128]{3,2,1,0:T(8,128)S(1)} %shard_map.92), channel_id=1, replica_groups={{0,32,64,96,128,160,192,224,256,288,320,352,384,416,448,480},{1,33,65,9..., dimensions={0} | all-to-all | bytes 393216 | tf_op jit(solution)/shard_map/all_to_all | solution.py:51
  132.9 0.0 copy-done.2
  132.9 0.7 shard_map.93
  (4 shorter events, 0.0 us)
Async XLA Ops:
  32.2 27.1 %copy-start.6 = (s32[64]{0:T(128)S(1)}, s32[64]{0:T(128)}, u32[]{:S(2)}) copy-start(s32[64]{0:T(128)} %sizes_hbm.1) | copy-start | bytes 772
  32.3 27.0 %copy-start = (f32[16,2,128,128]{3,2,1,0:T(8,128)S(1)}, f32[16,2,128,128]{3,2,1,0:T(8,128)}, u32[]{:S(2)}) copy-start(f32[16,2,128,128]{3,2,1,0:T(8,128)} %left.1) | copy-start | bytes 6291460
  32.3 27.0 %copy-start.1 = (f32[16,2,128,128]{3,2,1,0:T(8,128)S(1)}, f32[16,2,128,128]{3,2,1,0:T(8,128)}, u32[]{:S(2)}) copy-start(f32[16,2,128,128]{3,2,1,0:T(8,128)} %right.1) | copy-start | bytes 6291460
  32.3 27.0 %copy-start.4 = (s32[2,16]{1,0:T(2,128)S(1)}, s32[2,16]{1,0:T(2,128)}, u32[]{:S(2)}) copy-start(s32[2,16]{1,0:T(2,128)} %coupling_hbm.1) | copy-start | bytes 388
  32.3 27.0 %copy-start.5 = (s32[64]{0:T(128)S(1)}, s32[64]{0:T(128)}, u32[]{:S(2)}) copy-start(s32[64]{0:T(128)} %assign_hbm.1) | copy-start | bytes 772
  54.2 8.8 %collective-permute-start = (f32[512,8,128]{2,1,0:T(8,128)S(1)}, f32[512,8,128]{2,1,0:T(8,128)S(1)}, u32[]{:S(2)}, u32[]{:S(2)}) collective-permute-start(f32[512,8,128]{2,1,0:T(8,128)S(1)} %bitcast.7), channel_id=1, source_target_pairs={{0,32},{1,33},{2,34},{3,35},{4,36},{5,37},{6,38},{7,39},{8,40},{9,... | collective-permute-start | bytes 6291464 | tf_op jit(solution)/shard_map/ppermute | solution.py:282
  116.3 5.6 %collective-permute-start.1 = (f32[2,16,8,8,128]{4,3,2,1,0:T(8,128)S(1)}, f32[2,16,8,8,128]{4,3,2,1,0:T(8,128)S(1)}, u32[]{:S(2)}, u32[]{:S(2)}) collective-permute-start(f32[2,16,8,8,128]{4,3,2,1,0:T(8,128)S(1)} %shard_map.90), channel_id=1, source_target_pairs={{0,32},{1,33},{2,34},{3,35},{4,36},{5,37},{6,38},{7,39},{8,40},{9,... | collective-permute-start | bytes 3145736 | tf_op jit(solution)/shard_map/ppermute | solution.py:320
  121.3 11.5 %copy-start.2 = (f32[2,8,128]{2,1,0:T(8,128)S(1)}, f32[2,8,128]{2,1,0:T(8,128)}, u32[]{:S(2)}) copy-start(f32[2,8,128]{2,1,0:T(8,128)} %psi.1) | copy-start | bytes 24580
  121.3 11.5 %copy-start.3 = (f32[2,8,128]{2,1,0:T(8,128)S(1)}, f32[2,8,128]{2,1,0:T(8,128)}, u32[]{:S(2)}) copy-start(f32[2,8,128]{2,1,0:T(8,128)} %get-tuple-element.10.sigma) | copy-start | bytes 24580

commit v12 on v11

--- a/solution.py
+++ b/solution.py
@@ -32,7 +32,7 @@
 
 def cube(x, zl, core, y, zh):
     z = 2 * zh + zl
-    return (x + core - 1) % 4 // 2, (y - core) % 8 // 2, (z - core) % 8 // 2, core
+    return (x - core) % 4 // 2, (y - core) % 8 // 2, (z - core) % 8 // 2, core
 
 
 def kind(x, zl, core, y, zh):

time: 134 us -> 134 us (level)
  starting transfers between devices: 8.36 us -> 3.83 us
  blocking collectives: 113 us -> 117 us
    all_to_all x6, blocking collectives: 113 us -> 117 us  [exchange(): return lax.all_to_all(parts, AXES, 0, 0, axis_index_groups=members)]
    ppermute x1, starting transfers between devices: 5.04 us -> 1.91 us  [on_device(): start_other = lax.ppermute(start_mine, AXES, OTHER_CORE)]
    ppermute x1, starting transfers between devices: 3.31 us -> 1.92 us  [on_device(): other = lax.ppermute(packed, AXES, OTHER_CORE)]
where the time goes in v12:
time: 134 us
  blocking collectives  117 us (87%)
  Pallas kernels  10 us (7%)
  starting transfers between devices  3.83 us (3%)
  waiting for transfers between devices  1.4 us (1%)
    all_to_all x6, blocking collectives, exchange(): return lax.all_to_all(parts, AXES, 0, 0, axis_index_groups=members)  117 us
  transfers between devices with their start and end apart: 2, of which 2 were waited for; matrix products, arithmetic and copies ran while one was open for 0% of the time, Pallas kernels for 4%

profile of v12, /device:TPU:1, one launch (start us, length us, event | category | flops | bytes accessed | tf_op | source)
XLA Modules:
  0.0 134.0 jit_solution(6805098801081920450)
XLA Ops:
  0.6 0.7 broadcast_in_dim.20
  1.3 30.8 %all_to_all.30 = f32[32,2,8,128]{3,2,1,0:T(8,128)S(1)} all-to-all(f32[32,2,8,128]{3,2,1,0:T(8,128)S(1)} %broadcast_in_dim.20), channel_id=1, replica_groups={{0,8,16,24,324,332,340,348,1,9,17,25,325,333,341,349,2,10,18,26,326,334..., dimensions={0} | all-to-all | bytes 524288 | tf_op jit(solution)/shard_map/all_to_all | solution.py:51
  32.2 0.1 broadcast_in_dim.22
  32.3 0.0 copy-start
  32.3 0.0 copy-start.1
  32.3 0.0 copy-start.4
  32.3 0.0 copy-start.5
  32.3 24.4 %all_to_all.31 = f32[8,64,8,128]{3,2,1,0:T(8,128)S(1)} all-to-all(f32[8,64,8,128]{3,2,1,0:T(8,128)S(1)} %broadcast_in_dim.22), channel_id=1, replica_groups={{0,4,128,132,68,64,196,192},{1,5,129,133,69,65,197,193},{2,6,130,134,70..., dimensions={0} | all-to-all | bytes 4194304 | tf_op jit(solution)/shard_map/all_to_all | solution.py:51
  56.7 1.9 %collective-permute-start = (f32[512,8,128]{2,1,0:T(8,128)S(1)}, f32[512,8,128]{2,1,0:T(8,128)S(1)}, u32[]{:S(2)}, u32[]{:S(2)}) collective-permute-start(f32[512,8,128]{2,1,0:T(8,128)S(1)} %bitcast.7), channel_id=1, source_target_pairs={{0,32},{1,33},{2,34},{3,35},{4,36},{5,37},{6,38},{7,39},{8,40},{9,... | collective-permute-start | bytes 6291464 | tf_op jit(solution)/shard_map/ppermute | solution.py:282
  58.6 0.0 copy-done.6
  58.6 0.0 copy-done
  58.6 0.0 copy-done.1
  58.7 0.0 copy-done.4
  58.7 0.0 copy-done.5
  58.7 2.7 %shard_map.85 = (f32[8,128]{1,0:T(8,128)S(1)}, s32[64]{0:T(128)S(1)}, f32[2,8,128]{2,1,0:T(8,128)S(1)}, bf16[16,2,128,256]{3,2,1,0:T(8,128)(2,1)S(1)}, bf16[16,2,128,256]{3,2,1,0:T(8,128)(2,1)S(1)}) custom-call(s32[2,16]{1,0:T(2,128)S(1)} %copy-done.4, s32[64]{0:T(128)S(1)} %copy-done.5, s32[64]{0:T(128)S(1)} %copy-done.6, f32[16,2,128,128]{3,2,1,0:T(8,128)S(1)} %copy-done, ...), custom_call_target="tpu_custom_call" | custom-call | flops 1073741824 | bytes 8388608 | tf_op jit(solution)/shard_map/pallas_call | solution.py:283
  61.3 0.9 shard_map.86.inner
  62.2 0.5 collective-permute-done.other
  62.7 1.7 %shard_map.87 = f32[16,3,8,128]{3,2,1,0:T(8,128)S(1)} custom-call(f32[8,128]{1,0:T(8,128)S(1)} %get-tuple-element.14.bases, f32[2,16,128,128]{3,2,1,0:T(8,128)S(1)} %shard_map.86.inner, f32[512,8,128]{2,1,0:T(8,128)S(1)} %collective-permute-done.other, bf16[16,2,128,256]{3,2,1,0:T(8,128)(2,1)S(1)} %get-tuple-element.15.lefts, ...), custom_call_target="tpu_custom_call" | custom-call | flops 1073741824 | bytes 1048576 | tf_op jit(solution)/shard_map/pallas_call | solution.py:306
  64.5 9.3 %all_to_all.32.parts = f32[16,3,8,128]{3,2,1,0:T(8,128)S(1)} all-to-all(f32[16,3,8,128]{3,2,1,0:T(8,128)S(1)} %shard_map.87), channel_id=1, replica_groups={{0,32,64,96,128,160,192,224,256,288,320,352,384,416,448,480},{1,33,65,9..., dimensions={0} | all-to-all | bytes 393216 | tf_op jit(solution)/shard_map/all_to_all | solution.py:51
  73.7 0.6 shard_map.88
  74.4 19.7 %all_to_all.33 = f32[32,2,8,128]{3,2,1,0:T(8,128)S(1)} all-to-all(f32[32,2,8,128]{3,2,1,0:T(8,128)S(1)} %get-tuple-element.18), channel_id=1, replica_groups={{0,8,16,24,324,332,340,348,1,9,17,25,325,333,341,349,2,10,18,26,326,334..., dimensions={0} | all-to-all | bytes 524288 | tf_op jit(solution)/shard_map/all_to_all | solution.py:51
  94.0 0.1 broadcast_in_dim.24
  94.2 23.5 %all_to_all.34 = f32[8,64,8,128]{3,2,1,0:T(8,128)S(1)} all-to-all(f32[8,64,8,128]{3,2,1,0:T(8,128)S(1)} %broadcast_in_dim.24), channel_id=1, replica_groups={{0,4,128,132,68,64,196,192},{1,5,129,133,69,65,197,193},{2,6,130,134,70..., dimensions={0} | all-to-all | bytes 4194304 | tf_op jit(solution)/shard_map/all_to_all | solution.py:51
  117.7 0.2 shard_map.90
  118.0 1.9 %collective-permute-start.1 = (f32[2,16,8,8,128]{4,3,2,1,0:T(8,128)S(1)}, f32[2,16,8,8,128]{4,3,2,1,0:T(8,128)S(1)}, u32[]{:S(2)}, u32[]{:S(2)}) collective-permute-start(f32[2,16,8,8,128]{4,3,2,1,0:T(8,128)S(1)} %shard_map.90), channel_id=1, source_target_pairs={{0,32},{1,33},{2,34},{3,35},{4,36},{5,37},{6,38},{7,39},{8,40},{9,... | collective-permute-start | bytes 3145736 | tf_op jit(solution)/shard_map/ppermute | solution.py:320
  119.9 0.9 shard_map.89.inner
  120.8 0.9 shard_map.91.sums
  121.7 0.9 collective-permute-done.1.packed
  122.5 1.5 %shard_map.92 = f32[16,3,8,128]{3,2,1,0:T(8,128)S(1)} custom-call(f32[2,16,128,128]{3,2,1,0:T(8,128)S(1)} %shard_map.89.inner, f32[2,16,8,8,128]{4,3,2,1,0:T(8,128)S(1)} %collective-permute-done.1.packed, bf16[16,2,128,256]{3,2,1,0:T(8,128)(2,1)S(1)} %get-tuple-element.15.lefts, bf16[16,2,128,256]{3,2,1,0:T(8,128)(2,1)S(1)} %get-tuple-element.16.rights, ...), custom_call_target="tpu_custom_call" | custom-call | flops 1073741824 | bytes 1048576 | tf_op jit(solution)/shard_map/pallas_call | solution.py:329
  124.0 9.3 %all_to_all.35.parts = f32[16,3,8,128]{3,2,1,0:T(8,128)S(1)} all-to-all(f32[16,3,8,128]{3,2,1,0:T(8,128)S(1)} %shard_map.92), channel_id=1, replica_groups={{0,32,64,96,128,160,192,224,256,288,320,352,384,416,448,480},{1,33,65,9..., dimensions={0} | all-to-all | bytes 393216 | tf_op jit(solution)/shard_map/all_to_all | solution.py:51
  133.3 0.0 copy-done.2
  133.3 0.7 shard_map.93
  (4 shorter events, 0.0 us)
Async XLA Ops:
  32.2 26.5 %copy-start.6 = (s32[64]{0:T(128)S(1)}, s32[64]{0:T(128)}, u32[]{:S(2)}) copy-start(s32[64]{0:T(128)} %sizes_hbm.1) | copy-start | bytes 772
  32.3 26.3 %copy-start = (f32[16,2,128,128]{3,2,1,0:T(8,128)S(1)}, f32[16,2,128,128]{3,2,1,0:T(8,128)}, u32[]{:S(2)}) copy-start(f32[16,2,128,128]{3,2,1,0:T(8,128)} %left.1) | copy-start | bytes 6291460
  32.3 26.3 %copy-start.1 = (f32[16,2,128,128]{3,2,1,0:T(8,128)S(1)}, f32[16,2,128,128]{3,2,1,0:T(8,128)}, u32[]{:S(2)}) copy-start(f32[16,2,128,128]{3,2,1,0:T(8,128)} %right.1) | copy-start | bytes 6291460
  32.3 26.3 %copy-start.4 = (s32[2,16]{1,0:T(2,128)S(1)}, s32[2,16]{1,0:T(2,128)}, u32[]{:S(2)}) copy-start(s32[2,16]{1,0:T(2,128)} %coupling_hbm.1) | copy-start | bytes 388
  32.3 26.3 %copy-start.5 = (s32[64]{0:T(128)S(1)}, s32[64]{0:T(128)}, u32[]{:S(2)}) copy-start(s32[64]{0:T(128)} %assign_hbm.1) | copy-start | bytes 772
  56.7 6.0 %collective-permute-start = (f32[512,8,128]{2,1,0:T(8,128)S(1)}, f32[512,8,128]{2,1,0:T(8,128)S(1)}, u32[]{:S(2)}, u32[]{:S(2)}) collective-permute-start(f32[512,8,128]{2,1,0:T(8,128)S(1)} %bitcast.7), channel_id=1, source_target_pairs={{0,32},{1,33},{2,34},{3,35},{4,36},{5,37},{6,38},{7,39},{8,40},{9,... | collective-permute-start | bytes 6291464 | tf_op jit(solution)/shard_map/ppermute | solution.py:282
  118.0 4.6 %collective-permute-start.1 = (f32[2,16,8,8,128]{4,3,2,1,0:T(8,128)S(1)}, f32[2,16,8,8,128]{4,3,2,1,0:T(8,128)S(1)}, u32[]{:S(2)}, u32[]{:S(2)}) collective-permute-start(f32[2,16,8,8,128]{4,3,2,1,0:T(8,128)S(1)} %shard_map.90), channel_id=1, source_target_pairs={{0,32},{1,33},{2,34},{3,35},{4,36},{5,37},{6,38},{7,39},{8,40},{9,... | collective-permute-start | bytes 3145736 | tf_op jit(solution)/shard_map/ppermute | solution.py:320
  121.7 11.7 %copy-start.2 = (f32[2,8,128]{2,1,0:T(8,128)S(1)}, f32[2,8,128]{2,1,0:T(8,128)}, u32[]{:S(2)}) copy-start(f32[2,8,128]{2,1,0:T(8,128)} %psi.1) | copy-start | bytes 24580
  121.7 11.7 %copy-start.3 = (f32[2,8,128]{2,1,0:T(8,128)S(1)}, f32[2,8,128]{2,1,0:T(8,128)}, u32[]{:S(2)}) copy-start(f32[2,8,128]{2,1,0:T(8,128)} %get-tuple-element.10.sigma) | copy-start | bytes 24580
